TPU v7x, 32 devices: a whole 2x2x4 slice. The times are simulated.
32 devices in a mesh: batch: 8 (over y, x, core), head: 4 (over z).
Axes of the slice: x: 2, y: 2, z: 4, core: 2. Of those that a mesh axis runs over, the one named last changes fastest.
Arguments:
- tokens: bfloat16 [16384, 768], P(('batch', 'head')), may hold values from -6 to 6
- lengths: int32 [16], P('batch'), may hold values from 513 to 1024, as said below
- block_swap: int32 [12], P('head'), may hold values from 0 to 1
- input_weight: bfloat16 [3, 768, 768], P(None, None, 'head'), may hold values from -0.21875 to 0.21875
- input_bias: float32 [2, 768], P(None, 'head'), may hold values from -3 to 3
- out_weight: bfloat16 [768, 768], replicated, may hold values from -1.25 to 1.25
- out_bias: float32 [768], replicated, may hold values from -3 to 3
- gain_one: float32 [768], replicated, may hold values from 0.25 to 1.75
- shift_one: float32 [768], replicated, may hold values from -3 to 3
- up_weight: bfloat16 [768, 3072], P(None, 'head'), may hold values from -0.21875 to 0.21875
- up_bias: float32 [3072], replicated, may hold values from -3 to 3
- down_weight: bfloat16 [3072, 768], P('head'), may hold values from -0.109375 to 0.109375
- down_bias: float32 [768], replicated, may hold values from -3 to 3
- gain_two: float32 [768], replicated, may hold values from 0.25 to 1.75
- shift_two: float32 [768], replicated, may hold values from -3 to 3
- cotangent: bfloat16 [16384, 768], P(('batch', 'head')), may hold values from -6 to 6
Outputs:
- mixed_out: bfloat16 [16384, 768], P(('batch', 'head'))
- grad_tokens: float32 [16384, 768], P(('batch', 'head'))
- grad_input_weight: float32 [3, 768, 768], P(None, None, 'head')
- grad_input_bias: float32 [2, 768], P(None, 'head')
- grad_out_weight: float32 [768, 768], replicated
- grad_out_bias: float32 [768], replicated
- grad_gain_one: float32 [768], replicated
- grad_shift_one: float32 [768], replicated
- grad_up_weight: float32 [768, 3072], P(None, 'head')
- grad_up_bias: float32 [3072], P('head')
- grad_down_weight: float32 [3072, 768], P('head')
- grad_down_bias: float32 [768], replicated
- grad_gain_two: float32 [768], replicated
- grad_shift_two: float32 [768], replicated
Inputs may be any that keep to these rules, and one draw needn't show every extreme that they name: `lengths`: one sequence has exactly 1024 tokens.
All inputs are finite; a program needn't handle non-finite values.
Results may differ from a plain program's by a relative error of at most 0.015.
Values may be sent and summed in bfloat16 or wider, within the bound.
No kernel may reach another device: no remote copies, remote signals or barrier semaphores. Data moves between devices by JAX's collectives and lax.ppermute only.
A program may use at most 128 MiB of HBM per device.

v0:
```python
import jax
import jax.numpy as jnp
from jax import lax
from jax.sharding import PartitionSpec as P

SEQ_LEN = 1024


EPSILON = 1e-05


def norm_parts(values, gain_row, shift_row):
    centred = values - jnp.mean(values, axis=-1, keepdims=True)
    inverse = lax.rsqrt(jnp.mean(centred * centred, axis=-1, keepdims=True) + EPSILON)
    unit_rows = centred * inverse
    return (unit_rows * gain_row + shift_row, unit_rows, inverse)


def norm_back(grad_rows, unit_rows, inverse, gain_row):
    scaled = grad_rows * gain_row
    grad_in = inverse * (
        scaled
        - jnp.mean(scaled, axis=-1, keepdims=True)
        - unit_rows * jnp.mean(scaled * unit_rows, axis=-1, keepdims=True)
    )
    return (grad_in, jnp.sum(grad_rows * unit_rows, axis=0), jnp.sum(grad_rows, axis=0))


def contract_rows(left_side, right_side):
    return lax.dot_general(
        left_side, right_side, (((0,), (0,)), ((), ())), preferred_element_type=jnp.float32
    )


def contract_cols(left_side, right_side):
    return lax.dot_general(
        left_side, right_side, (((1,), (1,)), ((), ())), preferred_element_type=jnp.float32
    )


def local(
    tokens,
    lengths,
    block_swap,
    input_weight,
    input_bias,
    out_weight,
    out_bias,
    gain_one,
    shift_one,
    up_weight,
    up_bias,
    down_weight,
    down_bias,
    gain_two,
    shift_two,
    cotangent,
):
    seq_count = lengths.shape[0]
    head_count = block_swap.shape[0]
    head_width = input_weight.shape[2]
    head_depth = head_width // head_count
    block_rows = SEQ_LEN // 2
    scaling = head_depth ** (-0.5)
    own_rows = tokens.shape[0]
    hidden_own = up_weight.shape[1]
    group_rows = lax.all_gather(tokens, "head", axis=0, tiled=True)
    all_rows = group_rows.shape[0]
    positions = jnp.arange(SEQ_LEN, dtype=jnp.int32)
    present = (positions[None, :] < lengths[:, None]).astype(jnp.float32)
    row_mask = lax.dynamic_slice_in_dim(
        present.reshape(all_rows), lax.axis_index("head") * own_rows, own_rows
    )[:, None]
    queries = (
        jnp.dot(group_rows, input_weight[0], preferred_element_type=jnp.float32) + input_bias[0]
    ).astype(jnp.bfloat16)
    key_rows = jnp.dot(group_rows, input_weight[1], preferred_element_type=jnp.float32).astype(
        jnp.bfloat16
    )
    value_rows = (
        jnp.dot(group_rows, input_weight[2], preferred_element_type=jnp.float32) + input_bias[1]
    ).astype(jnp.bfloat16)
    layout = (seq_count, 2, block_rows, head_count, head_depth)
    swapped = block_swap == 1
    flipped = swapped[None, None, None, :, None]
    key_block = key_rows.reshape(layout)
    value_block = value_rows.reshape(layout)
    key_partner = jnp.where(flipped, key_block[:, ::-1], key_block)
    value_partner = jnp.where(flipped, value_block[:, ::-1], value_block)
    blocks = present.reshape(seq_count, 2, block_rows)
    live_keys = jnp.where(
        swapped[None, None, :, None], blocks[:, ::-1, None, :], blocks[:, :, None, :]
    )
    item_count = seq_count * 2
    item_shape = (item_count, block_rows, head_count, head_depth)
    query_items = queries.reshape(item_shape)
    key_items = key_partner.reshape(item_shape)
    value_items = value_partner.reshape(item_shape)
    live_items = live_keys.reshape(item_count, head_count, block_rows)

    def attend(element):
        query_block, key_now, value_now, live_block = element
        scores = (
            jnp.einsum("iha,jha->hij", query_block, key_now, preferred_element_type=jnp.float32)
            * scaling
        )
        open_keys = live_block[:, None, :] > 0.5
        anyone = jnp.max(live_block, axis=-1)[:, None, None]
        largest = jnp.max(jnp.where(open_keys, scores, -1e30), axis=-1, keepdims=True)
        largest = jnp.where(anyone > 0.5, largest, 0.0)
        weights = jnp.exp(jnp.where(open_keys, scores - largest, -10000.0))
        totals = jnp.sum(weights, axis=-1, keepdims=True) + (1.0 - anyone)
        mixing = (weights / totals).astype(jnp.bfloat16)
        context = jnp.einsum("hij,jha->iha", mixing, value_now, preferred_element_type=jnp.float32)
        return (context.astype(jnp.bfloat16), largest, totals)

    context_items, largest_items, total_items = lax.map(
        attend, (query_items, key_items, value_items, live_items)
    )
    context_own = lax.all_to_all(
        context_items.reshape(all_rows, head_width), "head", split_axis=0, concat_axis=1, tiled=True
    )
    projected = jnp.dot(context_own, out_weight, preferred_element_type=jnp.float32) + out_bias
    first_norm, unit_one, inverse_one = norm_parts(
        tokens.astype(jnp.float32) + projected, gain_one, shift_one
    )
    normed_low = first_norm.astype(jnp.bfloat16)
    bias_own = lax.dynamic_slice_in_dim(up_bias, lax.axis_index("head") * hidden_own, hidden_own)
    normed_group = lax.all_gather(normed_low, "head", axis=0, tiled=True)
    pre = jnp.dot(normed_group, up_weight, preferred_element_type=jnp.float32) + bias_own
    hidden = jax.nn.gelu(pre, approximate=False).astype(jnp.bfloat16)
    branch = (
        lax.psum_scatter(
            jnp.dot(hidden, down_weight, preferred_element_type=jnp.float32),
            "head",
            scatter_dimension=0,
            tiled=True,
        )
        + down_bias
    )
    second, unit_two, inverse_two = norm_parts(first_norm + branch, gain_two, shift_two)
    mixed_out = (second * row_mask).astype(jnp.bfloat16)
    grad_output = cotangent.astype(jnp.float32) * row_mask
    grad_second, grad_gain_two, grad_shift_two = norm_back(
        grad_output, unit_two, inverse_two, gain_two
    )
    grad_branch = grad_second.astype(jnp.bfloat16)
    grad_down_bias = jnp.sum(grad_branch.astype(jnp.float32), axis=0)
    unused_value, activation_back = jax.vjp(
        lambda inner: jax.nn.gelu(inner, approximate=False), pre
    )
    branch_group = lax.all_gather(grad_branch, "head", axis=0, tiled=True)
    grad_down_weight = contract_rows(hidden, branch_group)
    grad_hidden = contract_cols(branch_group, down_weight)
    grad_pre = activation_back(grad_hidden)[0].astype(jnp.bfloat16)
    grad_up_bias = jnp.sum(grad_pre.astype(jnp.float32), axis=0)
    grad_up_weight = contract_rows(normed_group, grad_pre)
    grad_normed = grad_second + lax.psum_scatter(
        contract_cols(grad_pre, up_weight), "head", scatter_dimension=0, tiled=True
    )
    grad_first, grad_gain_one, grad_shift_one = norm_back(
        grad_normed, unit_one, inverse_one, gain_one
    )
    grad_proj = grad_first.astype(jnp.bfloat16)
    grad_out_bias = jnp.sum(grad_proj.astype(jnp.float32), axis=0)
    grad_out_weight = contract_rows(context_own, grad_proj)
    grad_context_own = contract_cols(grad_proj, out_weight).astype(jnp.bfloat16)
    grad_context = lax.all_to_all(grad_context_own, "head", split_axis=1, concat_axis=0, tiled=True)
    grad_items = grad_context.reshape(item_shape)

    def attend_back(element):
        query_block, key_now, value_now, live_block, largest, totals, grad_now = element
        scores = (
            jnp.einsum("iha,jha->hij", query_block, key_now, preferred_element_type=jnp.float32)
            * scaling
        )
        open_keys = live_block[:, None, :] > 0.5
        chances = jnp.exp(jnp.where(open_keys, scores - largest, -10000.0)) / totals
        grad_mix = jnp.einsum(
            "iha,jha->hij", grad_now, value_now, preferred_element_type=jnp.float32
        )
        grad_scores = (
            chances * (grad_mix - jnp.sum(grad_mix * chances, axis=-1, keepdims=True))
        ).astype(jnp.bfloat16)
        grad_query = (
            jnp.einsum("hij,jha->iha", grad_scores, key_now, preferred_element_type=jnp.float32)
            * scaling
        ).astype(jnp.bfloat16)
        grad_key = (
            jnp.einsum("hij,iha->jha", grad_scores, query_block, preferred_element_type=jnp.float32)
            * scaling
        ).astype(jnp.bfloat16)
        grad_value = jnp.einsum(
            "hij,iha->jha",
            chances.astype(jnp.bfloat16),
            grad_now,
            preferred_element_type=jnp.float32,
        ).astype(jnp.bfloat16)
        return (grad_query, grad_key, grad_value)

    query_grads, key_grads, value_grads = lax.map(
        attend_back,
        (query_items, key_items, value_items, live_items, largest_items, total_items, grad_items),
    )
    grad_queries = query_grads.reshape(all_rows, head_width)
    key_back = key_grads.reshape(layout)
    value_back = value_grads.reshape(layout)
    grad_keys = jnp.where(flipped, key_back[:, ::-1], key_back).reshape(all_rows, head_width)
    grad_values = jnp.where(flipped, value_back[:, ::-1], value_back).reshape(all_rows, head_width)
    grad_input_weight = jnp.stack(
        [
            contract_rows(group_rows, grad_queries),
            contract_rows(group_rows, grad_keys),
            contract_rows(group_rows, grad_values),
        ]
    )
    grad_input_bias = jnp.stack(
        [
            jnp.sum(grad_queries.astype(jnp.float32), axis=0),
            jnp.sum(grad_values.astype(jnp.float32), axis=0),
        ]
    )
    total_rows = contract_cols(grad_queries, input_weight[0])
    total_rows = total_rows + contract_cols(grad_keys, input_weight[1])
    grad_tokens = grad_first + lax.psum_scatter(
        (total_rows + contract_cols(grad_values, input_weight[2])).astype(jnp.bfloat16),
        "head",
        scatter_dimension=0,
        tiled=True,
    ).astype(jnp.float32)
    vectors = jnp.stack(
        [
            grad_out_bias,
            grad_gain_one,
            grad_shift_one,
            grad_down_bias,
            grad_gain_two,
            grad_shift_two,
        ]
    )
    sharded = lax.psum(
        (grad_input_weight, grad_input_bias, grad_up_weight, grad_up_bias, grad_down_weight),
        "batch",
    )
    shared = lax.psum((grad_out_weight, vectors), ("batch", "head"))
    shared_vectors = shared[1]
    return (
        mixed_out,
        grad_tokens,
        sharded[0],
        sharded[1],
        shared[0],
        shared_vectors[0],
        shared_vectors[1],
        shared_vectors[2],
        sharded[2],
        sharded[3],
        sharded[4],
        shared_vectors[3],
        shared_vectors[4],
        shared_vectors[5],
    )


def solution(mesh):
    placed = (
        P(("batch", "head"), None),
        P("batch"),
        P("head"),
        P(None, None, "head"),
        P(None, "head"),
        P(),
        P(),
        P(),
        P(),
        P(None, "head"),
        P(),
        P("head", None),
        P(),
        P(),
        P(),
        P(("batch", "head"), None),
    )
    return jax.shard_map(
        local,
        mesh=mesh,
        in_specs=placed,
        out_specs=(
            P(("batch", "head"), None),
            P(("batch", "head"), None),
            P(None, None, "head"),
            P(None, "head"),
            P(),
            P(),
            P(),
            P(),
            P(None, "head"),
            P("head"),
            P("head", None),
            P(),
            P(),
            P(),
        ),
        check_vma=False,
    )
```

profile of v0, /device:TPU:0, one launch (start us, length us, event | category | flops | bytes accessed | tf_op | source)
XLA Modules:
  0.0 989.3 jit_solution(16779338274163449386)
XLA Ops:
  11.9 63.9 %all-gather.4.cloned.1.call-done = bf16[2048,768]{1,0:T(8,128)(2,1)} async-done(((bf16[512,768]{1,0:T(8,128)(2,1)}), bf16[2048,768]{1,0:T(8,128)(2,1)}) %all-gather.4.cloned.1.call-update) | async-done | bytes 3145744 | tf_op jit(solution)/shard_map/all_gather | solution.py:67
  75.8 3.1 fusion.62
  79.5 7.2 rev.15
  86.7 4.0 convolution_convert_fusion
  93.2 8.1 rev.17
  101.3 3.0 broadcast_select_fusion.3
  110.4 23.5 %while.28 = (s32[]{:T(128)}, bf16[4,512,3,64]{1,3,2,0:T(8,128)(2,1)}, f32[4,3,512,1]{2,1,3,0:T(4,128)}, f32[4,3,512,1]{2,1,3,0:T(4,128)}, bf16[4,512,3,64]{1,3,2...) while((s32[]{:T(128)}, ...), condition=%wide.region_4.5_spmd, body=%wide.region_0.4_spmd.sunk | while | flops 210868224 | bytes 10333878 | solution.py:117
  133.9 23.8 %all_to_all.35 = bf16[4,512,192]{1,2,0:T(8,128)(2,1)S(1)} all-to-all(bf16[4,512,192]{1,2,0:T(8,128)(2,1)} %bitcast.28), channel_id=1, replica_groups=mesh['batch'=8,'head'=4] {'head'}, dimensions={0} | all-to-all | bytes 1572864 | tf_op jit(solution)/shard_map/all_to_all | solution.py:120
  157.8 2.7 fusion.93
  163.7 61.1 %all-gather.6.cloned.1.call-done = bf16[2048,768]{1,0:T(8,128)(2,1)} async-done(((bf16[512,768]{1,0:T(8,128)(2,1)}), bf16[2048,768]{1,0:T(8,128)(2,1)}) %all-gather.6.cloned.1.call-update) | async-done | bytes 3145744 | tf_op jit(solution)/shard_map/all_gather | solution.py:129
  224.8 18.4 %multiply_convert_fusion.1 = (bf16[2048,768]{1,0:T(8,128)(2,1)S(1)}, f32[2048,768]{1,0:T(8,128)}, f32[2048,768]{1,0:T(8,128)}) fusion(f32[768]{0:T(1024)} %dynamic_slice.42, bf16[2048,768]{1,0:T(8,128)(2,1)} %all-gather.6.cloned.1.call-done, bf16[768,768]{1,0:T(8,128)(2,1)S(1)} %copy-done), kind=kOutput, calls=%fused_computation.74 | convolution fusion | flops 2519728128 | bytes 20057088 | tf_op jit(solution)/shard_map/dot_general | solution.py:130
  244.9 4.5 fusion.94
  252.2 106.8 %reduce-scatter.4.cloned.1.call-done = f32[512,768]{1,0:T(8,128)} async-done(((f32[2048,768]{1,0:T(8,128)}), f32[512,768]{1,0:T(8,128)}) %reduce-scatter.4.cloned.1.call-update) | async-done | bytes 1572880 | tf_op jit(solution)/shard_map/reduce_scatter | solution.py:133
  365.5 63.7 %all-gather.8.cloned.1.call-done = bf16[2048,768]{1,0:T(8,128)(2,1)} async-done(((bf16[512,768]{1,0:T(8,128)(2,1)}), bf16[2048,768]{1,0:T(8,128)(2,1)}) %all-gather.8.cloned.1.call-update) | async-done | bytes 3145744 | tf_op jit(solution)/shard_map/all_gather | solution.py:152
  429.2 11.0 %convert_reduce_fusion = (f32[768]{0:T(1024)}, bf16[2048,768]{1,0:T(8,128)(2,1)S(1)}) fusion(f32[2048,768]{1,0:T(8,128)} %get-tuple-element.230, f32[2048,768]{1,0:T(8,128)} %get-tuple-element.246, f32[768]{0:T(1024)} %dynamic_slice.42, bf16[2048,768]{1,0:T(8,128)(2,1)} %all-gather.8.cloned.1.call-done, bf16[768,768]{1,0:T(8,128)(2,1)} %param.31), kind=kOutput, calls=%fused_computation.71 | convolution fusion | flops 2442657024 | bytes 20060160 | tf_op jit(solution)/shard_map/dot_general | solution.py:36
  441.9 4.5 fusion.95
  446.6 109.5 %reduce-scatter.6.cloned.1.call-done = f32[512,768]{1,0:T(8,128)} async-done(((f32[2048,768]{1,0:T(8,128)}), f32[512,768]{1,0:T(8,128)}) %reduce-scatter.6.cloned.1.call-update) | async-done | bytes 1572880 | tf_op jit(solution)/shard_map/reduce_scatter | solution.py:158
  556.1 4.4 multiply_reduce_fusion.2
  563.3 24.3 %all_to_all.36 = bf16[512,4,192]{0,2,1:T(8,128)(2,1)S(1)} all-to-all(bf16[512,4,192]{0,2,1:T(8,128)(2,1)S(1)} %bitcast.215), channel_id=1, replica_groups=mesh['batch'=8,'head'=4] {'head'}, dimensions={1} | all-to-all | bytes 1572864 | tf_op jit(solution)/shard_map/all_to_all | solution.py:168
  589.6 32.5 %while.29 = (s32[]{:T(128)}, bf16[4,512,3,64]{1,3,2,0:T(8,128)(2,1)S(1)}, bf16[4,512,3,64]{1,3,2,0:T(8,128)(2,1)}, bf16[4,512,3,64]{1,3,2,0:T(8,128)(2,1)}, bf16...) while((s32[]{:T(128)}, ...), condition=%wide.region_17.18_spmd, body=%wide.region_15.17_spmd.sunk | while | flops 511672320 | bytes 25627260 | solution.py:201
  624.4 7.2 rev.19
  631.6 3.7 convert_reduce_fusion.3
  639.5 9.6 rev.18
  651.0 2.7 reshape.308
  657.0 2.8 add_convert_fusion
  659.9 7.1 fusion.97
  669.2 7.1 fusion.96
  680.9 44.0 %psum.52 = f32[6,768]{1,0:T(8,128)S(1)} all-reduce(f32[6,768]{1,0:T(8,128)S(1)} %stack.55), channel_id=1, replica_groups=mesh['batch'=8,'head'=4] {'batch','head'}, use_global_device_ids=true, to_apply=%region_30.31 | all-reduce | flops 4608 | bytes 36864 | tf_op jit(solution)/shard_map/psum | solution.py:245
  726.0 13.7 %all-reduce = (f32[2,192]{1,0:T(2,128)}, f32[768]{0:T(1024)}) all-reduce(f32[2,192]{1,0:T(2,128)S(1)} %pad_maximum_fusion.1, f32[768]{0:T(1024)S(1)} %copy-done.43), channel_id=1, replica_groups=mesh['batch'=8,'head'=4] {'batch'}, use_global_device_ids=true, to_apply=%region_22.23 | all-reduce | flops 1152 | bytes 9216 | tf_op jit(solution)/shard_map/psum | solution.py:241
  742.2 119.4 %all-reduce.5.cloned.1.call-done = f32[768,768]{1,0:T(8,128)} async-done(((f32[768,768]{1,0:T(8,128)}), f32[768,768]{1,0:T(8,128)}) %all-reduce.5.cloned.1.call-update) | async-done | bytes 2359312 | tf_op jit(solution)/shard_map/psum | solution.py:245
  861.6 111.1 %all-reduce.7.cloned.1.call-done = (f32[3,768,192]{1,2,0:T(8,128)}, f32[768,768]{1,0:T(8,128)}, f32[768,768]{1,0:T(8,128)}) async-done(((f32[3,768,192]{1,2,0:T(8,128)}, f32[768,768]{1,0:T(8,128)}, f32[768,768]{1,0:T(8,128)}), (f32[3,768,192]{1,2,0:T(8,128)}, f32[768,768]{1,0:T(8,128)}, f32[768,768]{1,0:T(8,128)})) %all-reduce.7.cloned.1.call-update) | async-done | bytes 6488080 | tf_op jit(solution)/shard_map/psum | solution.py:241
  972.7 2.9 copy.104
  (261 shorter events, 118.6 us)
Async XLA Ops:
  7.2 217.6 %copy-start = (bf16[768,768]{1,0:T(8,128)(2,1)S(1)}, bf16[768,768]{1,0:T(8,128)(2,1)}, u32[]{:S(2)}) copy-start(bf16[768,768]{1,0:T(8,128)(2,1)} %param.29) | copy-start | bytes 3538948
  7.2 68.6 %all-gather.4.cloned.1.call-start = ((), (), s32[]{:S(2)}) async-start(), calls=%async_computation.5 | async-start | bytes 3932160 | tf_op jit(solution)/shard_map/all_gather | solution.py:67
  7.9 216.8 %all-gather.6.cloned.1.call-start = ((), (), s32[]{:S(2)}) async-start(), calls=%async_computation.6 | async-start | bytes 3932160 | tf_op jit(solution)/shard_map/all_gather | solution.py:129
  10.4 90.9 %copy-start.40 = (pred[3]{0:T(512)(128)(4,1)}, pred[3]{0:T(512)(128)(4,1)S(1)}, u32[]{:S(2)}) copy-start(pred[3]{0:T(512)(128)(4,1)S(1)} %broadcast_compare_fusion.1) | copy-start | bytes 13
  110.4 47.3 %copy-start.46 = (f32[768]{0:T(1024)S(1)}, f32[768]{0:T(1024)}, u32[]{:S(2)}) copy-start(f32[768]{0:T(1024)} %param.26) | copy-start | bytes 9220
  133.9 23.8 %copy-start.7 = (bf16[4,512,3,64]{1,3,2,0:T(8,128)(2,1)}, bf16[4,512,3,64]{1,3,2,0:T(8,128)(2,1)S(1)}, u32[]{:S(2)}) copy-start(bf16[4,512,3,64]{1,3,2,0:T(8,128)(2,1)S(1)} %get-tuple-element.475) | copy-start | bytes 2359300
  133.9 23.8 %copy-start.16 = (bf16[4,512,3,64]{1,3,2,0:T(8,128)(2,1)}, bf16[4,512,3,64]{1,3,2,0:T(8,128)(2,1)S(1)}, u32[]{:S(2)}) copy-start(bf16[4,512,3,64]{1,3,2,0:T(8,128)(2,1)S(1)} %get-tuple-element.484) | copy-start | bytes 2359300
  162.0 196.9 %reduce-scatter.4.cloned.1.call-start = ((), (), s32[]{:S(2)}) async-start(), calls=%async_computation.7 | async-start | bytes 7864320 | tf_op jit(solution)/shard_map/reduce_scatter | solution.py:133
  224.8 20.2 %copy-start.44 = (bf16[768,768]{1,0:T(8,128)(2,1)S(1)}, bf16[768,768]{1,0:T(8,128)(2,1)}, u32[]{:S(2)}) copy-start(bf16[768,768]{1,0:T(8,128)(2,1)} %param.31) | copy-start | bytes 3538948
  249.4 179.8 %all-gather.8.cloned.1.call-start = ((), (), s32[]{:S(2)}) async-start(), calls=%async_computation.8 | async-start | bytes 3932160 | tf_op jit(solution)/shard_map/all_gather | solution.py:152
  365.0 191.1 %reduce-scatter.6.cloned.1.call-start = ((), (), s32[]{:S(2)}) async-start(), calls=%async_computation.9 | async-start | bytes 7864320 | tf_op jit(solution)/shard_map/reduce_scatter | solution.py:158
  446.5 109.6 %copy-start.15 = (bf16[512,768]{1,0:T(8,128)(2,1)S(1)}, bf16[512,768]{1,0:T(8,128)(2,1)}, u32[]{:S(2)}) copy-start(bf16[512,768]{1,0:T(8,128)(2,1)} %param.35) | copy-start | bytes 2359300
  446.5 109.6 %copy-start.25 = (f32[768]{0:T(1024)S(1)}, f32[768]{0:T(1024)}, u32[]{:S(2)}) copy-start(f32[768]{0:T(1024)} %param.33) | copy-start | bytes 9220
  446.5 109.6 %copy-start.27 = (f32[512]{0:T(512)S(1)}, f32[512]{0:T(512)}, u32[]{:S(2)}) copy-start(f32[512]{0:T(512)} %dynamic_slice.43) | copy-start | bytes 6148
  446.5 109.6 %copy-start.29 = (f32[512]{0:T(512)S(1)}, f32[512]{0:T(512)}, u32[]{:S(2)}) copy-start(f32[512]{0:T(512)} %copy-done.28) | copy-start | bytes 6148
  446.5 109.6 %copy-start.31 = (f32[512]{0:T(512)S(1)}, f32[512]{0:T(512)}, u32[]{:S(2)}) copy-start(f32[512]{0:T(512)} %copy-done.30) | copy-start | bytes 6148
  446.5 109.6 %copy-start.33 = (f32[512]{0:T(512)S(1)}, f32[512]{0:T(512)}, u32[]{:S(2)}) copy-start(f32[512]{0:T(512)} %copy-done.32) | copy-start | bytes 6148
  446.5 109.6 %copy-start.42 = (f32[768]{0:T(1024)S(1)}, f32[768]{0:T(1024)}, u32[]{:S(2)}) copy-start(f32[768]{0:T(1024)} %param.34) | copy-start | bytes 9220
  446.5 293.2 %reduce-scatter.8.cloned.1.call-start = ((), (), s32[]{:S(2)}) async-start(), calls=%async_computation.10 | async-start | bytes 3932160 | tf_op jit(solution)/shard_map/reduce_scatter | solution.py:225
  563.0 26.6 %copy-start.8 = (bf16[4,512,3,64]{1,3,2,0:T(8,128)(2,1)S(1)}, bf16[4,512,3,64]{1,3,2,0:T(8,128)(2,1)}, u32[]{:S(2)}) copy-start(bf16[4,512,3,64]{1,3,2,0:T(8,128)(2,1)} %copy-done.7) | copy-start | bytes 2359300
  622.1 31.6 %copy-start.11 = (bf16[4,512,3,64]{1,3,2,0:T(8,128)(2,1)}, bf16[4,512,3,64]{1,3,2,0:T(8,128)(2,1)S(1)}, u32[]{:S(2)}) copy-start(bf16[4,512,3,64]{1,3,2,0:T(8,128)(2,1)S(1)} %get-tuple-element.120) | copy-start | bytes 2359300
  622.1 9.4 copy-start.41
  624.4 13.4 %copy-start.13 = (bf16[4,512,3,64]{1,3,2,0:T(8,128)(2,1)S(1)}, bf16[4,512,3,64]{1,3,2,0:T(8,128)(2,1)}, u32[]{:S(2)}) copy-start(bf16[4,512,3,64]{1,3,2,0:T(8,128)(2,1)} %get-tuple-element.121) | copy-start | bytes 2359300
  637.8 19.3 %copy-start.9 = (bf16[2048,192]{0,1:T(8,128)(2,1)}, bf16[2048,192]{0,1:T(8,128)(2,1)S(1)}, u32[]{:S(2)}) copy-start(bf16[2048,192]{0,1:T(8,128)(2,1)S(1)} %reshape.310) | copy-start | bytes 2359300
  659.8 7.1 copy-start.6
  659.8 201.8 %all-reduce.5.cloned.1.call-start = ((), (), s32[]{:S(2)}) async-start(), calls=%async_computation.11 | async-start | bytes 4718592 | tf_op jit(solution)/shard_map/psum | solution.py:245
  659.9 7.1 copy-start.18
  669.2 303.5 %all-reduce.7.cloned.1.call-start = ((), (), s32[]{:S(2)}) async-start(), calls=%async_computation.12 | async-start | bytes 12976128 | tf_op jit(solution)/shard_map/psum | solution.py:241
  669.2 7.1 copy-start.4
  669.2 7.1 copy-start.10
  680.1 45.6 %copy-start.12 = (bf16[4,512,3,64]{1,3,2,0:T(8,128)(2,1)S(1)}, bf16[4,512,3,64]{1,3,2,0:T(8,128)(2,1)}, u32[]{:S(2)}) copy-start(bf16[4,512,3,64]{1,3,2,0:T(8,128)(2,1)} %copy-done.11) | copy-start | bytes 2359300
  680.1 45.8 %copy-start.43 = (f32[768]{0:T(1024)S(1)}, f32[768]{0:T(1024)}, u32[]{:S(2)}) copy-start(f32[768]{0:T(1024)} %get-tuple-element.222) | copy-start | bytes 9220
  (25 other events, 54.3 us)
Sparse Core Ops, SparseCore 0:
  9.6 66.1 all-gather.3
  162.2 62.5 all-gather.5
  249.6 109.3 reduce-scatter.3
  365.1 64.0 all-gather.7
  446.7 109.3 reduce-scatter.5
  659.9 60.3 reduce-scatter.7
  726.4 135.1 all-reduce.4
  866.8 105.8 all-reduce.6
where the time goes:
time: 1000 us; the launch traced here: 989 us
  waiting for transfers between devices  636 us (64%)
  matrix products  109 us (11%)
  blocking collectives  106 us (11%)
  local copies, waits for them, and re-layouts  75.2 us (8%)
  other arithmetic  46.3 us (5%)
  between operations  15.2 us (2%)
    psum x1, waiting for transfers between devices, local(): shared = lax.psum((grad_out_weight, vectors), ('batch', 'head'))  119 us
    psum x1, waiting for transfers between devices, local(): lax.psum((grad_input_weight, grad_input_bias, grad_up_weight, grad_up_bia...  111 us
    reduce_scatter x1, waiting for transfers between devices, local(): lax.psum_scatter(contract_cols(grad_pre, up_weight), 'head', scatter_dime...  110 us
    reduce_scatter x1, waiting for transfers between devices, local(): lax.psum_scatter(jnp.dot(hidden, down_weight, preferred_element_type=jnp....  107 us
    all_gather x1, waiting for transfers between devices, local(): group_rows = lax.all_gather(tokens, 'head', axis=0, tiled=True)  63.9 us
    all_gather x1, waiting for transfers between devices, local(): branch_group = lax.all_gather(grad_branch, 'head', axis=0, tiled=True)  63.7 us
    all_gather x1, waiting for transfers between devices, local(): normed_group = lax.all_gather(normed_low, 'head', axis=0, tiled=True)  61.1 us
    psum x1, blocking collectives, local(): shared = lax.psum((grad_out_weight, vectors), ('batch', 'head'))  44 us
  transfers between devices with their start and end apart: 8, of which 7 were waited for; matrix products, arithmetic and copies ran while one was open for 3% of the time, Pallas kernels for 0%

commit v1 on v0

v1 whole, which is shorter than its diff:
```python
import functools

import jax
import jax.numpy as jnp
from jax import lax
from jax.experimental import pallas as pl
from jax.experimental.pallas import tpu as pltpu
from jax.sharding import PartitionSpec as P

SEQ_LEN = 1024
EPSILON = 1e-05
F32 = jnp.float32
BF16 = jnp.bfloat16
VMEM_LIMIT = 48 * 1024 * 1024


def norm_parts(values, gain_row, shift_row):
    centred = values - jnp.mean(values, axis=-1, keepdims=True)
    inverse = lax.rsqrt(jnp.mean(centred * centred, axis=-1, keepdims=True) + EPSILON)
    unit_rows = centred * inverse
    return (unit_rows * gain_row + shift_row, unit_rows, inverse)


def norm_back(grad_rows, unit_rows, inverse, gain_row):
    scaled = grad_rows * gain_row
    grad_in = inverse * (
        scaled
        - jnp.mean(scaled, axis=-1, keepdims=True)
        - unit_rows * jnp.mean(scaled * unit_rows, axis=-1, keepdims=True)
    )
    return (grad_in, jnp.sum(grad_rows * unit_rows, axis=0), jnp.sum(grad_rows, axis=0))


def dot(left_side, right_side, left_dim=1, right_dim=0):
    return lax.dot_general(
        left_side,
        right_side,
        (((left_dim,), (right_dim,)), ((), ())),
        preferred_element_type=F32,
    )


def lane_pick(values, heads, depth):
    lane = lax.broadcasted_iota(jnp.int32, (1, len(values) * depth), 1)
    picked = jnp.full(lane.shape, values[0], jnp.int32)
    for j in range(1, len(values)):
        picked = jnp.where(lane >= j * depth, values[j], picked)
    return picked


def attend_kernel(
    heads, depth, info, tokens, partner, weight, bias, q_out, k_out, v_out, context_out, stats_out
):
    shard = pl.program_id(0)
    total_heads = heads * pl.num_programs(0)
    swaps = [info[shard * heads + j] for j in range(heads)]
    own_live, partner_live = info[total_heads], info[total_heads + 1]
    rows = tokens.shape[0]
    width = heads * depth
    x, xp = tokens[...], partner[...]
    swapped = lane_pick(swaps, heads, depth) == 1
    q = (dot(x, weight[0, 0]) + bias[0, 0]).astype(BF16)
    k = jnp.where(swapped, dot(xp, weight[1, 0]), dot(x, weight[1, 0])).astype(BF16)
    v = (jnp.where(swapped, dot(xp, weight[2, 0]), dot(x, weight[2, 0])) + bias[1, 0]).astype(BF16)
    q = q * (depth**-0.5)
    q_out[0], k_out[0], v_out[0] = q, k, v
    key_index = lax.broadcasted_iota(jnp.int32, (rows, 1), 0)
    stats = []
    pieces = []
    for j in range(heads):
        cut = slice(j * depth, (j + 1) * depth)
        live = jnp.where(swaps[j] == 1, partner_live, own_live)
        open_keys = key_index < live
        anyone = jnp.where(live > 0, 1.0, 0.0).astype(F32)
        scores = dot(k[:, cut], q[:, cut], 1, 1)
        largest = jnp.max(jnp.where(open_keys, scores, -1e30), axis=0, keepdims=True)
        largest = jnp.where(anyone > 0.5, largest, 0.0)
        weights = jnp.exp(jnp.where(open_keys, scores - largest, -10000.0))
        totals = jnp.sum(weights, axis=0, keepdims=True) + (1.0 - anyone)
        mixing = (weights * (1.0 / totals)).astype(BF16)
        stats.append(largest + jnp.log(totals))
        pieces.append(dot(v[:, cut], mixing, 0, 0))
    context_out[0] = jnp.concatenate(pieces, axis=0).T.astype(BF16)
    stats_out[0] = jnp.concatenate(
        stats + [jnp.zeros((8 - heads, rows), F32)], axis=0
    )


def attend_back_kernel(
    heads,
    depth,
    info,
    tokens_t,
    partner_t,
    weight,
    q_in,
    k_in,
    v_in,
    grad_in,
    stats_in,
    own_out,
    partner_out,
    weight_out,
    bias_out,
):
    shard = pl.program_id(0)
    total_heads = heads * pl.num_programs(0)
    swaps = [info[shard * heads + j] for j in range(heads)]
    own_live, partner_live = info[total_heads], info[total_heads + 1]
    rows = q_in.shape[1]
    q, k, v, grad = q_in[0], k_in[0], v_in[0], grad_in[0]
    stats = stats_in[0]
    key_index = lax.broadcasted_iota(jnp.int32, (rows, 1), 0)
    gq, gk, gv = [], [], []
    for j in range(heads):
        cut = slice(j * depth, (j + 1) * depth)
        live = jnp.where(swaps[j] == 1, partner_live, own_live)
        open_keys = key_index < live
        scores = dot(k[:, cut], q[:, cut], 1, 1)
        chances = jnp.exp(jnp.where(open_keys, scores - stats[j : j + 1, :], -10000.0))
        grad_mix = dot(v[:, cut], grad[:, cut], 1, 1)
        shared = jnp.sum(grad_mix * chances, axis=0, keepdims=True)
        grad_scores = (chances * (grad_mix - shared)).astype(BF16)
        gk.append(dot(grad_scores, q[:, cut]))
        gv.append(dot(chances.astype(BF16), grad[:, cut]))
        gq.append(dot(k[:, cut], grad_scores, 0, 0))
    grad_q = (jnp.concatenate(gq, axis=0).T * (depth**-0.5)).astype(BF16)
    grad_k = jnp.concatenate(gk, axis=1).astype(BF16)
    grad_v = jnp.concatenate(gv, axis=1).astype(BF16)
    swapped = lane_pick(swaps, heads, depth) == 1
    nothing = jnp.zeros((), BF16)
    k_own, k_far = jnp.where(swapped, nothing, grad_k), jnp.where(swapped, grad_k, nothing)
    v_own, v_far = jnp.where(swapped, nothing, grad_v), jnp.where(swapped, grad_v, nothing)
    own = (
        dot(grad_q, weight[0, 0], 1, 1)
        + dot(k_own, weight[1, 0], 1, 1)
        + dot(v_own, weight[2, 0], 1, 1)
    )
    far = dot(k_far, weight[1, 0], 1, 1) + dot(v_far, weight[2, 0], 1, 1)

    @pl.when(shard == 0)
    def first():
        own_out[...] = own
        partner_out[...] = far

    @pl.when(shard > 0)
    def later():
        own_out[...] += own
        partner_out[...] += far

    xt, xpt = tokens_t[...], partner_t[...]
    weight_out[0, 0] = dot(xt, grad_q).astype(BF16)
    weight_out[1, 0] = (dot(xt, k_own) + dot(xpt, k_far)).astype(BF16)
    weight_out[2, 0] = (dot(xt, v_own) + dot(xpt, v_far)).astype(BF16)
    bias_out[0] = jnp.concatenate(
        [
            jnp.sum(grad_q.astype(F32), axis=0, keepdims=True),
            jnp.sum(grad_v.astype(F32), axis=0, keepdims=True),
            jnp.zeros((6, grad_q.shape[1]), F32),
        ],
        axis=0,
    )


def attend(info, tokens, partner, weight, bias, shards, heads, depth):
    rows, dim = tokens.shape
    width = heads * depth
    per_shard = pl.BlockSpec((1, rows, width), lambda s: (s, 0, 0))
    items = jax.ShapeDtypeStruct((shards, rows, width), BF16)
    return pl.pallas_call(
        functools.partial(attend_kernel, heads, depth),
        grid=(shards,),
        in_specs=[
            pl.BlockSpec(memory_space=pltpu.SMEM),
            pl.BlockSpec((rows, dim), lambda s: (0, 0)),
            pl.BlockSpec((rows, dim), lambda s: (0, 0)),
            pl.BlockSpec((3, 1, dim, width), lambda s: (0, s, 0, 0)),
            pl.BlockSpec((2, 1, 1, width), lambda s: (0, s, 0, 0)),
        ],
        out_specs=[per_shard] * 4 + [pl.BlockSpec((1, 8, rows), lambda s: (s, 0, 0))],
        out_shape=[items] * 4 + [jax.ShapeDtypeStruct((shards, 8, rows), F32)],
        compiler_params=pltpu.CompilerParams(vmem_limit_bytes=VMEM_LIMIT),
        cost_estimate=pl.CostEstimate(
            flops=10 * rows * dim * dim + 4 * rows * rows * dim,
            bytes_accessed=20 * rows * dim,
            transcendentals=shards * heads * rows * rows,
        ),
        name="attend",
    )(info, tokens, partner, weight, bias)


def attend_back(info, tokens_t, partner_t, weight, q, k, v, grad, stats, shards, heads, depth):
    dim, rows = tokens_t.shape
    width = heads * depth
    per_shard = pl.BlockSpec((1, rows, width), lambda s: (s, 0, 0))
    weight_spec = pl.BlockSpec((3, 1, dim, width), lambda s: (0, s, 0, 0))
    whole = pl.BlockSpec((rows, dim), lambda s: (0, 0))
    return pl.pallas_call(
        functools.partial(attend_back_kernel, heads, depth),
        grid=(shards,),
        in_specs=[
            pl.BlockSpec(memory_space=pltpu.SMEM),
            pl.BlockSpec((dim, rows), lambda s: (0, 0)),
            pl.BlockSpec((dim, rows), lambda s: (0, 0)),
            weight_spec,
            per_shard,
            per_shard,
            per_shard,
            per_shard,
            pl.BlockSpec((1, 8, rows), lambda s: (s, 0, 0)),
        ],
        out_specs=[
            whole,
            whole,
            weight_spec,
            pl.BlockSpec((1, 8, width), lambda s: (s, 0, 0)),
        ],
        out_shape=[
            jax.ShapeDtypeStruct((rows, dim), F32),
            jax.ShapeDtypeStruct((rows, dim), F32),
            jax.ShapeDtypeStruct((3, shards, dim, width), BF16),
            jax.ShapeDtypeStruct((shards, 8, width), F32),
        ],
        compiler_params=pltpu.CompilerParams(vmem_limit_bytes=VMEM_LIMIT),
        cost_estimate=pl.CostEstimate(
            flops=20 * rows * dim * dim + 10 * rows * rows * dim,
            bytes_accessed=32 * rows * dim,
            transcendentals=shards * heads * rows * rows,
        ),
        name="attend_back",
    )(info, tokens_t, partner_t, weight, q, k, v, grad, stats)


def local(
    batch_size,
    shards,
    tokens,
    lengths,
    block_swap,
    input_weight,
    input_bias,
    out_weight,
    out_bias,
    gain_one,
    shift_one,
    up_weight,
    up_bias,
    down_weight,
    down_bias,
    gain_two,
    shift_two,
    cotangent,
):
    heads = block_swap.shape[0]
    rows, dim = tokens.shape
    width = input_weight.shape[2]
    depth = width // heads
    hidden_own = up_weight.shape[1]
    both = ("head", "batch")
    batch_at, head_at = lax.axis_index("batch"), lax.axis_index("head")
    blocks = SEQ_LEN // rows
    length = lax.dynamic_index_in_dim(lengths, head_at // blocks, 0, keepdims=False)
    block_at = head_at % blocks
    own_live = jnp.clip(length - block_at * rows, 0, rows)
    partner_live = jnp.clip(length - (blocks - 1 - block_at) * rows, 0, rows)
    row_mask = (jnp.arange(rows, dtype=jnp.int32) < own_live).astype(F32)[:, None]

    partner = lax.ppermute(tokens, "head", [(i, i ^ 1) for i in range(shards)])
    part = dim // batch_size

    def share(weight, axis):
        piece = lax.dynamic_slice_in_dim(weight, batch_at * part, part, axis)
        return lax.all_gather(piece, both, axis=axis, tiled=True)

    weight_all = share(input_weight, 1).reshape(3, shards, dim, width)
    up_all = share(up_weight, 0).reshape(shards, dim, hidden_own)
    down_all = share(down_weight, 0).reshape(shards, hidden_own, dim)
    small = jnp.concatenate([input_bias.reshape(-1), block_swap.astype(F32)])
    small = lax.all_gather(small, "head")
    bias_all = small[:, : 2 * width].reshape(shards, 2, 1, width).transpose(1, 0, 2, 3)
    info = jnp.concatenate(
        [
            small[:, 2 * width :].reshape(-1).astype(jnp.int32),
            jnp.stack([own_live, partner_live]).astype(jnp.int32),
        ]
    )

    q, k, v, context, stats = attend(
        info, tokens, partner, weight_all, bias_all, shards, heads, depth
    )
    out_parts = out_weight.reshape(shards, width, dim)
    projected = (
        jnp.einsum("sta,sad->td", context, out_parts, preferred_element_type=F32) + out_bias
    )
    first_norm, unit_one, inverse_one = norm_parts(
        tokens.astype(F32) + projected, gain_one, shift_one
    )
    normed_low = first_norm.astype(BF16)
    up_bias_parts = up_bias.reshape(shards, 1, hidden_own)
    pre = jnp.einsum("td,sdh->sth", normed_low, up_all, preferred_element_type=F32) + up_bias_parts
    hidden, activation_back = jax.vjp(lambda inner: jax.nn.gelu(inner, approximate=False), pre)
    hidden = hidden.astype(BF16)
    branch = jnp.einsum("sth,shd->td", hidden, down_all, preferred_element_type=F32) + down_bias
    second, unit_two, inverse_two = norm_parts(first_norm + branch, gain_two, shift_two)
    mixed_out = (second * row_mask).astype(BF16)
    grad_output = cotangent.astype(F32) * row_mask
    grad_second, grad_gain_two, grad_shift_two = norm_back(
        grad_output, unit_two, inverse_two, gain_two
    )
    grad_branch = grad_second.astype(BF16)
    grad_down_bias = jnp.sum(grad_branch.astype(F32), axis=0)
    grad_down = jnp.einsum("sth,td->shd", hidden, grad_branch, preferred_element_type=F32)
    grad_hidden = jnp.einsum("td,shd->sth", grad_branch, down_all, preferred_element_type=F32)
    grad_pre = activation_back(grad_hidden)[0].astype(BF16)
    grad_up_bias = jnp.sum(grad_pre.astype(F32), axis=1)
    grad_up = jnp.einsum("td,sth->sdh", normed_low, grad_pre, preferred_element_type=F32)
    grad_normed = grad_second + jnp.einsum(
        "sth,sdh->td", grad_pre, up_all, preferred_element_type=F32
    )
    grad_first, grad_gain_one, grad_shift_one = norm_back(
        grad_normed, unit_one, inverse_one, gain_one
    )
    grad_proj = grad_first.astype(BF16)
    grad_out_bias = jnp.sum(grad_proj.astype(F32), axis=0)
    grad_out = jnp.einsum("sta,td->sad", context, grad_proj, preferred_element_type=F32)
    grad_context = jnp.einsum(
        "td,sad->sta", grad_proj, out_parts, preferred_element_type=F32
    ).astype(BF16)

    own_rows, partner_rows, grad_weight, grad_bias = attend_back(
        info, tokens.T, partner.T, weight_all, q, k, v, grad_context, stats, shards, heads, depth
    )
    from_partner = lax.ppermute(
        partner_rows.astype(BF16), "head", [(i, i ^ 1) for i in range(shards)]
    )
    grad_tokens = grad_first + own_rows + from_partner.astype(F32)

    def collect(grads, axis):
        piece = lax.psum_scatter(grads, both, scatter_dimension=axis, tiled=True)
        return lax.all_gather(piece, "batch", axis=axis, tiled=True).astype(F32)

    grad_down_own = collect(grad_down.astype(BF16).reshape(shards * hidden_own, dim), 0)
    grad_up_own = collect(grad_up.astype(BF16).reshape(shards * dim, hidden_own), 0)
    grad_out_piece = lax.psum_scatter(
        grad_out.astype(BF16).reshape(shards * width, dim), both, scatter_dimension=0, tiled=True
    )
    grad_out_all = lax.all_gather(grad_out_piece, both, axis=0, tiled=True).astype(F32)
    grad_input_weight = collect(grad_weight.reshape(3, shards * dim, width), 1)

    bias_sums = grad_bias[:, :2].transpose(1, 0, 2).reshape(2, dim)
    vectors = jnp.concatenate(
        [
            jnp.stack(
                [
                    grad_out_bias,
                    grad_gain_one,
                    grad_shift_one,
                    grad_down_bias,
                    grad_gain_two,
                    grad_shift_two,
                ]
            ),
            bias_sums,
            grad_up_bias.reshape(-1, dim),
        ],
        axis=0,
    )
    vectors = jnp.sum(lax.all_gather(vectors, both), axis=0)
    grad_input_bias = lax.dynamic_slice_in_dim(vectors[6:8], head_at * width, width, 1)
    grad_up_bias_own = lax.dynamic_slice_in_dim(
        vectors[8:].reshape(-1), head_at * hidden_own, hidden_own
    )
    return (
        mixed_out,
        grad_tokens,
        grad_input_weight,
        grad_input_bias,
        grad_out_all,
        vectors[0],
        vectors[1],
        vectors[2],
        grad_up_own,
        grad_up_bias_own,
        grad_down_own,
        vectors[3],
        vectors[4],
        vectors[5],
    )


def solution(mesh):
    rows_spec = P(("batch", "head"), None)
    placed = (
        rows_spec,
        P("batch"),
        P("head"),
        P(None, None, "head"),
        P(None, "head"),
        P(),
        P(),
        P(),
        P(),
        P(None, "head"),
        P(),
        P("head", None),
        P(),
        P(),
        P(),
        rows_spec,
    )
    return jax.shard_map(
        functools.partial(local, mesh.shape["batch"], mesh.shape["head"]),
        mesh=mesh,
        in_specs=placed,
        out_specs=(
            rows_spec,
            rows_spec,
            P(None, None, "head"),
            P(None, "head"),
            P(),
            P(),
            P(),
            P(),
            P(None, "head"),
            P("head"),
            P("head", None),
            P(),
            P(),
            P(),
        ),
        check_vma=False,
    )
```

time: 1000 us -> 842 us (0.84)
  blocking collectives: 106 us -> 38.3 us
  matrix products: 109 us -> 57.8 us
  Pallas kernels: 0 us -> 39.1 us
  other arithmetic: 46.3 us -> 18.4 us
  waiting for transfers between devices: 636 us -> 611 us
  local copies, waits for them, and re-layouts: 75.2 us -> 54.9 us
    psum x2 -> x0, waiting for transfers between devices: 231 us -> none  [the longest x1 119 us: local(): shared = lax.psum((grad_out_weight, vectors), ('batch', 'head'))]
    unnamed x8 -> x12, waiting for transfers between devices: 0.8 us -> 106 us
    psum x2 -> x0, blocking collectives: 57.8 us -> none  [the longest x1 44 us: local(): shared = lax.psum((grad_out_weight, vectors), ('batch', 'head'))]
    all_gather x3 -> x7, waiting for transfers between devices: 189 us -> 244 us  [the longest x3 126 us: share(): return lax.all_gather(piece, both, axis=axis, tiled=True)]
    dot_general x46 -> x9, matrix products: 109 us -> 57.8 us  [the longest x1 20.2 us: local(): jnp.einsum('td,sdh->sth', normed_low, up_all, preferred_element_type=F32)]
    all_to_all x2 -> x0, blocking collectives: 48.1 us -> none  [the longest x1 24.3 us: local(): lax.all_to_all(grad_context_own, 'head', split_axis=1, concat_axis=0, til...]
    pallas_call x0 -> x2, Pallas kernels: none -> 39.1 us  [the longest x1 25.2 us: attend_back(): pl.pallas_call(functools.partial(attend_back_kernel, heads, depth), grid=...]
    rev x5 -> x0, local copies, waits for them, and re-layouts: 32.1 us -> none  [the longest x1 9.57 us: local(): key_back[:, ::-1]]
  transfers between devices with their start and end apart: 8 -> 13, of which waited for: 7 -> 12; matrix products, arithmetic and copies ran while one was open for 3% -> 11% of each run, Pallas kernels for 0% -> 5%
where the time goes in v1:
time: 842 us; the launch traced here: 841 us
  waiting for transfers between devices  611 us (73%)
  matrix products  57.8 us (7%)
  local copies, waits for them, and re-layouts  54.9 us (7%)
  Pallas kernels  39.1 us (5%)
  blocking collectives  38.3 us (5%)
  other arithmetic  18.4 us (2%)
  between operations  16.4 us (2%)
    reduce_scatter x2, waiting for transfers between devices, collect(): piece = lax.psum_scatter(grads, both, scatter_dimension=axis, tiled=True)  201 us
    all_gather x3, waiting for transfers between devices, share(): return lax.all_gather(piece, both, axis=axis, tiled=True)  126 us
    unnamed x12, waiting for transfers between devices  106 us
    all_gather x1, waiting for transfers between devices, local(): lax.all_gather(grad_out_piece, both, axis=0, tiled=True).astype(F32)  52.3 us
    reduce_scatter x1, waiting for transfers between devices, local(): lax.psum_scatter(grad_out.astype(BF16).reshape(shards * width, dim), both...  43.3 us
    unnamed x82, local copies, waits for them, and re-layouts  37.5 us
    all_gather x1, waiting for transfers between devices, local(): vectors = jnp.sum(lax.all_gather(vectors, both), axis=0)  34.6 us
    all_gather x2, waiting for transfers between devices, collect(): return lax.all_gather(piece, 'batch', axis=axis, tiled=True).astype(F32)  31 us
  transfers between devices with their start and end apart: 13, of which 12 were waited for; matrix products, arithmetic and copies ran while one was open for 11% of the time, Pallas kernels for 5%

profile of v1, /device:TPU:0, one launch (start us, length us, event | category | flops | bytes accessed | tf_op | source)
XLA Modules:
  0.0 841.0 jit_solution(16792669376709509326)
XLA Ops:
  14.1 3.1 collective-permute-start
  20.6 24.4 %all-reduce = f32[1548]{0:T(1024)S(1)} all-reduce(f32[1548]{0:T(1024)S(1)} %maximum_dynamic-update-slice_fusion), channel_id=2, replica_groups=mesh['batch'=8,'head'=4] {'head'}, use_global_device_ids=true, to_apply=%add | all-reduce | flops 1548 | bytes 12384
  48.0 37.2 %all-gather.11.cloned.1.call-done = bf16[3,3072,192]{2,0,1:T(4,128)(2,1)} async-done(((bf16[3,96,192]{2,0,1:T(4,128)(2,1)}), bf16[3,3072,192]{2,0,1:T(4,128)(2,1)}) %all-gather.11.cloned.1.call-update) | async-done | bytes 3538960 | tf_op jit(solution)/shard_map/all_gather | solution.py:273
  85.2 5.6 copy.69
  90.8 13.9 %attend.1 = (bf16[4,512,192]{2,1,0:T(8,128)(2,1)S(1)}, bf16[4,512,192]{2,1,0:T(8,128)(2,1)S(1)}, bf16[4,512,192]{2,1,0:T(8,128)(2,1)S(1)}, bf16[4,512,192]{2,1,0:T(8,128)(2,1)S(1)}, f32[4,8,512]{2,1,0:T(8,128)S(1)}) custom-call(s32[14]{0:T(128)S(1)} %pad_add_fusion.info, bf16[512,768]{1,0:T(8,128)(2,1)S(1)} %copy-done.1, bf16[512,768]{1,0:T(8,128)(2,1)S(1)} %copy-done.6, ...), custom_call_target="tpu_custom_call" | custom-call | flops 3825205248 | bytes 7864320 | tf_op jit(solution)/shard_map/attend/pallas_call | solution.py:170
  107.9 43.0 %all-gather.13.cloned.1.call-done = bf16[3072,768]{1,0:T(8,128)(2,1)} async-done(((bf16[96,768]{1,0:T(8,128)(2,1)}), bf16[3072,768]{1,0:T(8,128)(2,1)}) %all-gather.13.cloned.1.call-update) | async-done | bytes 4718608 | tf_op jit(solution)/shard_map/all_gather | solution.py:273
  150.9 20.2 %fusion.9 = (bf16[4,512,768]{2,1,0:T(8,128)(2,1)}, f32[4,512,768]{2,1,0:T(8,128)}, f32[4,768,512]{1,2,0:T(8,128)}) fusion(f32[4,768]{1,0:T(4,128)S(1)} %copy-done.22, bf16[4,768,768]{2,1,0:T(8,128)(2,1)} %bitcast.164, f32[512,768]{1,0:T(8,128)} %copy-done.15, f32[768]{0:T(1024)S(1)} %copy-done.29, f32[768]{0:T(1024)S(1)} %copy-done.24, ...), kind=kOutput, calls=%fused_computation.18 | convolution fusion | flops 2521694208 | bytes 22042624 | tf_op jit(solution)/shard_map/td,sdh->sth/dot_general | solution.py:300
  171.1 45.7 %all-gather.15.cloned.1.call-done = bf16[3072,768]{1,0:T(8,128)(2,1)} async-done(((bf16[96,768]{1,0:T(8,128)(2,1)}), bf16[3072,768]{1,0:T(8,128)(2,1)}) %all-gather.15.cloned.1.call-update) | async-done | bytes 4718608 | tf_op jit(solution)/shard_map/all_gather | solution.py:273
  216.8 6.7 fusion.43
  226.4 7.8 convert_reduce_fusion
  234.3 3.0 multiply_reduce_fusion.1
  239.8 7.4 convolution_convert_fusion.1
  248.7 6.7 convolution_convert_fusion
  255.5 3.2 convolution_convert_fusion.3
  265.0 25.2 %attend_back.1 = (f32[512,768]{1,0:T(8,128)}, f32[512,768]{1,0:T(8,128)}, bf16[3,4,768,192]{3,2,1,0:T(8,128)(2,1)}, f32[4,8,192]{2,1,0:T(8,128)S(1)}) custom-call(s32[14]{0:T(128)S(1)} %pad_add_fusion.info, bf16[768,512]{1,0:T(8,128)(2,1)S(1)} %bitcast.152, bf16[768,512]{1,0:T(8,128)(2,1)S(1)} %bitcast.153, bf16[3,4,768,192]{3,2,1,0:T(8,128)(2,1)} %bitcast.160, ...), custom_call_target="tpu_custom_call" | custom-call | flops 8053063680 | bytes 12582912 | tf_op jit(solution)/shard_map/attend_back/pallas_call | solution.py:198
  291.6 43.3 %reduce-scatter.7.cloned.1.call-done = bf16[24,768]{1,0:T(8,128)(2,1)} async-done(((bf16[768,768]{1,0:T(8,128)(2,1)}), bf16[24,768]{1,0:T(8,128)(2,1)}) %reduce-scatter.7.cloned.1.call-update) | async-done | bytes 36880 | tf_op jit(solution)/shard_map/reduce_scatter | solution.py:344
  335.0 9.4 %copy.93 = bf16[3,3072,192]{2,0,1:T(4,128)(2,1)} copy(bf16[3,3072,192]{2,1,0:T(8,128)(2,1)} %bitcast.161) | data formatting | bytes 7077888
  344.4 13.0 %reshape.148 = bf16[3072,576]{1,0:T(8,128)(2,1)} reshape(bf16[3072,3,192]{2,1,0:T(4,128)(2,1)} %bitcast.155) | data formatting | bytes 7077888
  357.5 88.8 %reduce-scatter.9.cloned.1.call-done = bf16[96,768]{1,0:T(8,128)(2,1)} async-done(((bf16[3072,768]{1,0:T(8,128)(2,1)}), bf16[96,768]{1,0:T(8,128)(2,1)}) %reduce-scatter.9.cloned.1.call-update) | async-done | bytes 147472 | tf_op jit(solution)/shard_map/reduce_scatter | solution.py:339
  446.4 112.3 %reduce-scatter.11.cloned.1.call-done = bf16[96,768]{1,0:T(8,128)(2,1)} async-done(((bf16[3072,768]{1,0:T(8,128)(2,1)}), bf16[96,768]{1,0:T(8,128)(2,1)}) %reduce-scatter.11.cloned.1.call-update) | async-done | bytes 147472 | tf_op jit(solution)/shard_map/reduce_scatter | solution.py:339
  561.6 17.1 %collective-permute-done.1 = bf16[512,768]{1,0:T(8,128)(2,1)} collective-permute-done((bf16[512,768]{1,0:T(8,128)(2,1)S(1)}, bf16[512,768]{1,0:T(8,128)(2,1)}, u32[]{:S(2)}, u32[]{:S(2)}) %collective-permute-start.1) | collective-permute-done | bytes 786464 | tf_op jit(solution)/shard_map/ppermute | solution.py:333
  578.7 3.0 convert_add_fusion
  581.8 34.6 %all-gather.23.cloned.1.call-done = f32[32,12,768]{2,1,0:T(8,128)} async-done(((f32[1,12,768]{2,1,0:T(8,128)}), f32[32,12,768]{2,1,0:T(8,128)}) %all-gather.23.cloned.1.call-update) | async-done | bytes 1179664 | tf_op jit(solution)/shard_map/all_gather | solution.py:368
  619.9 52.3 %all-gather.17.cloned.1.call-done = bf16[768,768]{1,0:T(8,128)(2,1)} async-done(((bf16[24,768]{1,0:T(8,128)(2,1)}), bf16[768,768]{1,0:T(8,128)(2,1)}) %all-gather.17.cloned.1.call-update) | async-done | bytes 1179664 | tf_op jit(solution)/shard_map/all_gather | solution.py:347
  672.2 2.8 convert_element_type.105
  675.1 105.6 %reduce-scatter.13.cloned.1.call-done = bf16[96,576]{1,0:T(8,128)(2,1)} async-done(((bf16[3072,576]{1,0:T(8,128)(2,1)}), bf16[96,576]{1,0:T(8,128)(2,1)}) %reduce-scatter.13.cloned.1.call-update) | async-done | bytes 110608
  781.7 14.0 %all_gather.38 = bf16[3,768,192]{2,0,1:T(4,128)(2,1)S(1)} all-gather(bf16[3,96,192]{2,0,1:T(4,128)(2,1)S(1)} %bitcast.162), channel_id=1, replica_groups=mesh['batch'=8,'head'=4] {'batch'}, dimensions={1}, use_global_device_ids=true | all-gather | bytes 995328 | tf_op jit(solution)/shard_map/all_gather | solution.py:340
  795.7 2.2 copy.81
  797.9 7.8 all-gather.19.cloned.1.call-done
  805.7 2.8 convert_element_type.108
  808.5 23.1 %all-gather.21.cloned.1.call-done = bf16[768,768]{1,0:T(8,128)(2,1)} async-done(((bf16[96,768]{1,0:T(8,128)(2,1)}), bf16[768,768]{1,0:T(8,128)(2,1)}) %all-gather.21.cloned.1.call-update) | async-done | bytes 1179664 | tf_op jit(solution)/shard_map/all_gather | solution.py:340
  831.7 2.8 convert_element_type.110
  (154 shorter events, 36.4 us)
Async XLA Ops:
  7.2 97.5 %copy-start = (bf16[768,768]{1,0:T(8,128)(2,1)S(1)}, bf16[768,768]{1,0:T(8,128)(2,1)}, u32[]{:S(2)}) copy-start(bf16[768,768]{1,0:T(8,128)(2,1)} %param.21) | copy-start | bytes 3538948
  7.2 12.0 %copy-start.32 = (u32[32]{0:T(128)S(1)}, u32[32]{0:T(128)}, u32[]{:S(2)}) copy-start(u32[32]{0:T(128)} %constant.128) | copy-start | bytes 388
  7.2 10.0 %copy-start.30 = (s32[2]{0:T(128)S(1)}, s32[2]{0:T(128)}, u32[]{:S(2)}) copy-start(s32[2]{0:T(128)} %param.17) | copy-start | bytes 28
  7.2 11.9 %copy-start.31 = (s32[3]{0:T(128)S(1)}, s32[3]{0:T(128)}, u32[]{:S(2)}) copy-start(s32[3]{0:T(128)} %param.18) | copy-start | bytes 40
  7.2 11.9 %copy-start.25 = (f32[2,192]{1,0:T(2,128)S(1)}, f32[2,192]{1,0:T(2,128)}, u32[]{:S(2)}) copy-start(f32[2,192]{1,0:T(2,128)} %param.20) | copy-start | bytes 4612
  7.2 38.0 %copy-start.21 = (f32[3072]{0:T(1024)S(1)}, f32[3072]{0:T(1024)}, u32[]{:S(2)}) copy-start(f32[3072]{0:T(1024)} %param.26) | copy-start | bytes 36868
  7.2 77.9 %all-gather.11.cloned.1.call-start = ((), (), s32[]{:S(2)}) async-start(), calls=%async_computation.4 | async-start | bytes 6488064 | tf_op jit(solution)/shard_map/all_gather | solution.py:273
  9.3 141.5 %all-gather.13.cloned.1.call-start = ((), (), s32[]{:S(2)}) async-start(), calls=%async_computation.5 | async-start | bytes 4866048 | tf_op jit(solution)/shard_map/all_gather | solution.py:273
  11.0 205.8 %all-gather.15.cloned.1.call-start = ((), (), s32[]{:S(2)}) async-start(), calls=%async_computation.6 | async-start | bytes 4866048 | tf_op jit(solution)/shard_map/all_gather | solution.py:273
  12.7 322.3 %reduce-scatter.7.cloned.1.call-start = ((), (), s32[]{:S(2)}) async-start(), calls=%async_computation.7 | async-start | bytes 1216512 | tf_op jit(solution)/shard_map/reduce_scatter | solution.py:344
  14.1 76.7 %copy-start.2 = (bf16[512,768]{0,1:T(8,128)(2,1)}, bf16[512,768]{0,1:T(8,128)(2,1)S(1)}, u32[]{:S(2)}) copy-start(bf16[512,768]{0,1:T(8,128)(2,1)S(1)} %copy.67) | copy-start | bytes 2359300
  14.1 31.8 %collective-permute-start = (bf16[512,768]{0,1:T(8,128)(2,1)S(1)}, bf16[512,768]{0,1:T(8,128)(2,1)S(1)}, u32[]{:S(2)}, u32[]{:S(2)}) collective-permute-start(bf16[512,768]{0,1:T(8,128)(2,1)S(1)} %copy.67), channel_id=1, source_target_pairs={{0,1},{1,0},{2,3},{3,2},{4,5},{5,4},{6,7},{7,6},{8,9},{9,8},{10,11... | collective-permute-start | bytes 2359304 | tf_op jit(solution)/shard_map/ppermute | solution.py:268
  48.0 42.8 %copy-start.1 = (bf16[512,768]{1,0:T(8,128)(2,1)S(1)}, bf16[512,768]{1,0:T(8,128)(2,1)}, u32[]{:S(2)}) copy-start(bf16[512,768]{1,0:T(8,128)(2,1)} %tokens.1) | copy-start | bytes 2359300
  90.8 14.0 %copy-start.27 = (f32[768]{0:T(1024)S(1)}, f32[768]{0:T(1024)}, u32[]{:S(2)}) copy-start(f32[768]{0:T(1024)} %param.22) | copy-start | bytes 9220
  104.8 46.1 %copy-start.22 = (f32[4,768]{1,0:T(4,128)S(1)}, f32[4,768]{1,0:T(4,128)}, u32[]{:S(2)}) copy-start(f32[4,768]{1,0:T(4,128)} %add.111) | copy-start | bytes 36868
  104.8 46.1 %copy-start.24 = (f32[768]{0:T(1024)S(1)}, f32[768]{0:T(1024)}, u32[]{:S(2)}) copy-start(f32[768]{0:T(1024)} %param.23) | copy-start | bytes 9220
  104.8 46.1 %copy-start.29 = (f32[768]{0:T(1024)S(1)}, f32[768]{0:T(1024)}, u32[]{:S(2)}) copy-start(f32[768]{0:T(1024)} %param.24) | copy-start | bytes 9220
  150.9 66.0 %copy-start.28 = (f32[768]{0:T(1024)S(1)}, f32[768]{0:T(1024)}, u32[]{:S(2)}) copy-start(f32[768]{0:T(1024)} %param.28) | copy-start | bytes 9220
  216.8 9.6 %copy-start.34 = (f32[4,512,768]{2,1,0:T(8,128)S(1)}, f32[4,512,768]{2,1,0:T(8,128)}, u32[]{:S(2)}) copy-start(f32[4,512,768]{2,1,0:T(8,128)} %get-tuple-element.79) | copy-start | bytes 18874372
  224.7 9.5 %slice-start = ((s8[4718592]{0:T(1024)(128)(4,1)}), s8[4194304]{0:T(1024)(128)(4,1)S(1)}, s32[]{:S(2)}) async-start(s8[4718592]{0:T(1024)(128)(4,1)} %bitcast.165), calls=%async_computation.15 | async-start | bytes 8388608
  226.4 7.9 copy-start.18
  226.4 7.9 copy-start.16
  226.4 7.9 slice-start.1
  239.8 206.6 %reduce-scatter.9.cloned.1.call-start = ((), (), s32[]{:S(2)}) async-start(), calls=%async_computation.9 | async-start | bytes 4866048 | tf_op jit(solution)/shard_map/reduce_scatter | solution.py:339
  247.3 311.4 %reduce-scatter.11.cloned.1.call-start = ((), (), s32[]{:S(2)}) async-start(), calls=%async_computation.11 | async-start | bytes 4866048 | tf_op jit(solution)/shard_map/reduce_scatter | solution.py:339
  255.4 361.0 %all-gather.23.cloned.1.call-start = ((), (), s32[]{:S(2)}) async-start(), calls=%async_computation.13 | async-start | bytes 1622016 | tf_op jit(solution)/shard_map/all_gather | solution.py:368
  291.6 380.6 %all-gather.17.cloned.1.call-start = ((), (), s32[]{:S(2)}) async-start(), calls=%async_computation.8 | async-start | bytes 1216512 | tf_op jit(solution)/shard_map/all_gather | solution.py:347
  335.0 445.7 %reduce-scatter.13.cloned.1.call-start = ((), (), s32[]{:S(2)}) async-start(), calls=%async_computation.14 | async-start | bytes 4055040
  357.5 221.3 %copy-start.14 = (f32[512,768]{1,0:T(8,128)S(1)}, f32[512,768]{1,0:T(8,128)}, u32[]{:S(2)}) copy-start(f32[512,768]{1,0:T(8,128)} %copy-done.13) | copy-start | bytes 4718596
  357.5 448.2 %all-gather.19.cloned.1.call-start = ((), (), s32[]{:S(2)}) async-start(), calls=%async_computation.10 | async-start | bytes 1327104 | tf_op jit(solution)/shard_map/all_gather | solution.py:340
  446.4 385.3 %all-gather.21.cloned.1.call-start = ((), (), s32[]{:S(2)}) async-start(), calls=%async_computation.12 | async-start | bytes 1327104 | tf_op jit(solution)/shard_map/all_gather | solution.py:340
  560.2 18.5 %collective-permute-start.1 = (bf16[512,768]{1,0:T(8,128)(2,1)S(1)}, bf16[512,768]{1,0:T(8,128)(2,1)}, u32[]{:S(2)}, u32[]{:S(2)}) collective-permute-start(bf16[512,768]{1,0:T(8,128)(2,1)S(1)} %convert_element_type.98), channel_id=1, source_target_pairs={{0,1},{1,0},{2,3},{3,2},{4,5},{5,4},{6,7},{7,6},{8,9},{9,8},{10,11... | collective-permute-start | bytes 2359304 | tf_op jit(solution)/shard_map/ppermute | solution.py:333
  (18 other events, 45.4 us)
Sparse Core Ops, SparseCore 0:
  11.5 73.6 all-gather.10
  88.7 62.1 all-gather.12
  154.3 62.4 all-gather.14
  239.9 95.0 reduce-scatter.6
  340.3 106.0 reduce-scatter.8
  452.6 106.0 reduce-scatter.10
  562.1 54.1 all-gather.22
  619.3 52.9 all-gather.16
  677.6 103.0 reduce-scatter.12
  782.4 23.2 all-gather.18
  807.6 24.0 all-gather.20

commit v2 on v1

v2 whole, which is shorter than its diff:
```python
import functools

import jax
import jax.numpy as jnp
from jax import lax
from jax.experimental import pallas as pl
from jax.experimental.pallas import tpu as pltpu
from jax.sharding import PartitionSpec as P

SEQ_LEN = 1024
EPSILON = 1e-05
F32 = jnp.float32
BF16 = jnp.bfloat16
VMEM_LIMIT = 56 * 1024 * 1024
PARAMS = pltpu.CompilerParams(vmem_limit_bytes=VMEM_LIMIT)
CORE, NEAR_X, NEAR_Y = 1, 2, 4
PARTS = 8


def dot(left_side, right_side, left_dim=1, right_dim=0):
    return lax.dot_general(
        left_side,
        right_side,
        (((left_dim,), (right_dim,)), ((), ())),
        preferred_element_type=F32,
    )


def unit_parts(values):
    centred = values - jnp.mean(values, axis=-1, keepdims=True)
    inverse = lax.rsqrt(jnp.mean(centred * centred, axis=-1, keepdims=True) + EPSILON)
    return centred * inverse, inverse


def norm_back(grad_rows, unit_rows, inverse, gain_row):
    scaled = grad_rows * gain_row
    return inverse * (
        scaled
        - jnp.mean(scaled, axis=-1, keepdims=True)
        - unit_rows * jnp.mean(scaled * unit_rows, axis=-1, keepdims=True)
    )


def column_sum(values):
    return jnp.sum(values, axis=0, keepdims=True)


def gelu_parts(inner):
    bell = jnp.exp(inner * inner * -0.5)
    t = 1.0 / (1.0 + jnp.abs(inner) * (0.3275911 * 0.5**0.5))
    poly = t * (
        0.254829592
        + t * (-0.284496736 + t * (1.421413741 + t * (-1.453152027 + t * 1.061405429)))
    )
    tail = 0.5 * poly * bell
    below = jnp.where(inner < 0.0, tail, 1.0 - tail)
    return inner * below, below + inner * bell * 0.3989422804014327


def lane_pick(values, depth):
    lane = lax.broadcasted_iota(jnp.int32, (1, len(values) * depth), 1)
    picked = jnp.full(lane.shape, values[0], jnp.int32)
    for j in range(1, len(values)):
        picked = jnp.where(lane >= j * depth, values[j], picked)
    return picked


class Info:
    def __init__(self, ref, heads, shards):
        self.ref, self.heads, self.base = ref, heads, heads * shards

    def swaps(self, shard):
        return [self.ref[shard * self.heads + j] for j in range(self.heads)]

    own_live = property(lambda self: self.ref[self.base])
    partner_live = property(lambda self: self.ref[self.base + 1])
    part = property(lambda self: self.ref[self.base + 2])
    head_at = property(lambda self: self.ref[self.base + 3])


def fill_weight(info, near, far, scratch):
    for spot in range(PARTS // 2):
        scratch[info.part ^ (2 * spot)] = near[spot, 0]
        scratch[info.part ^ (2 * spot + 1)] = far[spot, 0]


def attend_kernel(
    heads,
    depth,
    info_ref,
    tokens,
    partner,
    near,
    far,
    bias,
    out_weight,
    vectors,
    qkv_out,
    context_out,
    stats_out,
    rows_out,
    normed_out,
    weight_scratch,
    total,
):
    shard, shards = pl.program_id(0), pl.num_programs(0)
    info = Info(info_ref, heads, shards)
    swaps = info.swaps(shard)
    rows, dim = tokens.shape
    width = heads * depth
    fill_weight(info, near, far, weight_scratch)
    weight = weight_scratch[...].reshape(dim, 3 * width)
    own = dot(tokens[...], weight) + bias[0, 0:1]
    other = dot(partner[...], weight[:, : 2 * width]) + bias[0, 0:1, : 2 * width]
    swapped = lane_pick(swaps + swaps, depth) == 1
    kv = jnp.where(swapped, other, own[:, : 2 * width]).astype(BF16)
    q = own[:, 2 * width :].astype(BF16) * (depth**-0.5)
    qkv_out[0, :, : 2 * width] = kv
    qkv_out[0, :, 2 * width :] = q
    key_index = lax.broadcasted_iota(jnp.int32, (rows, 1), 0)
    stats = []
    pieces = []
    for j in range(heads):
        cut = slice(j * depth, (j + 1) * depth)
        live = jnp.where(swaps[j] == 1, info.partner_live, info.own_live)
        open_keys = key_index < live
        anyone = jnp.where(live > 0, 1.0, 0.0).astype(F32)
        scores = dot(kv[:, cut], q[:, cut], 1, 1)
        largest = jnp.max(jnp.where(open_keys, scores, -1e30), axis=0, keepdims=True)
        largest = jnp.where(anyone > 0.5, largest, 0.0)
        weights = jnp.exp(jnp.where(open_keys, scores - largest, -10000.0))
        totals = column_sum(weights) + (1.0 - anyone)
        mixing = (weights * (1.0 / totals)).astype(BF16)
        stats.append(largest + jnp.log(totals))
        pieces.append(dot(kv[:, width + j * depth : width + (j + 1) * depth], mixing, 0, 0))
    context = jnp.concatenate(pieces, axis=0).T.astype(BF16)
    context_out[0] = context
    stats_out[0] = jnp.concatenate(stats + [jnp.zeros((8 - heads, rows), F32)], axis=0)
    projected = dot(context, out_weight[info.head_at ^ shard])

    @pl.when(shard == 0)
    def first():
        total[...] = projected

    @pl.when(shard > 0)
    def later():
        total[...] += projected

    @pl.when(shard == shards - 1)
    def finish():
        values = tokens[...].astype(F32) + (total[...] + vectors[0:1])
        rows_out[...] = values
        unit, _ = unit_parts(values)
        normed_out[...] = (unit * vectors[1:2] + vectors[2:3]).astype(BF16)


def forward_kernel(last, normed, weight, bias, *refs):
    step, steps = pl.program_id(0), pl.num_programs(0)
    if last:
        (info, branch_in, rows_in, cotangent, vectors) = refs[:5]
        (hidden_out, slope_out, mixed_out, second_out, grad_out, sums_out, total) = refs[5:]
    else:
        (hidden_out, slope_out, total) = refs
    dim = normed.shape[1]
    block = weight[0].reshape(-1, 2 * dim)
    pre = dot(normed[...], block[:, :dim], 1, 1) + bias[0]
    hidden, slope = gelu_parts(pre)
    hidden = hidden.astype(BF16)
    hidden_out[...] = hidden
    slope_out[...] = slope
    partial = dot(hidden, block[:, dim:])

    @pl.when(step == 0)
    def first():
        total[...] = partial

    @pl.when(step > 0)
    def later():
        total[...] += partial

    if not last:
        return

    @pl.when(step == steps - 1)
    def finish():
        unit_one, _ = unit_parts(rows_in[...])
        first_norm = unit_one * vectors[0:1] + vectors[1:2]
        unit, inverse = unit_parts(first_norm + (branch_in[...] + total[...] + vectors[2:3]))
        present = lax.broadcasted_iota(jnp.int32, (normed.shape[0], 1), 0) < info[0]
        mask = jnp.where(present, 1.0, 0.0).astype(F32)
        mixed_out[...] = ((unit * vectors[3:4] + vectors[4:5]) * mask).astype(BF16)
        incoming = cotangent[...].astype(F32) * mask
        grad = norm_back(incoming, unit, inverse, vectors[3:4])
        second_out[...] = grad
        low = grad.astype(BF16)
        grad_out[...] = low
        sums_out[...] = jnp.concatenate(
            [
                column_sum(low.astype(F32)),
                column_sum(incoming * unit),
                column_sum(incoming),
                jnp.zeros((5, dim), F32),
            ],
            axis=0,
        )


def backward_kernel(last, normed, grad_branch, weight, hidden, slope, *refs):
    step, steps = pl.program_id(0), pl.num_programs(0)
    if last:
        (info, normed_in, rows_in, second_in, context, vectors) = refs[:6]
        (grads_out, bias_out, first_out, proj_out, sums_out, near_out, far_out) = refs[6:13]
        (total, chunks) = refs[13:]
    else:
        (grads_out, bias_out, total) = refs
    dim = normed.shape[1]
    shards, piece = weight.shape[1], weight.shape[2]
    block = weight[0].reshape(-1, 2 * dim)
    grad_rows = grad_branch[...]
    grad_pre = dot(grad_rows, block[:, dim:], 1, 1) * slope[...]
    grad_pre = grad_pre.astype(BF16)
    bias_out[0] = jnp.broadcast_to(column_sum(grad_pre.astype(F32)), bias_out.shape[1:])
    up = dot(grad_pre, normed[...], 0, 0)
    grads_out[0, :, :, :dim] = up.astype(BF16).reshape(shards, piece, dim)
    down = dot(hidden[...], grad_rows, 0, 0)
    grads_out[0, :, :, dim:] = down.astype(BF16).reshape(shards, piece, dim)
    partial = dot(grad_pre, block[:, :dim])

    @pl.when(step == 0)
    def first():
        total[...] = partial

    @pl.when(step > 0)
    def later():
        total[...] += partial

    if not last:
        return

    @pl.when(step == steps - 1)
    def finish():
        unit, inverse = unit_parts(rows_in[...])
        grad_normed = second_in[...] + (normed_in[...] + total[...])
        grad = norm_back(grad_normed, unit, inverse, vectors[0:1])
        first_out[...] = grad
        low = grad.astype(BF16)
        proj_out[...] = low
        sums_out[...] = jnp.concatenate(
            [
                column_sum(low.astype(F32)),
                column_sum(grad_normed * unit),
                column_sum(grad_normed),
                jnp.zeros((5, dim), F32),
            ],
            axis=0,
        )
        low_t = low.T
        part = info[1]
        for q in range(shards):
            value = dot(low_t, context[q]).astype(BF16)
            chunks[...] = value.reshape(chunks.shape)
            for spot in range(PARTS // 2):
                near_out[spot, q] = chunks[part ^ (2 * spot)]
                far_out[spot, q] = chunks[part ^ (2 * spot + 1)]


def attend_back_kernel(
    heads,
    depth,
    info_ref,
    tokens,
    partner,
    grad_proj,
    near,
    far,
    out_weight,
    qkv_in,
    stats_in,
    own_out,
    partner_out,
    near_out,
    far_out,
    bias_out,
    weight_scratch,
    tokens_t,
    partner_t,
    total,
    chunks,
):
    shard, shards = pl.program_id(0), pl.num_programs(0)
    info = Info(info_ref, heads, shards)
    swaps = info.swaps(shard)
    rows, dim = tokens.shape
    width = heads * depth

    @pl.when(shard == 0)
    def turn():
        tokens_t[...] = tokens[...].T
        partner_t[...] = partner[...].T

    fill_weight(info, near, far, weight_scratch)
    weight = weight_scratch[...].reshape(dim, 3 * width)
    grad = dot(grad_proj[...], out_weight[info.head_at ^ shard], 1, 1).astype(BF16)
    k, v, q = (qkv_in[0, :, i * width : (i + 1) * width] for i in range(3))
    stats = stats_in[0]
    key_index = lax.broadcasted_iota(jnp.int32, (rows, 1), 0)
    gq, gk, gv = [], [], []
    for j in range(heads):
        cut = slice(j * depth, (j + 1) * depth)
        live = jnp.where(swaps[j] == 1, info.partner_live, info.own_live)
        open_keys = key_index < live
        scores = dot(k[:, cut], q[:, cut], 1, 1)
        chances = jnp.exp(jnp.where(open_keys, scores - stats[j : j + 1, :], -10000.0))
        grad_mix = dot(v[:, cut], grad[:, cut], 1, 1)
        shared = column_sum(grad_mix * chances)
        grad_scores = (chances * (grad_mix - shared)).astype(BF16)
        gk.append(dot(grad_scores, q[:, cut]))
        gv.append(dot(chances.astype(BF16), grad[:, cut]))
        gq.append(dot(k[:, cut], grad_scores, 0, 0))
    grad_q = (jnp.concatenate(gq, axis=0).T * (depth**-0.5)).astype(BF16)
    grad_kv = jnp.concatenate(gk + gv, axis=1).astype(BF16)
    swapped = lane_pick(swaps + swaps, depth) == 1
    nothing = jnp.zeros((), BF16)
    grad_own = jnp.concatenate([jnp.where(swapped, nothing, grad_kv), grad_q], axis=1)
    grad_far = jnp.where(swapped, grad_kv, nothing)
    own = dot(grad_own, weight, 1, 1)
    other = dot(grad_far, weight[:, : 2 * width], 1, 1)

    @pl.when(shard == 0)
    def first():
        own_out[...] = own
        total[...] = other

    @pl.when(shard > 0)
    def later():
        own_out[...] += own
        total[...] += other

    @pl.when(shard == shards - 1)
    def finish():
        partner_out[...] = total[...].astype(BF16)

    grads = dot(tokens_t[...], grad_own)
    grads_kv = grads[:, : 2 * width] + dot(partner_t[...], grad_far)
    grads = jnp.concatenate([grads_kv, grads[:, 2 * width :]], axis=1).astype(BF16)
    chunks[...] = grads.reshape(chunks.shape)
    for spot in range(PARTS // 2):
        near_out[spot, 0] = chunks[info.part ^ (2 * spot)]
        far_out[spot, 0] = chunks[info.part ^ (2 * spot + 1)]
    bias_out[0] = jnp.broadcast_to(
        jnp.concatenate(
            [column_sum(grad_kv.astype(F32)), column_sum(grad_q.astype(F32))], axis=1
        ),
        bias_out.shape[1:],
    )


def fold_core_kernel(*refs):
    count = (len(refs) - 4) // 2
    mine, received, outs = refs[:count], refs[count : 2 * count], refs[2 * count :]
    for spot in range(4):
        parts = [a[spot, 0].astype(F32) + b[spot, 0].astype(F32) for a, b in zip(mine, received)]
        used = sum(part.shape[1] for part in parts)
        if used < outs[spot].shape[2]:
            parts.append(jnp.zeros((parts[0].shape[0], outs[spot].shape[2] - used), F32))
        value = jnp.concatenate(parts, axis=1) if len(parts) > 1 else parts[0]
        outs[spot][0] = value.astype(outs[spot].dtype)


def fold_chips_kernel(own, a, b, c, *outs):
    for q, out in enumerate(outs):
        value = own[q] + (a[q].astype(F32) + b[q].astype(F32)) + c[q].astype(F32)
        out[...] = value.astype(out.dtype)


def settle_feed_kernel(info, near, far, up_out, down_out, out_out, up_scratch, out_scratch):
    dim = down_out.shape[2]
    for core, source in enumerate((near, far)):
        for spot in range(PARTS // 2):
            place = info[1] ^ (2 * spot + core)
            value = source[spot].astype(F32)
            up_scratch[place] = value[:, :dim]
            down_out[place] = value[:, dim : 2 * dim]
            out_scratch[place] = value[:, 2 * dim :]
    up_out[...] = up_scratch[...].reshape(-1, dim).T
    shards = out_out.shape[0]
    turned = out_scratch[...].reshape(-1, dim).T.reshape(shards, -1, dim)
    for q in range(shards):
        out_out[info[2] ^ q] = turned[q]


def settle_input_kernel(info, near, far, out):
    width = out.shape[3]
    for core, source in enumerate((near, far)):
        for spot in range(PARTS // 2):
            place = info[1] ^ (2 * spot + core)
            value = source[spot].astype(F32)
            for i in range(3):
                out[(i + 1) % 3, place] = value[:, i * width : (i + 1) * width]


def shape(dims, dtype):
    return jax.ShapeDtypeStruct(dims, dtype)


def whole(*dims):
    return pl.BlockSpec(dims, lambda *_: (0,) * len(dims))


SMEM = pl.BlockSpec(memory_space=pltpu.SMEM)


def attend(info, tokens, partner, near, far, bias, out_weight, vectors, heads, depth):
    rows, dim = tokens.shape
    spots, shards, piece, lanes = near.shape
    width = heads * depth
    weight_spec = pl.BlockSpec((spots, 1, piece, lanes), lambda s: (0, s, 0, 0))
    return pl.pallas_call(
        functools.partial(attend_kernel, heads, depth),
        grid=(shards,),
        in_specs=[
            SMEM,
            whole(rows, dim),
            whole(rows, dim),
            weight_spec,
            weight_spec,
            pl.BlockSpec((1, 8, lanes), lambda s: (s, 0, 0)),
            whole(shards, width, dim),
            whole(8, dim),
        ],
        out_specs=[
            pl.BlockSpec((1, rows, lanes), lambda s: (s, 0, 0)),
            pl.BlockSpec((1, rows, width), lambda s: (s, 0, 0)),
            pl.BlockSpec((1, 8, rows), lambda s: (s, 0, 0)),
            whole(rows, dim),
            whole(rows, dim),
        ],
        out_shape=[
            shape((shards, rows, lanes), BF16),
            shape((shards, rows, width), BF16),
            shape((shards, 8, rows), F32),
            shape((rows, dim), F32),
            shape((rows, dim), BF16),
        ],
        scratch_shapes=[pltpu.VMEM((PARTS, piece, lanes), BF16), pltpu.VMEM((rows, dim), F32)],
        compiler_params=PARAMS,
        cost_estimate=pl.CostEstimate(
            flops=12 * rows * dim * dim + 16 * rows * rows * dim,
            bytes_accessed=24 * rows * dim,
            transcendentals=shards * heads * rows * rows,
        ),
        name="attend",
    )(info, tokens, partner, near, far, bias, out_weight, vectors)


def feed_forward(last, normed, weight, bias, *extra):
    rows, dim = normed.shape
    spots, shards, piece, lanes = weight.shape
    tile = shards * piece
    in_specs = [
        whole(rows, dim),
        pl.BlockSpec((1, shards, piece, lanes), lambda s: (s, 0, 0, 0)),
        pl.BlockSpec((1, 1, tile), lambda s: (s, 0, 0)),
    ]
    out_specs = [pl.BlockSpec((rows, tile), lambda s: (0, s))] * 2
    out_shape = [shape((rows, spots * tile), BF16), shape((rows, spots * tile), F32)]
    scratch = []
    if last:
        in_specs += [SMEM] + [whole(rows, dim)] * 3 + [whole(8, dim)]
        out_specs += [whole(rows, dim)] * 3 + [whole(8, dim)]
        out_shape += [
            shape((rows, dim), BF16),
            shape((rows, dim), F32),
            shape((rows, dim), BF16),
            shape((8, dim), F32),
        ]
        scratch = [pltpu.VMEM((rows, dim), F32)]
    else:
        out_specs.append(whole(rows, dim))
        out_shape.append(shape((rows, dim), F32))
    return pl.pallas_call(
        functools.partial(forward_kernel, last),
        grid=(spots,),
        in_specs=in_specs,
        out_specs=out_specs,
        out_shape=out_shape,
        scratch_shapes=scratch,
        compiler_params=PARAMS,
        cost_estimate=pl.CostEstimate(
            flops=4 * rows * dim * tile * spots,
            bytes_accessed=24 * rows * dim,
            transcendentals=2 * rows * tile * spots,
        ),
        name="feed_last" if last else "feed_first",
    )(normed, weight, bias, *extra)


def feed_back(last, normed, grad_branch, weight, hidden, slope, *extra):
    rows, dim = normed.shape
    spots, shards, piece, lanes = weight.shape
    tile = shards * piece
    weight_spec = pl.BlockSpec((1, shards, piece, lanes), lambda s: (s, 0, 0, 0))
    in_specs = [
        whole(rows, dim),
        whole(rows, dim),
        weight_spec,
        pl.BlockSpec((rows, tile), lambda s: (0, s)),
        pl.BlockSpec((rows, tile), lambda s: (0, s)),
    ]
    out_specs = [weight_spec, pl.BlockSpec((1, 8, tile), lambda s: (s, 0, 0))]
    out_shape = [shape(weight.shape, BF16), shape((spots, 8, tile), F32)]
    scratch = []
    if last:
        width = extra[4].shape[2]
        in_specs += [SMEM] + [whole(rows, dim)] * 3 + [whole(shards, rows, width), whole(8, dim)]
        out_specs += [whole(rows, dim)] * 2 + [whole(8, dim)]
        out_specs += [whole(spots, shards, piece, width)] * 2
        out_shape += [
            shape((rows, dim), F32),
            shape((rows, dim), BF16),
            shape((8, dim), F32),
            shape((spots, shards, piece, width), BF16),
            shape((spots, shards, piece, width), BF16),
        ]
        scratch = [pltpu.VMEM((rows, dim), F32), pltpu.VMEM((PARTS, piece, width), BF16)]
    else:
        out_specs.append(whole(rows, dim))
        out_shape.append(shape((rows, dim), F32))
    return pl.pallas_call(
        functools.partial(backward_kernel, last),
        grid=(spots,),
        in_specs=in_specs,
        out_specs=out_specs,
        out_shape=out_shape,
        scratch_shapes=scratch,
        compiler_params=PARAMS,
        cost_estimate=pl.CostEstimate(
            flops=8 * rows * dim * tile * spots,
            bytes_accessed=36 * rows * dim,
            transcendentals=0,
        ),
        name="feed_back_last" if last else "feed_back_first",
    )(normed, grad_branch, weight, hidden, slope, *extra)


def attend_back(
    info, tokens, partner, grad_proj, near, far, out_weight, qkv, stats, heads, depth
):
    rows, dim = tokens.shape
    spots, shards, piece, lanes = near.shape
    width = heads * depth
    weight_spec = pl.BlockSpec((spots, 1, piece, lanes), lambda s: (0, s, 0, 0))
    return pl.pallas_call(
        functools.partial(attend_back_kernel, heads, depth),
        grid=(shards,),
        in_specs=[
            SMEM,
            whole(rows, dim),
            whole(rows, dim),
            whole(rows, dim),
            weight_spec,
            weight_spec,
            whole(shards, width, dim),
            pl.BlockSpec((1, rows, lanes), lambda s: (s, 0, 0)),
            pl.BlockSpec((1, 8, rows), lambda s: (s, 0, 0)),
        ],
        out_specs=[
            whole(rows, dim),
            whole(rows, dim),
            weight_spec,
            weight_spec,
            pl.BlockSpec((1, 8, lanes), lambda s: (s, 0, 0)),
        ],
        out_shape=[
            shape((rows, dim), F32),
            shape((rows, dim), BF16),
            shape(near.shape, BF16),
            shape(far.shape, BF16),
            shape((shards, 8, lanes), F32),
        ],
        scratch_shapes=[
            pltpu.VMEM((PARTS, piece, lanes), BF16),
            pltpu.VMEM((dim, rows), BF16),
            pltpu.VMEM((dim, rows), BF16),
            pltpu.VMEM((rows, dim), F32),
            pltpu.VMEM((PARTS, piece, lanes), BF16),
        ],
        compiler_params=PARAMS,
        cost_estimate=pl.CostEstimate(
            flops=24 * rows * dim * dim + 40 * rows * rows * dim,
            bytes_accessed=32 * rows * dim,
            transcendentals=shards * heads * rows * rows,
        ),
        name="attend_back",
    )(info, tokens, partner, grad_proj, near, far, out_weight, qkv, stats)


def fold_core(mine, received, lanes):
    spots, shards, piece = mine[0].shape[:3]
    specs = [
        pl.BlockSpec((spots, 1, piece, a.shape[3]), lambda s: (0, s, 0, 0))
        for a in mine + received
    ]
    return pl.pallas_call(
        fold_core_kernel,
        grid=(shards,),
        in_specs=specs,
        out_specs=[pl.BlockSpec((1, piece, lanes), lambda s: (s, 0, 0))] * spots,
        out_shape=[shape((shards, piece, lanes), F32)]
        + [shape((shards, piece, lanes), BF16)] * (spots - 1),
        compiler_params=PARAMS,
        cost_estimate=pl.CostEstimate(
            flops=spots * shards * piece * lanes,
            bytes_accessed=8 * spots * shards * piece * lanes,
            transcendentals=0,
        ),
        name="fold_core",
    )(*mine, *received)


def fold_chips(own, received):
    shards, piece, lanes = own.shape
    cut = 256 if lanes % 256 == 0 else lanes
    spec = pl.BlockSpec((shards, piece, cut), lambda s: (0, 0, s))
    return pl.pallas_call(
        fold_chips_kernel,
        grid=(lanes // cut,),
        in_specs=[spec] * 4,
        out_specs=[pl.BlockSpec((piece, cut), lambda s: (0, s))] * shards,
        out_shape=[shape((piece, lanes), F32)] + [shape((piece, lanes), BF16)] * (shards - 1),
        compiler_params=PARAMS,
        cost_estimate=pl.CostEstimate(
            flops=4 * shards * piece * lanes,
            bytes_accessed=12 * shards * piece * lanes,
            transcendentals=0,
        ),
        name="fold_chips",
    )(own, *received)


class Mover:
    def __init__(self, batch_size, shards):
        self.batch_size, self.shards = batch_size, shards

    def batch(self, value, mask):
        return lax.ppermute(value, "batch", [(i, i ^ mask) for i in range(self.batch_size)])

    def head(self, value, mask):
        return lax.ppermute(value, "head", [(i, i ^ mask) for i in range(self.shards)])

    def around(self, value):
        return [self.batch(value, mask) for mask in (NEAR_X, NEAR_Y, NEAR_X | NEAR_Y)]

    def along(self, values):
        return [self.head(value, q) for q, value in enumerate(values, 1)]

    def gather(self, piece):
        column = jnp.stack([piece] + self.along([piece] * (self.shards - 1)))
        near = jnp.stack([column] + self.around(column))
        return near, self.batch(near, CORE)

    def reduce(self, own, send):
        masks = (NEAR_X, NEAR_Y, NEAR_X | NEAR_Y)
        received = [self.batch(value, mask) for value, mask in zip(send, masks)]
        sums = fold_chips(own, received)
        total = sums[0]
        for value in self.along(sums[1:]):
            total = total + value.astype(F32)
        total = total.astype(BF16)
        mask = PARTS
        while mask < self.batch_size:
            total = (total.astype(F32) + self.batch(total, mask).astype(F32)).astype(BF16)
            mask *= 2
        return total

    def spread(self, piece):
        near = jnp.stack([piece] + self.around(piece))
        return near, self.batch(near, CORE)

    def total(self, value):
        mask = 1
        while mask < self.batch_size:
            value = value + self.batch(value, mask)
            mask *= 2
        mask = 1
        while mask < self.shards:
            value = value + self.head(value, mask)
            mask *= 2
        return value


def exchange_bits(value, axes):
    for axis, bit in axes:
        value = jnp.where(bit == 1, jnp.flip(value, axis), value)
    return value


def stack8(*rows):
    rows = [row.reshape(1, -1) for row in rows]
    return jnp.concatenate(rows + [jnp.zeros((8 - len(rows), rows[0].shape[1]), F32)], axis=0)


def local(
    batch_size,
    shards,
    tokens,
    lengths,
    block_swap,
    input_weight,
    input_bias,
    out_weight,
    out_bias,
    gain_one,
    shift_one,
    up_weight,
    up_bias,
    down_weight,
    down_bias,
    gain_two,
    shift_two,
    cotangent,
):
    move = Mover(batch_size, shards)
    heads = block_swap.shape[0]
    rows, dim = tokens.shape
    width = input_weight.shape[2]
    depth = width // heads
    hidden_own = up_weight.shape[1]
    piece = dim // PARTS
    batch_at, head_at = lax.axis_index("batch"), lax.axis_index("head")
    part = batch_at % PARTS
    part_bits = [(part >> i) & 1 for i in range(3)]
    head_bits = [(head_at >> i) & 1 for i in range(2)]
    blocks = SEQ_LEN // rows
    length = lax.dynamic_index_in_dim(lengths, head_at // blocks, 0, keepdims=False)
    block_at = head_at % blocks
    own_live = jnp.clip(length - block_at * rows, 0, rows)
    partner_live = jnp.clip(length - (blocks - 1 - block_at) * rows, 0, rows)

    input_piece = lax.dynamic_slice_in_dim(input_weight, part * piece, piece, 1)
    input_piece = jnp.concatenate([input_piece[1], input_piece[2], input_piece[0]], axis=1)
    small = jnp.concatenate([input_bias.reshape(-1), block_swap.astype(F32)])
    small = jnp.stack([small] + move.along([small] * (shards - 1)))
    input_near, input_far = move.gather(input_piece)
    partner = move.head(tokens, 1)
    up_piece = lax.dynamic_slice_in_dim(up_weight, part * piece, piece, 1).T
    down_piece = lax.dynamic_slice_in_dim(down_weight, part * piece, piece, 0)
    feed_piece = jnp.concatenate([up_piece, down_piece], axis=1)
    feed_piece, partner = lax.optimization_barrier((feed_piece, partner))
    feed_near, feed_far = move.gather(feed_piece)

    info = jnp.concatenate(
        [
            small[:, 2 * width :].reshape(-1).astype(jnp.int32),
            jnp.stack([own_live, partner_live, part, head_at]).astype(jnp.int32),
        ]
    )
    short_info = jnp.stack([own_live, part, head_at]).astype(jnp.int32)
    bias = jnp.concatenate(
        [jnp.zeros((shards, width), F32), small[:, width : 2 * width], small[:, :width]], axis=1
    )
    bias = jnp.broadcast_to(bias[:, None], (shards, 8, 3 * width))
    bits = [(0, head_bits[1]), (1, head_bits[0])]
    bits += [(2, part_bits[2]), (3, part_bits[1]), (4, part_bits[0])]
    up_bias_rel = exchange_bits(up_bias.reshape(2, 2, 2, 2, 2, piece), bits)
    up_bias_rel = up_bias_rel.transpose(4, 2, 3, 0, 1, 5).reshape(2, 4, 1, shards * piece)
    out_parts = out_weight.reshape(shards, width, dim)

    qkv, context, stats, rows_one, normed = attend(
        info,
        tokens,
        partner,
        input_near,
        input_far,
        bias,
        out_parts,
        stack8(out_bias, gain_one, shift_one),
        heads,
        depth,
    )
    hidden_near, slope_near, branch = feed_forward(False, normed, feed_near, up_bias_rel[0])
    hidden_far, slope_far, mixed_out, grad_second, grad_branch, sums_two = feed_forward(
        True,
        normed,
        feed_far,
        up_bias_rel[1],
        short_info,
        branch,
        rows_one,
        cotangent,
        stack8(gain_one, shift_one, down_bias, gain_two, shift_two),
    )

    feed_grads_far, up_bias_far, grad_normed = feed_back(
        False, normed, grad_branch, feed_far, hidden_far, slope_far
    )
    feed_received = move.batch(feed_grads_far, CORE)
    (
        feed_grads_near,
        up_bias_near,
        grad_first,
        grad_proj,
        sums_one,
        out_grads_near,
        out_grads_far,
    ) = feed_back(
        True,
        normed,
        grad_branch,
        feed_near,
        hidden_near,
        slope_near,
        short_info,
        grad_normed,
        rows_one,
        grad_second,
        context,
        stack8(gain_one),
    )
    out_received = move.batch(out_grads_far, CORE)
    lanes = -(-(2 * dim + width) // 256) * 256
    feed_own, *feed_send = fold_core(
        [feed_grads_near, out_grads_near], [feed_received, out_received], lanes
    )
    own_rows, partner_rows, input_grads_near, input_grads_far, bias_sums = attend_back(
        info,
        tokens,
        partner,
        grad_proj,
        input_near,
        input_far,
        out_parts,
        qkv,
        stats,
        heads,
        depth,
    )
    feed_total = move.reduce(feed_own, feed_send)
    out_total = feed_total[:, 2 * dim : 2 * dim + width]
    out_total = [out_total] + move.along([out_total] * (shards - 1))
    feed_total = jnp.concatenate([feed_total[:, : 2 * dim]] + out_total, axis=1)
    feed_done = move.spread(feed_total)

    from_partner = move.head(partner_rows, 1)
    input_received = move.batch(input_grads_far, CORE)
    input_own, *input_send = fold_core([input_grads_near], [input_received], 3 * width)
    input_total = move.reduce(input_own, input_send)
    input_done = move.spread(input_total)
    grad_tokens = grad_first + own_rows + from_partner.astype(F32)

    up_bias_grad = jnp.stack([up_bias_near[:, 0], up_bias_far[:, 0]])
    up_bias_grad = up_bias_grad.reshape(2, 2, 2, 2, 2, piece).transpose(3, 4, 1, 2, 0, 5)
    up_bias_grad = exchange_bits(up_bias_grad, bits).reshape(-1, dim)
    bias_sums = exchange_bits(bias_sums[:, 0].reshape(2, 2, 3, width), bits[:2])
    bias_sums = bias_sums.reshape(shards, 3, width).transpose(1, 0, 2).reshape(3, dim)
    vectors = move.total(
        jnp.concatenate([sums_one[:3], sums_two[:3], bias_sums[2:], bias_sums[1:2], up_bias_grad])
    )
    grad_input_bias = lax.dynamic_slice_in_dim(vectors[6:8], head_at * width, width, 1)
    grad_up_bias = lax.dynamic_slice_in_dim(
        vectors[8:].reshape(-1), head_at * hidden_own, hidden_own
    )

    grad_up, grad_down, grad_out = pl.pallas_call(
        settle_feed_kernel,
        in_specs=[SMEM] + [whole(4, piece, 2 * dim + shards * width)] * 2,
        out_shape=[
            shape((dim, hidden_own), F32),
            shape((PARTS, piece, dim), F32),
            shape((shards, width, dim), F32),
        ],
        scratch_shapes=[pltpu.VMEM((PARTS, piece, dim), F32)] * 2,
        compiler_params=PARAMS,
        name="settle_feed",
    )(short_info, *feed_done)
    grad_input_weight = pl.pallas_call(
        settle_input_kernel,
        in_specs=[SMEM] + [whole(4, piece, 3 * width)] * 2,
        out_shape=shape((3, PARTS, piece, width), F32),
        compiler_params=PARAMS,
        name="settle_input",
    )(short_info, *input_done)
    return (
        mixed_out,
        grad_tokens,
        grad_input_weight.reshape(3, dim, width),
        grad_input_bias,
        grad_out.reshape(dim, dim),
        vectors[0],
        vectors[1],
        vectors[2],
        grad_up,
        grad_up_bias,
        grad_down.reshape(hidden_own, dim),
        vectors[3],
        vectors[4],
        vectors[5],
    )


def solution(mesh):
    rows_spec = P(("batch", "head"), None)
    placed = (
        rows_spec,
        P("batch"),
        P("head"),
        P(None, None, "head"),
        P(None, "head"),
        P(),
        P(),
        P(),
        P(),
        P(None, "head"),
        P(),
        P("head", None),
        P(),
        P(),
        P(),
        rows_spec,
    )
    return jax.shard_map(
        functools.partial(local, mesh.shape["batch"], mesh.shape["head"]),
        mesh=mesh,
        in_specs=placed,
        out_specs=(
            rows_spec,
            rows_spec,
            P(None, None, "head"),
            P(None, "head"),
            P(),
            P(),
            P(),
            P(),
            P(None, "head"),
            P("head"),
            P("head", None),
            P(),
            P(),
            P(),
        ),
        check_vma=False,
    )
```

time: 842 us -> 459 us (0.55)
  waiting for transfers between devices: 611 us -> 230 us
  Pallas kernels: 39.1 us -> 129 us
  starting transfers between devices: 4.91 us -> 66.1 us
  matrix products: 57.8 us -> 0 us
  blocking collectives: 38.3 us -> 0 us
  local copies, waits for them, and re-layouts: 54.9 us -> 19.8 us
  between operations: 16.4 us -> 2.6 us
    reduce_scatter x3 -> x0, waiting for transfers between devices: 244 us -> none  [the longest x2 201 us: collect(): piece = lax.psum_scatter(grads, both, scatter_dimension=axis, tiled=True)]
    all_gather x7 -> x0, waiting for transfers between devices: 244 us -> none  [the longest x3 126 us: share(): return lax.all_gather(piece, both, axis=axis, tiled=True)]
    ppermute x2 -> x50, waiting for transfers between devices: 17.1 us -> 230 us  [the longest x28 138 us: batch(): lax.ppermute(value, 'batch', [(i, i ^ mask) for i in range(self.batch_siz...]
    unnamed x12 -> x0, waiting for transfers between devices: 106 us -> none
    pallas_call x0 -> x10, Pallas kernels: none -> 81.5 us  [the longest x2 28 us: feed_back(): pl.pallas_call(functools.partial(backward_kernel, last), grid=(spots,), i...]
    ppermute x2 -> x50, starting transfers between devices: 4.46 us -> 66.1 us  [the longest x22 40.9 us: head(): lax.ppermute(value, 'head', [(i, i ^ mask) for i in range(self.shards)])]
    dot_general x9 -> x0, matrix products: 57.8 us -> none  [the longest x1 20.2 us: local(): jnp.einsum('td,sdh->sth', normed_low, up_all, preferred_element_type=F32)]
    unnamed x82 -> x57, local copies, waits for them, and re-layouts: 37.5 us -> 7.7 us
  transfers between devices with their start and end apart: 13 -> 50, of which waited for: 12 -> 30; matrix products, arithmetic and copies ran while one was open for 11% -> 5% of each run, Pallas kernels for 5% -> 20%
where the time goes in v2:
time: 459 us; the launch traced here: 458 us
  waiting for transfers between devices  230 us (50%)
  Pallas kernels  129 us (28%)
  starting transfers between devices  66.1 us (14%)
  local copies, waits for them, and re-layouts  19.8 us (4%)
  other arithmetic  11 us (2%)
    ppermute x28, waiting for transfers between devices, batch(): lax.ppermute(value, 'batch', [(i, i ^ mask) for i in range(self.batch_siz...  138 us
    ppermute x22, waiting for transfers between devices, head(): lax.ppermute(value, 'head', [(i, i ^ mask) for i in range(self.shards)])  91.7 us
    ppermute x22, starting transfers between devices, head(): lax.ppermute(value, 'head', [(i, i ^ mask) for i in range(self.shards)])  40.9 us
    pallas_call x1, Pallas kernels, attend_back(): pl.pallas_call(functools.partial(attend_back_kernel, heads, depth), grid=...  28.2 us
    pallas_call x2, Pallas kernels, feed_back(): pl.pallas_call(functools.partial(backward_kernel, last), grid=(spots,), i...  28 us
    ppermute x28, starting transfers between devices, batch(): lax.ppermute(value, 'batch', [(i, i ^ mask) for i in range(self.batch_siz...  25.2 us
    pallas_call x2, Pallas kernels, feed_forward(): pl.pallas_call(functools.partial(forward_kernel, last), grid=(spots,), in...  24.5 us
    pallas_call x1, Pallas kernels, attend(): pl.pallas_call(functools.partial(attend_kernel, heads, depth), grid=(shar...  18.9 us
  transfers between devices with their start and end apart: 50, of which 30 were waited for; matrix products, arithmetic and copies ran while one was open for 5% of the time, Pallas kernels for 20%

profile of v2, /device:TPU:0, one launch (start us, length us, event | category | flops | bytes accessed | tf_op | source)
XLA Modules:
  0.0 458.0 jit_solution(14032561551914692748)
XLA Ops:
  0.7 3.1 collective-permute-start.3
  5.0 16.5 %collective-permute-done.3.partner = bf16[512,768]{1,0:T(8,128)(2,1)S(1)} collective-permute-done((bf16[512,768]{1,0:T(8,128)(2,1)}, bf16[512,768]{1,0:T(8,128)(2,1)S(1)}, u32[]{:S(2)}, u32[]{:S(2)}) %collective-permute-start.3) | collective-permute-done | bytes 786464 | tf_op jit(solution)/shard_map/ppermute | solution.py:649
  21.5 3.8 collective-permute-start.13
  25.9 7.5 %collective-permute-done.13 = bf16[96,1536]{1,0:T(8,128)(2,1)S(1)} collective-permute-done((bf16[96,1536]{1,0:T(8,128)(2,1)S(1)}, bf16[96,1536]{1,0:T(8,128)(2,1)S(1)}, u32[]{:S(2)}, u32[]{:S(2)}) %collective-permute-start.13) | collective-permute-done | bytes 294944 | tf_op jit(solution)/shard_map/ppermute | solution.py:649
  33.3 16.2 %collective-permute-done.12 = bf16[96,1536]{1,0:T(8,128)(2,1)S(1)} collective-permute-done((bf16[96,1536]{1,0:T(8,128)(2,1)S(1)}, bf16[96,1536]{1,0:T(8,128)(2,1)S(1)}, u32[]{:S(2)}, u32[]{:S(2)}) %collective-permute-start.12) | collective-permute-done | bytes 294944 | tf_op jit(solution)/shard_map/ppermute | solution.py:649
  53.3 24.5 %collective-permute-done.15 = bf16[4,96,1536]{2,1,0:T(8,128)(2,1)S(1)} collective-permute-done((bf16[4,96,1536]{2,1,0:T(8,128)(2,1)S(1)}, bf16[4,96,1536]{2,1,0:T(8,128)(2,1)S(1)}, u32[]{:S(2)}, u32[]{:S(2)}) %collective-permute-start.15) | collective-permute-done | bytes 1179680 | tf_op jit(solution)/shard_map/ppermute | solution.py:646
  80.2 22.9 %collective-permute-done.16 = bf16[4,96,1536]{2,1,0:T(8,128)(2,1)S(1)} collective-permute-done((bf16[4,96,1536]{2,1,0:T(8,128)(2,1)S(1)}, bf16[4,96,1536]{2,1,0:T(8,128)(2,1)S(1)}, u32[]{:S(2)}, u32[]{:S(2)}) %collective-permute-start.16) | collective-permute-done | bytes 1179680 | tf_op jit(solution)/shard_map/ppermute | solution.py:646
  122.0 9.7 %collective-permute-done.8 = bf16[4,96,576]{2,1,0:T(8,128)(2,1)S(1)} collective-permute-done((bf16[4,96,576]{2,1,0:T(8,128)(2,1)S(1)}, bf16[4,96,576]{2,1,0:T(8,128)(2,1)S(1)}, u32[]{:S(2)}, u32[]{:S(2)}) %collective-permute-start.8) | collective-permute-done | bytes 442400 | tf_op jit(solution)/shard_map/ppermute | solution.py:646
  131.8 3.8 collective-permute-start.1
  137.1 5.6 %collective-permute-done.9 = bf16[4,96,576]{2,1,0:T(8,128)(2,1)S(1)} collective-permute-done((bf16[4,96,576]{2,1,0:T(8,128)(2,1)S(1)}, bf16[4,96,576]{2,1,0:T(8,128)(2,1)S(1)}, u32[]{:S(2)}, u32[]{:S(2)}) %collective-permute-start.9) | collective-permute-done | bytes 442400 | tf_op jit(solution)/shard_map/ppermute | solution.py:646
  150.7 18.9 %attend.1 = (bf16[4,512,576]{2,1,0:T(8,128)(2,1)}, bf16[4,512,192]{2,1,0:T(8,128)(2,1)}, f32[4,8,512]{2,1,0:T(8,128)}, f32[512,768]{1,0:T(8,128)}, bf16[512,768]{1,0:T(8,128)(2,1)}) custom-call(s32[16]{0:T(128)} %concatenate.33.info_ref, bf16[512,768]{1,0:T(8,128)(2,1)} %tokens.3, bf16[512,768]{1,0:T(8,128)(2,1)} %copy-done.23, ...), custom_call_target="tpu_custom_call" | custom-call | flops 6845104128 | bytes 9437184 | tf_op jit(solution)/shard_map/attend/pallas_call | solution.py:418
  169.6 10.3 %feed_first.1 = (bf16[512,1536]{1,0:T(8,128)(2,1)}, f32[512,1536]{1,0:T(8,128)}, f32[512,768]{1,0:T(8,128)}) custom-call(bf16[512,768]{1,0:T(8,128)(2,1)} %get-tuple-element.65.normed, bf16[4,4,96,1536]{3,2,1,0:T(8,128)(2,1)} %pad_maximum_fusion.weight, f32[4,1,384]{2,1,0:T(1,128)} %squeeze.42.bias), custom_call_target="tpu_custom_call" | custom-call | flops 2415919104 | bytes 9437184 | tf_op jit(solution)/shard_map/feed_first/pallas_call | solution.py:481
  179.9 14.1 %feed_last.1 = (bf16[512,1536]{1,0:T(8,128)(2,1)}, f32[512,1536]{1,0:T(8,128)}, bf16[512,768]{1,0:T(8,128)(2,1)}, f32[512,768]{1,0:T(8,128)}, bf16[512,768]{1,0:T(8,128)(2,1)}, /*index=5*/f32[8,768]{1,0:T(8,128)}) custom-call(bf16[512,768]{1,0:T(8,128)(2,1)} %get-tuple-element.65.normed, bf16[4,4,96,1536]{3,2,1,0:T(8,128)(2,1)} %collective-permute-done.17.weight, ...), custom_call_target="tpu_custom_call" | custom-call | flops 2415919104 | bytes 9437184 | tf_op jit(solution)/shard_map/feed_last/pallas_call | solution.py:481
  194.1 11.5 %feed_back_first.1 = (bf16[4,4,96,1536]{3,2,1,0:T(8,128)(2,1)}, f32[4,8,384]{2,1,0:T(8,128)}, f32[512,768]{1,0:T(8,128)}) custom-call(bf16[512,768]{1,0:T(8,128)(2,1)} %get-tuple-element.65.normed, bf16[512,768]{1,0:T(8,128)(2,1)} %get-tuple-element.70.grad_branch, bf16[4,4,96,1536]{3,2,1,0:T(8,128)(2,1)} %collective-permute-done.17.weight, ...), custom_call_target="tpu_custom_call" | custom-call | flops 4831838208 | bytes 14155776 | tf_op jit(solution)/shard_map/feed_back_first/pallas_call | solution.py:529
  205.8 16.5 %feed_back_last.1 = (bf16[4,4,96,1536]{3,2,1,0:T(8,128)(2,1)}, f32[4,8,384]{2,1,0:T(8,128)}, f32[512,768]{1,0:T(8,128)}, bf16[512,768]{1,0:T(8,128)(2,1)}, f32[8...) custom-call(bf16[512,768]{1,0:T(8,128)(2,1)} %get-tuple-element.65.normed, ...), custom_call_target="tpu_custom_call" | custom-call | flops 4831838208 | bytes 14155776 | tf_op jit(solution)/shard_map/feed_back_last/pallas_call | solution.py:529
  225.7 6.9 %fold_core.3 = (f32[4,96,1792]{2,1,0:T(8,128)}, bf16[4,96,1792]{2,1,0:T(8,128)(2,1)}, bf16[4,96,1792]{2,1,0:T(8,128)(2,1)}, bf16[4,96,1792]{2,1,0:T(8,128)(2,1)}) custom-call(bf16[4,4,96,1536]{3,2,1,0:T(8,128)(2,1)} %get-tuple-element.99.refs_0_, bf16[4,4,96,192]{3,2,1,0:T(8,128)(2,1)} %get-tuple-element.100.refs_1_, ...), custom_call_target="tpu_custom_call" | custom-call | flops 2752512 | bytes 22020096 | tf_op jit(solution)/shard_map/fold_core/pallas_call | solution.py:604
  236.1 28.2 %attend_back.1 = (f32[512,768]{1,0:T(8,128)}, bf16[512,768]{1,0:T(8,128)(2,1)}, bf16[4,4,96,576]{3,2,1,0:T(8,128)(2,1)}, bf16[4,4,96,576]{3,2,1,0:T(8,128)(2,1)}, f32[4,8,576]{2,1,0:T(8,128)}) custom-call(s32[16]{0:T(128)} %concatenate.33.info_ref, bf16[512,768]{1,0:T(8,128)(2,1)} %tokens.3, bf16[512,768]{1,0:T(8,128)(2,1)} %copy-done.23, ...), custom_call_target="tpu_custom_call" | custom-call | flops 15300820992 | bytes 12582912 | tf_op jit(solution)/shard_map/attend_back/pallas_call | solution.py:553
  265.8 30.0 %collective-permute-done.38.b = bf16[4,96,1792]{2,1,0:T(8,128)(2,1)S(1)} collective-permute-done((bf16[4,96,1792]{2,1,0:T(8,128)(2,1)}, bf16[4,96,1792]{2,1,0:T(8,128)(2,1)S(1)}, u32[]{:S(2)}, u32[]{:S(2)}) %collective-permute-start.38) | collective-permute-done | bytes 1376288 | tf_op jit(solution)/shard_map/ppermute | solution.py:646
  297.4 6.2 %fold_chips.3 = (f32[96,1792]{1,0:T(8,128)}, bf16[96,1792]{1,0:T(8,128)(2,1)}, bf16[96,1792]{1,0:T(8,128)(2,1)}, bf16[96,1792]{1,0:T(8,128)(2,1)}) custom-call(f32[4,96,1792]{2,1,0:T(8,128)} %get-tuple-element.103.own, bf16[4,96,1792]{2,1,0:T(8,128)(2,1)} %copy-done.5, bf16[4,96,1792]{2,1,0:T(8,128)(2,1)} %copy-done.6, bf16[4,96,1792]{2,1,0:T(8,128)(2,1)} %copy-done.7), custom_call_target="tpu_custom_call" | custom-call | flops 2752512 | bytes 8257536 | tf_op jit(solution)/shard_map/fold_chips/pallas_call | solution.py:625
  303.6 3.8 collective-permute-start.40
  309.9 10.9 %collective-permute-done.40 = bf16[96,1792]{1,0:T(8,128)(2,1)S(1)} collective-permute-done((bf16[96,1792]{1,0:T(8,128)(2,1)}, bf16[96,1792]{1,0:T(8,128)(2,1)S(1)}, u32[]{:S(2)}, u32[]{:S(2)}) %collective-permute-start.40) | collective-permute-done | bytes 344096 | tf_op jit(solution)/shard_map/ppermute | solution.py:649
  320.8 13.5 %collective-permute-done.41 = bf16[96,1792]{1,0:T(8,128)(2,1)S(1)} collective-permute-done((bf16[96,1792]{1,0:T(8,128)(2,1)}, bf16[96,1792]{1,0:T(8,128)(2,1)S(1)}, u32[]{:S(2)}, u32[]{:S(2)}) %collective-permute-start.41) | collective-permute-done | bytes 344096 | tf_op jit(solution)/shard_map/ppermute | solution.py:649
  338.0 5.1 %collective-permute-start.44 = (bf16[96,192]{1,0:T(8,128)(2,1)S(1)}, bf16[96,192]{1,0:T(8,128)(2,1)S(1)}, u32[]{:S(2)}, u32[]{:S(2)}) collective-permute-start(bf16[96,192]{1,0:T(8,128)(2,1)S(1)} %slice.119), channel_id=1, source_target_pairs={{0,2},{1,3},{2,0},{3,1},{4,6},{5,7},{6,4},{7,5},{8,10},{9,11},{10,... | collective-permute-start | bytes 110600 | tf_op jit(solution)/shard_map/ppermute | solution.py:649
  350.9 10.3 %collective-permute-done.48 = bf16[96,2304]{1,0:T(8,128)(2,1)S(1)} collective-permute-done((bf16[96,2304]{1,0:T(8,128)(2,1)S(1)}, bf16[96,2304]{1,0:T(8,128)(2,1)S(1)}, u32[]{:S(2)}, u32[]{:S(2)}) %collective-permute-start.48) | collective-permute-done | bytes 442400 | tf_op jit(solution)/shard_map/ppermute | solution.py:646
  361.2 4.7 %collective-permute-done.47 = bf16[96,2304]{1,0:T(8,128)(2,1)S(1)} collective-permute-done((bf16[96,2304]{1,0:T(8,128)(2,1)S(1)}, bf16[96,2304]{1,0:T(8,128)(2,1)S(1)}, u32[]{:S(2)}, u32[]{:S(2)}) %collective-permute-start.47) | collective-permute-done | bytes 442400 | tf_op jit(solution)/shard_map/ppermute | solution.py:646
  366.9 4.7 %fold_core.2 = (f32[4,96,576]{2,1,0:T(8,128)}, bf16[4,96,576]{2,1,0:T(8,128)(2,1)}, bf16[4,96,576]{2,1,0:T(8,128)(2,1)}, bf16[4,96,576]{2,1,0:T(8,128)(2,1)}) custom-call(bf16[4,4,96,576]{3,2,1,0:T(8,128)(2,1)} %get-tuple-element.84.refs_0_, bf16[4,4,96,576]{3,2,1,0:T(8,128)(2,1)} %collective-permute-done.19.refs_1_), custom_call_target="tpu_custom_call" | custom-call | flops 884736 | bytes 7077888 | tf_op jit(solution)/shard_map/fold_core/pallas_call | solution.py:604
  378.3 18.3 %collective-permute-done.31 = f32[12,768]{1,0:T(8,128)S(1)} collective-permute-done((f32[12,768]{1,0:T(8,128)S(1)}, f32[12,768]{1,0:T(8,128)S(1)}, u32[]{:S(2)}, u32[]{:S(2)}) %collective-permute-start.31) | collective-permute-done | bytes 36896 | tf_op jit(solution)/shard_map/ppermute | solution.py:646
  401.9 3.3 collective-permute-done.33
  413.7 11.7 %collective-permute-done.34 = f32[12,768]{1,0:T(8,128)S(1)} collective-permute-done((f32[12,768]{1,0:T(8,128)S(1)}, f32[12,768]{1,0:T(8,128)S(1)}, u32[]{:S(2)}, u32[]{:S(2)}) %collective-permute-start.34) | collective-permute-done | bytes 36896 | tf_op jit(solution)/shard_map/ppermute | solution.py:649
  429.3 3.0 collective-permute-done.25
  442.0 3.5 convert_add_fusion
  452.1 5.9 %settle_feed.1 = (f32[768,768]{1,0:T(8,128)}, f32[8,96,768]{2,1,0:T(8,128)}, f32[4,192,768]{2,1,0:T(8,128)}) custom-call(s32[3]{0:T(128)} %pad_add_fusion.refs_0_.info, bf16[4,96,2304]{2,1,0:T(8,128)(2,1)} %copy-done.2, bf16[4,96,2304]{2,1,0:T(8,128)(2,1)} %collective-permute-done.49.far), custom_call_target="tpu_custom_call" | custom-call | tf_op jit(solution)/shard_map/settle_feed/pallas_call | solution.py:864
  (226 shorter events, 100.6 us)
Async XLA Ops:
  0.7 20.8 %collective-permute-start.3 = (bf16[512,768]{1,0:T(8,128)(2,1)}, bf16[512,768]{1,0:T(8,128)(2,1)S(1)}, u32[]{:S(2)}, u32[]{:S(2)}) collective-permute-start(bf16[512,768]{1,0:T(8,128)(2,1)} %tokens.3), channel_id=1, source_target_pairs={{0,1},{1,0},{2,3},{3,2},{4,5},{5,4},{6,7},{7,6},{8,9},{9,8},{10,11... | collective-permute-start | bytes 2359304 | tf_op jit(solution)/shard_map/ppermute | solution.py:649
  25.3 24.2 %collective-permute-start.12 = (bf16[96,1536]{1,0:T(8,128)(2,1)S(1)}, bf16[96,1536]{1,0:T(8,128)(2,1)S(1)}, u32[]{:S(2)}, u32[]{:S(2)}) collective-permute-start(bf16[96,1536]{1,0:T(8,128)(2,1)S(1)} %pad_maximum_fusion.6), channel_id=1, source_target_pairs={{0,2},{1,3},{2,0},{3,1},{4,6},{5,7},{6,4},{7,5},{8,10},{9,11},{10,... | collective-permute-start | bytes 884744 | tf_op jit(solution)/shard_map/ppermute | solution.py:649
  25.3 24.2 %collective-permute-start.11 = (bf16[96,1536]{1,0:T(8,128)(2,1)S(1)}, bf16[96,1536]{1,0:T(8,128)(2,1)S(1)}, u32[]{:S(2)}, u32[]{:S(2)}) collective-permute-start(bf16[96,1536]{1,0:T(8,128)(2,1)S(1)} %pad_maximum_fusion.6), channel_id=1, source_target_pairs={{0,1},{1,0},{2,3},{3,2},{4,5},{5,4},{6,7},{7,6},{8,9},{9,8},{10,11... | collective-permute-start | bytes 884744 | tf_op jit(solution)/shard_map/ppermute | solution.py:649
  49.7 28.1 %collective-permute-start.15 = (bf16[4,96,1536]{2,1,0:T(8,128)(2,1)S(1)}, bf16[4,96,1536]{2,1,0:T(8,128)(2,1)S(1)}, u32[]{:S(2)}, u32[]{:S(2)}) collective-permute-start(bf16[4,96,1536]{2,1,0:T(8,128)(2,1)S(1)} %get-tuple-element.151), channel_id=1, source_target_pairs={{0,16},{4,20},{8,24},{12,28},{16,0},{20,4},{24,8},{28,12},{1,17},{... | collective-permute-start | bytes 3538952 | tf_op jit(solution)/shard_map/ppermute | solution.py:646
  51.3 28.9 %collective-permute-start.14 = (bf16[4,96,1536]{2,1,0:T(8,128)(2,1)S(1)}, bf16[4,96,1536]{2,1,0:T(8,128)(2,1)S(1)}, u32[]{:S(2)}, u32[]{:S(2)}) collective-permute-start(bf16[4,96,1536]{2,1,0:T(8,128)(2,1)S(1)} %get-tuple-element.151), channel_id=1, source_target_pairs={{0,8},{4,12},{8,0},{12,4},{16,24},{20,28},{24,16},{28,20},{1,9},{5... | collective-permute-start | bytes 3538952 | tf_op jit(solution)/shard_map/ppermute | solution.py:646
  52.8 50.3 %collective-permute-start.16 = (bf16[4,96,1536]{2,1,0:T(8,128)(2,1)S(1)}, bf16[4,96,1536]{2,1,0:T(8,128)(2,1)S(1)}, u32[]{:S(2)}, u32[]{:S(2)}) collective-permute-start(bf16[4,96,1536]{2,1,0:T(8,128)(2,1)S(1)} %get-tuple-element.151), channel_id=1, source_target_pairs={{0,24},{4,28},{8,16},{12,20},{16,8},{20,12},{24,0},{28,4},{1,25},{... | collective-permute-start | bytes 3538952 | tf_op jit(solution)/shard_map/ppermute | solution.py:646
  105.6 74.3 %collective-permute-start.17 = (bf16[4,4,96,1536]{3,2,1,0:T(8,128)(2,1)}, bf16[4,4,96,1536]{3,2,1,0:T(8,128)(2,1)}, u32[]{:S(2)}, u32[]{:S(2)}) collective-permute-start(bf16[4,4,96,1536]{3,2,1,0:T(8,128)(2,1)} %pad_maximum_fusion.weight), channel_id=1, source_target_pairs={{0,4},{4,0},{8,12},{12,8},{16,20},{20,16},{24,28},{28,24},{1,5},{5... | collective-permute-start | bytes 14155784 | tf_op jit(solution)/shard_map/ppermute | solution.py:646
  111.7 37.4 %collective-permute-start.2 = (f32[387]{0:T(512)S(1)}, f32[387]{0:T(512)S(1)}, u32[]{:S(2)}, u32[]{:S(2)}) collective-permute-start(f32[387]{0:T(512)S(1)} %pad_maximum_fusion.10), channel_id=1, source_target_pairs={{0,3},{1,2},{2,1},{3,0},{4,7},{5,6},{6,5},{7,4},{8,11},{9,10},{10,... | collective-permute-start | bytes 4652 | tf_op jit(solution)/shard_map/ppermute | solution.py:649
  120.1 15.4 %collective-permute-start.7 = (bf16[4,96,576]{2,1,0:T(8,128)(2,1)S(1)}, bf16[4,96,576]{2,1,0:T(8,128)(2,1)S(1)}, u32[]{:S(2)}, u32[]{:S(2)}) collective-permute-start(bf16[4,96,576]{2,1,0:T(8,128)(2,1)S(1)} %get-tuple-element.156), channel_id=1, source_target_pairs={{0,8},{4,12},{8,0},{12,4},{16,24},{20,28},{24,16},{28,20},{1,9},{5... | collective-permute-start | bytes 1327112 | tf_op jit(solution)/shard_map/ppermute | solution.py:646
  121.5 21.2 %collective-permute-start.9 = (bf16[4,96,576]{2,1,0:T(8,128)(2,1)S(1)}, bf16[4,96,576]{2,1,0:T(8,128)(2,1)S(1)}, u32[]{:S(2)}, u32[]{:S(2)}) collective-permute-start(bf16[4,96,576]{2,1,0:T(8,128)(2,1)S(1)} %get-tuple-element.156), channel_id=1, source_target_pairs={{0,24},{4,28},{8,16},{12,20},{16,8},{20,12},{24,0},{28,4},{1,25},{... | collective-permute-start | bytes 1327112 | tf_op jit(solution)/shard_map/ppermute | solution.py:646
  131.8 17.4 %collective-permute-start.1 = (f32[387]{0:T(512)S(1)}, f32[387]{0:T(512)S(1)}, u32[]{:S(2)}, u32[]{:S(2)}) collective-permute-start(f32[387]{0:T(512)S(1)} %pad_maximum_fusion.10), channel_id=1, source_target_pairs={{0,2},{1,3},{2,0},{3,1},{4,6},{5,7},{6,4},{7,5},{8,10},{9,11},{10,... | collective-permute-start | bytes 4652 | tf_op jit(solution)/shard_map/ppermute | solution.py:649
  135.5 13.6 %collective-permute-start = (f32[387]{0:T(512)S(1)}, f32[387]{0:T(512)S(1)}, u32[]{:S(2)}, u32[]{:S(2)}) collective-permute-start(f32[387]{0:T(512)S(1)} %pad_maximum_fusion.10), channel_id=1, source_target_pairs={{0,1},{1,0},{2,3},{3,2},{4,5},{5,4},{6,7},{7,6},{8,9},{9,8},{10,11... | collective-permute-start | bytes 4652 | tf_op jit(solution)/shard_map/ppermute | solution.py:649
  205.6 19.3 %collective-permute-start.35 = (bf16[4,4,96,1536]{3,2,1,0:T(8,128)(2,1)}, bf16[4,4,96,1536]{3,2,1,0:T(8,128)(2,1)}, u32[]{:S(2)}, u32[]{:S(2)}) collective-permute-start(bf16[4,4,96,1536]{3,2,1,0:T(8,128)(2,1)} %get-tuple-element.101), channel_id=1, source_target_pairs={{0,4},{4,0},{8,12},{12,8},{16,20},{20,16},{24,28},{28,24},{1,5},{5... | collective-permute-start | bytes 14155784 | tf_op jit(solution)/shard_map/ppermute | solution.py:646
  232.6 33.2 %collective-permute-start.37 = (bf16[4,96,1792]{2,1,0:T(8,128)(2,1)}, bf16[4,96,1792]{2,1,0:T(8,128)(2,1)S(1)}, u32[]{:S(2)}, u32[]{:S(2)}) collective-permute-start(bf16[4,96,1792]{2,1,0:T(8,128)(2,1)} %get-tuple-element.104), channel_id=1, source_target_pairs={{0,8},{4,12},{8,0},{12,4},{16,24},{20,28},{24,16},{28,20},{1,9},{5... | collective-permute-start | bytes 4128776 | tf_op jit(solution)/shard_map/ppermute | solution.py:646
  234.0 61.8 %collective-permute-start.38 = (bf16[4,96,1792]{2,1,0:T(8,128)(2,1)}, bf16[4,96,1792]{2,1,0:T(8,128)(2,1)S(1)}, u32[]{:S(2)}, u32[]{:S(2)}) collective-permute-start(bf16[4,96,1792]{2,1,0:T(8,128)(2,1)} %get-tuple-element.105), channel_id=1, source_target_pairs={{0,16},{4,20},{8,24},{12,28},{16,0},{20,4},{24,8},{28,12},{1,17},{... | collective-permute-start | bytes 4128776 | tf_op jit(solution)/shard_map/ppermute | solution.py:646
  235.3 60.5 %collective-permute-start.39 = (bf16[4,96,1792]{2,1,0:T(8,128)(2,1)}, bf16[4,96,1792]{2,1,0:T(8,128)(2,1)S(1)}, u32[]{:S(2)}, u32[]{:S(2)}) collective-permute-start(bf16[4,96,1792]{2,1,0:T(8,128)(2,1)} %get-tuple-element.106), channel_id=1, source_target_pairs={{0,24},{4,28},{8,16},{12,20},{16,8},{20,12},{24,0},{28,4},{1,25},{... | collective-permute-start | bytes 4128776 | tf_op jit(solution)/shard_map/ppermute | solution.py:646
  264.3 102.5 %collective-permute-start.19 = (bf16[4,4,96,576]{3,2,1,0:T(8,128)(2,1)}, bf16[4,4,96,576]{3,2,1,0:T(8,128)(2,1)}, u32[]{:S(2)}, u32[]{:S(2)}) collective-permute-start(bf16[4,4,96,576]{3,2,1,0:T(8,128)(2,1)} %get-tuple-element.85), channel_id=1, source_target_pairs={{0,4},{4,0},{8,12},{12,8},{16,20},{20,16},{24,28},{28,24},{1,5},{5... | collective-permute-start | bytes 5308424 | tf_op jit(solution)/shard_map/ppermute | solution.py:646
  303.6 17.2 %collective-permute-start.40 = (bf16[96,1792]{1,0:T(8,128)(2,1)}, bf16[96,1792]{1,0:T(8,128)(2,1)S(1)}, u32[]{:S(2)}, u32[]{:S(2)}) collective-permute-start(bf16[96,1792]{1,0:T(8,128)(2,1)} %get-tuple-element.108), channel_id=1, source_target_pairs={{0,1},{1,0},{2,3},{3,2},{4,5},{5,4},{6,7},{7,6},{8,9},{9,8},{10,11... | collective-permute-start | bytes 1032200 | tf_op jit(solution)/shard_map/ppermute | solution.py:649
  307.4 26.9 %collective-permute-start.41 = (bf16[96,1792]{1,0:T(8,128)(2,1)}, bf16[96,1792]{1,0:T(8,128)(2,1)S(1)}, u32[]{:S(2)}, u32[]{:S(2)}) collective-permute-start(bf16[96,1792]{1,0:T(8,128)(2,1)} %get-tuple-element.109), channel_id=1, source_target_pairs={{0,2},{1,3},{2,0},{3,1},{4,6},{5,7},{6,4},{7,5},{8,10},{9,11},{10,... | collective-permute-start | bytes 1032200 | tf_op jit(solution)/shard_map/ppermute | solution.py:649
  308.4 25.8 %collective-permute-start.42 = (bf16[96,1792]{1,0:T(8,128)(2,1)}, bf16[96,1792]{1,0:T(8,128)(2,1)S(1)}, u32[]{:S(2)}, u32[]{:S(2)}) collective-permute-start(bf16[96,1792]{1,0:T(8,128)(2,1)} %get-tuple-element.110), channel_id=1, source_target_pairs={{0,3},{1,2},{2,1},{3,0},{4,7},{5,6},{6,5},{7,4},{8,11},{9,10},{10,... | collective-permute-start | bytes 1032200 | tf_op jit(solution)/shard_map/ppermute | solution.py:649
  347.3 13.8 %collective-permute-start.48 = (bf16[96,2304]{1,0:T(8,128)(2,1)S(1)}, bf16[96,2304]{1,0:T(8,128)(2,1)S(1)}, u32[]{:S(2)}, u32[]{:S(2)}) collective-permute-start(bf16[96,2304]{1,0:T(8,128)(2,1)S(1)} %concatenate.41), channel_id=1, source_target_pairs={{0,24},{4,28},{8,16},{12,20},{16,8},{20,12},{24,0},{28,4},{1,25},{... | collective-permute-start | bytes 1327112 | tf_op jit(solution)/shard_map/ppermute | solution.py:646
  348.8 17.0 %collective-permute-start.47 = (bf16[96,2304]{1,0:T(8,128)(2,1)S(1)}, bf16[96,2304]{1,0:T(8,128)(2,1)S(1)}, u32[]{:S(2)}, u32[]{:S(2)}) collective-permute-start(bf16[96,2304]{1,0:T(8,128)(2,1)S(1)} %concatenate.41), channel_id=1, source_target_pairs={{0,16},{4,20},{8,24},{12,28},{16,0},{20,4},{24,8},{28,12},{1,17},{... | collective-permute-start | bytes 1327112 | tf_op jit(solution)/shard_map/ppermute | solution.py:646
  350.2 16.3 %collective-permute-start.46 = (bf16[96,2304]{1,0:T(8,128)(2,1)S(1)}, bf16[96,2304]{1,0:T(8,128)(2,1)S(1)}, u32[]{:S(2)}, u32[]{:S(2)}) collective-permute-start(bf16[96,2304]{1,0:T(8,128)(2,1)S(1)} %concatenate.41), channel_id=1, source_target_pairs={{0,8},{4,12},{8,0},{12,4},{16,24},{20,28},{24,16},{28,20},{1,9},{5... | collective-permute-start | bytes 1327112 | tf_op jit(solution)/shard_map/ppermute | solution.py:646
  366.7 85.4 %collective-permute-start.49 = (bf16[4,96,2304]{2,1,0:T(8,128)(2,1)S(1)}, bf16[4,96,2304]{2,1,0:T(8,128)(2,1)}, u32[]{:S(2)}, u32[]{:S(2)}) collective-permute-start(bf16[4,96,2304]{2,1,0:T(8,128)(2,1)S(1)} %pad_maximum_fusion.2.near), channel_id=1, source_target_pairs={{0,4},{4,0},{8,12},{12,8},{16,20},{20,16},{24,28},{28,24},{1,5},{5... | collective-permute-start | bytes 5308424 | tf_op jit(solution)/shard_map/ppermute | solution.py:646
  371.5 34.9 %collective-permute-start.20 = (bf16[4,96,576]{2,1,0:T(8,128)(2,1)}, bf16[4,96,576]{2,1,0:T(8,128)(2,1)S(1)}, u32[]{:S(2)}, u32[]{:S(2)}) collective-permute-start(bf16[4,96,576]{2,1,0:T(8,128)(2,1)} %get-tuple-element.87), channel_id=1, source_target_pairs={{0,8},{4,12},{8,0},{12,4},{16,24},{20,28},{24,16},{28,20},{1,9},{5... | collective-permute-start | bytes 1327112 | tf_op jit(solution)/shard_map/ppermute | solution.py:646
  373.2 35.1 %collective-permute-start.21 = (bf16[4,96,576]{2,1,0:T(8,128)(2,1)}, bf16[4,96,576]{2,1,0:T(8,128)(2,1)S(1)}, u32[]{:S(2)}, u32[]{:S(2)}) collective-permute-start(bf16[4,96,576]{2,1,0:T(8,128)(2,1)} %get-tuple-element.88), channel_id=1, source_target_pairs={{0,16},{4,20},{8,24},{12,28},{16,0},{20,4},{24,8},{28,12},{1,17},{... | collective-permute-start | bytes 1327112 | tf_op jit(solution)/shard_map/ppermute | solution.py:646
  373.9 34.4 %collective-permute-start.22 = (bf16[4,96,576]{2,1,0:T(8,128)(2,1)}, bf16[4,96,576]{2,1,0:T(8,128)(2,1)S(1)}, u32[]{:S(2)}, u32[]{:S(2)}) collective-permute-start(bf16[4,96,576]{2,1,0:T(8,128)(2,1)} %get-tuple-element.89), channel_id=1, source_target_pairs={{0,24},{4,28},{8,16},{12,20},{16,8},{20,12},{24,0},{28,4},{1,25},{... | collective-permute-start | bytes 1327112 | tf_op jit(solution)/shard_map/ppermute | solution.py:646
  376.9 19.7 %collective-permute-start.31 = (f32[12,768]{1,0:T(8,128)S(1)}, f32[12,768]{1,0:T(8,128)S(1)}, u32[]{:S(2)}, u32[]{:S(2)}) collective-permute-start(f32[12,768]{1,0:T(8,128)S(1)} %add.73), channel_id=1, source_target_pairs={{0,8},{4,12},{8,0},{12,4},{16,24},{20,28},{24,16},{28,20},{1,9},{5... | collective-permute-start | bytes 110600 | tf_op jit(solution)/shard_map/ppermute | solution.py:646
  405.2 36.7 %collective-permute-start.18 = (bf16[512,768]{1,0:T(8,128)(2,1)}, bf16[512,768]{1,0:T(8,128)(2,1)}, u32[]{:S(2)}, u32[]{:S(2)}) collective-permute-start(bf16[512,768]{1,0:T(8,128)(2,1)} %get-tuple-element.83), channel_id=1, source_target_pairs={{0,1},{1,0},{2,3},{3,2},{4,5},{5,4},{6,7},{7,6},{8,9},{9,8},{10,11... | collective-permute-start | bytes 2359304 | tf_op jit(solution)/shard_map/ppermute | solution.py:649
  406.4 19.0 %collective-permute-start.34 = (f32[12,768]{1,0:T(8,128)S(1)}, f32[12,768]{1,0:T(8,128)S(1)}, u32[]{:S(2)}, u32[]{:S(2)}) collective-permute-start(f32[12,768]{1,0:T(8,128)S(1)} %add.76), channel_id=1, source_target_pairs={{0,2},{1,3},{2,0},{3,1},{4,6},{5,7},{6,4},{7,5},{8,10},{9,11},{10,... | collective-permute-start | bytes 110600 | tf_op jit(solution)/shard_map/ppermute | solution.py:649
  411.7 17.6 %collective-permute-start.23 = (bf16[96,576]{1,0:T(8,128)(2,1)}, bf16[96,576]{1,0:T(8,128)(2,1)S(1)}, u32[]{:S(2)}, u32[]{:S(2)}) collective-permute-start(bf16[96,576]{1,0:T(8,128)(2,1)} %get-tuple-element.91), channel_id=1, source_target_pairs={{0,1},{1,0},{2,3},{3,2},{4,5},{5,4},{6,7},{7,6},{8,9},{9,8},{10,11... | collective-permute-start | bytes 331784 | tf_op jit(solution)/shard_map/ppermute | solution.py:649
  412.5 16.8 %collective-permute-start.24 = (bf16[96,576]{1,0:T(8,128)(2,1)}, bf16[96,576]{1,0:T(8,128)(2,1)S(1)}, u32[]{:S(2)}, u32[]{:S(2)}) collective-permute-start(bf16[96,576]{1,0:T(8,128)(2,1)} %get-tuple-element.92), channel_id=1, source_target_pairs={{0,2},{1,3},{2,0},{3,1},{4,6},{5,7},{6,4},{7,5},{8,10},{9,11},{10,... | collective-permute-start | bytes 331784 | tf_op jit(solution)/shard_map/ppermute | solution.py:649
  (44 other events, 275.9 us)

commit v3 on v2

--- a/solution.py
+++ b/solution.py
@@ -154,39 +154,59 @@
         normed_out[...] = (unit * vectors[1:2] + vectors[2:3]).astype(BF16)
 
 
-def forward_kernel(last, normed, weight, bias, *refs):
-    step, steps = pl.program_id(0), pl.num_programs(0)
-    if last:
-        (info, branch_in, rows_in, cotangent, vectors) = refs[:5]
-        (hidden_out, slope_out, mixed_out, second_out, grad_out, sums_out, total) = refs[5:]
-    else:
-        (hidden_out, slope_out, total) = refs
-    dim = normed.shape[1]
-    block = weight[0].reshape(-1, 2 * dim)
-    pre = dot(normed[...], block[:, :dim], 1, 1) + bias[0]
-    hidden, slope = gelu_parts(pre)
-    hidden = hidden.astype(BF16)
-    hidden_out[...] = hidden
-    slope_out[...] = slope
-    partial = dot(hidden, block[:, dim:])
-
-    @pl.when(step == 0)
+def tile_of(near, far):
+    step, half = pl.program_id(0), pl.num_programs(0) // 2
+    return jnp.where(step < half, near[0], far[0]).reshape(-1, near.shape[3])
+
+
+def add_up(total, partial):
+    @pl.when(pl.program_id(0) == 0)
     def first():
         total[...] = partial
 
-    @pl.when(step > 0)
+    @pl.when(pl.program_id(0) > 0)
     def later():
         total[...] += partial
 
-    if not last:
-        return
-
-    @pl.when(step == steps - 1)
+
+def at_end(run):
+    pl.when(pl.program_id(0) == pl.num_programs(0) - 1)(run)
+
+
+def eight_rows(*rows):
+    width = rows[0].shape[1]
+    return jnp.concatenate([*rows, jnp.zeros((8 - len(rows), width), F32)], axis=0)
+
+
+def feed_up_kernel(normed, near, far, bias, hidden_out, slope_out):
+    pre = dot(normed[...], tile_of(near, far), 1, 1) + bias[0]
+    hidden, slope = gelu_parts(pre)
+    hidden_out[...] = hidden.astype(BF16)
+    slope_out[...] = slope
+
+
+def feed_down_kernel(
+    info,
+    hidden,
+    near,
+    far,
+    rows_in,
+    cotangent,
+    vectors,
+    mixed_out,
+    second_out,
+    grad_out,
+    sums_out,
+    total,
+):
+    add_up(total, dot(hidden[...], tile_of(near, far)))
+
+    @at_end
     def finish():
         unit_one, _ = unit_parts(rows_in[...])
         first_norm = unit_one * vectors[0:1] + vectors[1:2]
-        unit, inverse = unit_parts(first_norm + (branch_in[...] + total[...] + vectors[2:3]))
-        present = lax.broadcasted_iota(jnp.int32, (normed.shape[0], 1), 0) < info[0]
+        unit, inverse = unit_parts(first_norm + (total[...] + vectors[2:3]))
+        present = lax.broadcasted_iota(jnp.int32, (hidden.shape[0], 1), 0) < info[0]
         mask = jnp.where(present, 1.0, 0.0).astype(F32)
         mixed_out[...] = ((unit * vectors[3:4] + vectors[4:5]) * mask).astype(BF16)
         incoming = cotangent[...].astype(F32) * mask
@@ -194,50 +214,37 @@
         second_out[...] = grad
         low = grad.astype(BF16)
         grad_out[...] = low
-        sums_out[...] = jnp.concatenate(
-            [
-                column_sum(low.astype(F32)),
-                column_sum(incoming * unit),
-                column_sum(incoming),
-                jnp.zeros((5, dim), F32),
-            ],
-            axis=0,
+        sums_out[...] = eight_rows(
+            column_sum(low.astype(F32)), column_sum(incoming * unit), column_sum(incoming)
         )
 
 
-def backward_kernel(last, normed, grad_branch, weight, hidden, slope, *refs):
-    step, steps = pl.program_id(0), pl.num_programs(0)
+def down_back_kernel(grad_branch, weight, hidden, slope, pre_out, grads_out, bias_out):
+    shards, piece, dim = grads_out.shape[1:]
+    grad_rows = grad_branch[...]
+    grad_pre = dot(grad_rows, weight[0].reshape(-1, dim), 1, 1) * slope[...]
+    grad_pre = grad_pre.astype(BF16)
+    pre_out[...] = grad_pre
+    bias_out[0] = jnp.broadcast_to(column_sum(grad_pre.astype(F32)), bias_out.shape[1:])
+    down = dot(hidden[...], grad_rows, 0, 0)
+    grads_out[0] = down.astype(BF16).reshape(shards, piece, dim)
+
+
+def up_back_kernel(last, normed, grad_pre, weight, *refs):
     if last:
         (info, normed_in, rows_in, second_in, context, vectors) = refs[:6]
-        (grads_out, bias_out, first_out, proj_out, sums_out, near_out, far_out) = refs[6:13]
-        (total, chunks) = refs[13:]
+        (grads_out, first_out, proj_out, sums_out, near_out, far_out, total, chunks) = refs[6:]
     else:
-        (grads_out, bias_out, total) = refs
-    dim = normed.shape[1]
-    shards, piece = weight.shape[1], weight.shape[2]
-    block = weight[0].reshape(-1, 2 * dim)
-    grad_rows = grad_branch[...]
-    grad_pre = dot(grad_rows, block[:, dim:], 1, 1) * slope[...]
-    grad_pre = grad_pre.astype(BF16)
-    bias_out[0] = jnp.broadcast_to(column_sum(grad_pre.astype(F32)), bias_out.shape[1:])
-    up = dot(grad_pre, normed[...], 0, 0)
-    grads_out[0, :, :, :dim] = up.astype(BF16).reshape(shards, piece, dim)
-    down = dot(hidden[...], grad_rows, 0, 0)
-    grads_out[0, :, :, dim:] = down.astype(BF16).reshape(shards, piece, dim)
-    partial = dot(grad_pre, block[:, :dim])
-
-    @pl.when(step == 0)
-    def first():
-        total[...] = partial
-
-    @pl.when(step > 0)
-    def later():
-        total[...] += partial
+        (grads_out, total) = refs
+    shards, piece, dim = grads_out.shape[1:]
+    up = dot(grad_pre[...], normed[...], 0, 0)
+    grads_out[0] = up.astype(BF16).reshape(shards, piece, dim)
+    add_up(total, dot(grad_pre[...], weight[0].reshape(-1, dim)))
 
     if not last:
         return
 
-    @pl.when(step == steps - 1)
+    @at_end
     def finish():
         unit, inverse = unit_parts(rows_in[...])
         grad_normed = second_in[...] + (normed_in[...] + total[...])
@@ -245,14 +252,8 @@
         first_out[...] = grad
         low = grad.astype(BF16)
         proj_out[...] = low
-        sums_out[...] = jnp.concatenate(
-            [
-                column_sum(low.astype(F32)),
-                column_sum(grad_normed * unit),
-                column_sum(grad_normed),
-                jnp.zeros((5, dim), F32),
-            ],
-            axis=0,
+        sums_out[...] = eight_rows(
+            column_sum(low.astype(F32)), column_sum(grad_normed * unit), column_sum(grad_normed)
         )
         low_t = low.T
         part = info[1]
@@ -267,6 +268,7 @@
 def attend_back_kernel(
     heads,
     depth,
+    first_shard,
     info_ref,
     tokens,
     partner,
@@ -276,6 +278,8 @@
     out_weight,
     qkv_in,
     stats_in,
+    own_in,
+    partner_in,
     own_out,
     partner_out,
     near_out,
@@ -284,16 +288,16 @@
     weight_scratch,
     tokens_t,
     partner_t,
-    total,
     chunks,
 ):
-    shard, shards = pl.program_id(0), pl.num_programs(0)
-    info = Info(info_ref, heads, shards)
+    step = pl.program_id(0)
+    shard = step + first_shard
+    info = Info(info_ref, heads, out_weight.shape[0])
     swaps = info.swaps(shard)
     rows, dim = tokens.shape
     width = heads * depth
 
-    @pl.when(shard == 0)
+    @pl.when(step == 0)
     def turn():
         tokens_t[...] = tokens[...].T
         partner_t[...] = partner[...].T
@@ -326,19 +330,15 @@
     own = dot(grad_own, weight, 1, 1)
     other = dot(grad_far, weight[:, : 2 * width], 1, 1)
 
-    @pl.when(shard == 0)
+    @pl.when(step == 0)
     def first():
-        own_out[...] = own
-        total[...] = other
-
-    @pl.when(shard > 0)
+        own_out[...] = own if own_in is None else own_in[...] + own
+        partner_out[...] = other if partner_in is None else partner_in[...] + other
+
+    @pl.when(step > 0)
     def later():
         own_out[...] += own
-        total[...] += other
-
-    @pl.when(shard == shards - 1)
-    def finish():
-        partner_out[...] = total[...].astype(BF16)
+        partner_out[...] += other
 
     grads = dot(tokens_t[...], grad_own)
     grads_kv = grads[:, : 2 * width] + dot(partner_t[...], grad_far)
@@ -373,15 +373,20 @@
         out[...] = value.astype(out.dtype)
 
 
-def settle_feed_kernel(info, near, far, up_out, down_out, out_out, up_scratch, out_scratch):
-    dim = down_out.shape[2]
+def settle_down_kernel(info, near, far, out):
+    for core, source in enumerate((near, far)):
+        for spot in range(PARTS // 2):
+            out[info[1] ^ (2 * spot + core)] = source[spot].astype(F32)
+
+
+def settle_up_kernel(info, near, far, up_out, out_out, up_scratch, out_scratch):
+    dim = up_out.shape[0]
     for core, source in enumerate((near, far)):
         for spot in range(PARTS // 2):
             place = info[1] ^ (2 * spot + core)
             value = source[spot].astype(F32)
             up_scratch[place] = value[:, :dim]
-            down_out[place] = value[:, dim : 2 * dim]
-            out_scratch[place] = value[:, 2 * dim :]
+            out_scratch[place] = value[:, dim:]
     up_out[...] = up_scratch[...].reshape(-1, dim).T
     shards = out_out.shape[0]
     turned = out_scratch[...].reshape(-1, dim).T.reshape(shards, -1, dim)
@@ -453,62 +458,104 @@
     )(info, tokens, partner, near, far, bias, out_weight, vectors)
 
 
-def feed_forward(last, normed, weight, bias, *extra):
+def cost(flops, moved, slow=0):
+    return pl.CostEstimate(flops=flops, bytes_accessed=moved, transcendentals=slow)
+
+
+def halves(weight):
+    spots, shards, piece, dim = weight.shape
+    return [
+        pl.BlockSpec((1, shards, piece, dim), lambda s: (jnp.minimum(s, spots - 1), 0, 0, 0)),
+        pl.BlockSpec((1, shards, piece, dim), lambda s: (jnp.maximum(s - spots, 0), 0, 0, 0)),
+    ]
+
+
+def feed_up(normed, near, far, bias):
     rows, dim = normed.shape
-    spots, shards, piece, lanes = weight.shape
+    spots, shards, piece, _ = near.shape
     tile = shards * piece
-    in_specs = [
-        whole(rows, dim),
-        pl.BlockSpec((1, shards, piece, lanes), lambda s: (s, 0, 0, 0)),
-        pl.BlockSpec((1, 1, tile), lambda s: (s, 0, 0)),
-    ]
-    out_specs = [pl.BlockSpec((rows, tile), lambda s: (0, s))] * 2
-    out_shape = [shape((rows, spots * tile), BF16), shape((rows, spots * tile), F32)]
-    scratch = []
-    if last:
-        in_specs += [SMEM] + [whole(rows, dim)] * 3 + [whole(8, dim)]
-        out_specs += [whole(rows, dim)] * 3 + [whole(8, dim)]
-        out_shape += [
+    steps = 2 * spots
+    columns = pl.BlockSpec((rows, tile), lambda s: (0, s))
+    return pl.pallas_call(
+        feed_up_kernel,
+        grid=(steps,),
+        in_specs=[
+            whole(rows, dim),
+            *halves(near),
+            pl.BlockSpec((1, 1, tile), lambda s: (s, 0, 0)),
+        ],
+        out_specs=[columns, columns],
+        out_shape=[shape((rows, steps * tile), BF16), shape((rows, steps * tile), F32)],
+        compiler_params=PARAMS,
+        cost_estimate=cost(4 * rows * dim * tile * steps, 30 * rows * dim, rows * tile * steps),
+        name="feed_up",
+    )(normed, near, far, bias)
+
+
+def feed_down(info, hidden, near, far, rows_one, cotangent, vectors):
+    rows, dim = rows_one.shape
+    spots, shards, piece, _ = near.shape
+    tile = shards * piece
+    steps = 2 * spots
+    return pl.pallas_call(
+        feed_down_kernel,
+        grid=(steps,),
+        in_specs=[
+            SMEM,
+            pl.BlockSpec((rows, tile), lambda s: (0, s)),
+            *halves(near),
+            whole(rows, dim),
+            whole(rows, dim),
+            whole(8, dim),
+        ],
+        out_specs=[whole(rows, dim)] * 3 + [whole(8, dim)],
+        out_shape=[
             shape((rows, dim), BF16),
             shape((rows, dim), F32),
             shape((rows, dim), BF16),
             shape((8, dim), F32),
-        ]
-        scratch = [pltpu.VMEM((rows, dim), F32)]
-    else:
-        out_specs.append(whole(rows, dim))
-        out_shape.append(shape((rows, dim), F32))
+        ],
+        scratch_shapes=[pltpu.VMEM((rows, dim), F32)],
+        compiler_params=PARAMS,
+        cost_estimate=cost(4 * rows * dim * tile * steps, 30 * rows * dim),
+        name="feed_down",
+    )(info, hidden, near, far, rows_one, cotangent, vectors)
+
+
+def down_back(half, grad_branch, weight, hidden, slope):
+    rows, dim = grad_branch.shape
+    spots, shards, piece, _ = weight.shape
+    tile = shards * piece
+    weight_spec = pl.BlockSpec((1, shards, piece, dim), lambda s: (s, 0, 0, 0))
+    columns = pl.BlockSpec((rows, tile), lambda s: (0, s + half * spots))
     return pl.pallas_call(
-        functools.partial(forward_kernel, last),
+        down_back_kernel,
         grid=(spots,),
-        in_specs=in_specs,
-        out_specs=out_specs,
-        out_shape=out_shape,
-        scratch_shapes=scratch,
+        in_specs=[whole(rows, dim), weight_spec, columns, columns],
+        out_specs=[
+            pl.BlockSpec((rows, tile), lambda s: (0, s)),
+            weight_spec,
+            pl.BlockSpec((1, 8, tile), lambda s: (s, 0, 0)),
+        ],
+        out_shape=[
+            shape((rows, spots * tile), BF16),
+            shape(weight.shape, BF16),
+            shape((spots, 8, tile), F32),
+        ],
         compiler_params=PARAMS,
-        cost_estimate=pl.CostEstimate(
-            flops=4 * rows * dim * tile * spots,
-            bytes_accessed=24 * rows * dim,
-            transcendentals=2 * rows * tile * spots,
-        ),
-        name="feed_last" if last else "feed_first",
-    )(normed, weight, bias, *extra)
-
-
-def feed_back(last, normed, grad_branch, weight, hidden, slope, *extra):
+        cost_estimate=cost(4 * rows * dim * tile * spots, 30 * rows * dim),
+        name="down_back",
+    )(grad_branch, weight, hidden, slope)
+
+
+def up_back(last, normed, grad_pre, weight, *extra):
     rows, dim = normed.shape
-    spots, shards, piece, lanes = weight.shape
+    spots, shards, piece, _ = weight.shape
     tile = shards * piece
-    weight_spec = pl.BlockSpec((1, shards, piece, lanes), lambda s: (s, 0, 0, 0))
-    in_specs = [
-        whole(rows, dim),
-        whole(rows, dim),
-        weight_spec,
-        pl.BlockSpec((rows, tile), lambda s: (0, s)),
-        pl.BlockSpec((rows, tile), lambda s: (0, s)),
-    ]
-    out_specs = [weight_spec, pl.BlockSpec((1, 8, tile), lambda s: (s, 0, 0))]
-    out_shape = [shape(weight.shape, BF16), shape((spots, 8, tile), F32)]
+    weight_spec = pl.BlockSpec((1, shards, piece, dim), lambda s: (s, 0, 0, 0))
+    in_specs = [whole(rows, dim), pl.BlockSpec((rows, tile), lambda s: (0, s)), weight_spec]
+    out_specs = [weight_spec]
+    out_shape = [shape(weight.shape, BF16)]
     scratch = []
     if last:
         width = extra[4].shape[2]
@@ -527,72 +574,89 @@
         out_specs.append(whole(rows, dim))
         out_shape.append(shape((rows, dim), F32))
     return pl.pallas_call(
-        functools.partial(backward_kernel, last),
+        functools.partial(up_back_kernel, last),
         grid=(spots,),
         in_specs=in_specs,
         out_specs=out_specs,
         out_shape=out_shape,
         scratch_shapes=scratch,
         compiler_params=PARAMS,
-        cost_estimate=pl.CostEstimate(
-            flops=8 * rows * dim * tile * spots,
-            bytes_accessed=36 * rows * dim,
-            transcendentals=0,
-        ),
-        name="feed_back_last" if last else "feed_back_first",
-    )(normed, grad_branch, weight, hidden, slope, *extra)
+        cost_estimate=cost(4 * rows * dim * tile * spots, 30 * rows * dim),
+        name="up_back",
+    )(normed, grad_pre, weight, *extra)
 
 
 def attend_back(
-    info, tokens, partner, grad_proj, near, far, out_weight, qkv, stats, heads, depth
+    info,
+    tokens,
+    partner,
+    grad_proj,
+    near,
+    far,
+    out_weight,
+    qkv,
+    stats,
+    heads,
+    depth,
+    first_shard,
+    count,
+    carried,
 ):
     rows, dim = tokens.shape
     spots, shards, piece, lanes = near.shape
     width = heads * depth
-    weight_spec = pl.BlockSpec((spots, 1, piece, lanes), lambda s: (0, s, 0, 0))
+    weight_in = pl.BlockSpec((spots, 1, piece, lanes), lambda s: (0, s + first_shard, 0, 0))
+    weight_out = pl.BlockSpec((spots, 1, piece, lanes), lambda s: (0, s, 0, 0))
+    kernel = functools.partial(attend_back_kernel, heads, depth, first_shard)
+    if not carried:
+        bare = kernel
+
+        def kernel(*refs):
+            bare(*refs[:9], None, None, *refs[9:])
+
     return pl.pallas_call(
-        functools.partial(attend_back_kernel, heads, depth),
-        grid=(shards,),
+        kernel,
+        grid=(count,),
         in_specs=[
             SMEM,
             whole(rows, dim),
             whole(rows, dim),
             whole(rows, dim),
-            weight_spec,
-            weight_spec,
+            weight_in,
+            weight_in,
             whole(shards, width, dim),
-            pl.BlockSpec((1, rows, lanes), lambda s: (s, 0, 0)),
-            pl.BlockSpec((1, 8, rows), lambda s: (s, 0, 0)),
-        ],
+            pl.BlockSpec((1, rows, lanes), lambda s: (s + first_shard, 0, 0)),
+            pl.BlockSpec((1, 8, rows), lambda s: (s + first_shard, 0, 0)),
+        ]
+        + [whole(rows, dim)] * len(carried),
         out_specs=[
             whole(rows, dim),
             whole(rows, dim),
-            weight_spec,
-            weight_spec,
+            weight_out,
+            weight_out,
             pl.BlockSpec((1, 8, lanes), lambda s: (s, 0, 0)),
         ],
         out_shape=[
             shape((rows, dim), F32),
-            shape((rows, dim), BF16),
-            shape(near.shape, BF16),
-            shape(far.shape, BF16),
-            shape((shards, 8, lanes), F32),
+            shape((rows, dim), F32),
+            shape((spots, count, piece, lanes), BF16),
+            shape((spots, count, piece, lanes), BF16),
+            shape((count, 8, lanes), F32),
         ],
         scratch_shapes=[
             pltpu.VMEM((PARTS, piece, lanes), BF16),
             pltpu.VMEM((dim, rows), BF16),
             pltpu.VMEM((dim, rows), BF16),
-            pltpu.VMEM((rows, dim), F32),
             pltpu.VMEM((PARTS, piece, lanes), BF16),
         ],
         compiler_params=PARAMS,
-        cost_estimate=pl.CostEstimate(
-            flops=24 * rows * dim * dim + 40 * rows * rows * dim,
-            bytes_accessed=32 * rows * dim,
-            transcendentals=shards * heads * rows * rows,
+        cost_estimate=cost(
+            count * (6 * rows * dim * dim + 10 * rows * rows * dim),
+            count * 8 * rows * dim,
+            count * heads * rows * rows,
         ),
         name="attend_back",
-    )(info, tokens, partner, grad_proj, near, far, out_weight, qkv, stats)
+    )(info, tokens, partner, grad_proj, near, far, out_weight, qkv, stats, *carried)
 
 
 def fold_core(mine, received, lanes):
@@ -618,22 +682,19 @@
     )(*mine, *received)
 
 
-def fold_chips(own, received):
+def fold_chips(own, received, first_stays=True):
     shards, piece, lanes = own.shape
     cut = 256 if lanes % 256 == 0 else lanes
     spec = pl.BlockSpec((shards, piece, cut), lambda s: (0, 0, s))
+    stays = F32 if first_stays else BF16
     return pl.pallas_call(
         fold_chips_kernel,
         grid=(lanes // cut,),
         in_specs=[spec] * 4,
         out_specs=[pl.BlockSpec((piece, cut), lambda s: (0, s))] * shards,
-        out_shape=[shape((piece, lanes), F32)] + [shape((piece, lanes), BF16)] * (shards - 1),
+        out_shape=[shape((piece, lanes), stays)] + [shape((piece, lanes), BF16)] * (shards - 1),
         compiler_params=PARAMS,
-        cost_estimate=pl.CostEstimate(
-            flops=4 * shards * piece * lanes,
-            bytes_accessed=12 * shards * piece * lanes,
-            transcendentals=0,
-        ),
+        cost_estimate=cost(4 * shards * piece * lanes, 12 * shards * piece * lanes),
         name="fold_chips",
     )(own, *received)
 
@@ -648,34 +709,29 @@
     def head(self, value, mask):
         return lax.ppermute(value, "head", [(i, i ^ mask) for i in range(self.shards)])
 
+    def chips(self, values):
+        masks = (NEAR_X, NEAR_Y, NEAR_X | NEAR_Y)
+        return [self.batch(value, mask) for value, mask in zip(values, masks)]
+
     def around(self, value):
-        return [self.batch(value, mask) for mask in (NEAR_X, NEAR_Y, NEAR_X | NEAR_Y)]
+        return self.chips([value] * 3)
 
     def along(self, values):
         return [self.head(value, q) for q, value in enumerate(values, 1)]
 
-    def gather(self, piece):
-        column = jnp.stack([piece] + self.along([piece] * (self.shards - 1)))
-        near = jnp.stack([column] + self.around(column))
-        return near, self.batch(near, CORE)
-
-    def reduce(self, own, send):
-        masks = (NEAR_X, NEAR_Y, NEAR_X | NEAR_Y)
-        received = [self.batch(value, mask) for value, mask in zip(send, masks)]
-        sums = fold_chips(own, received)
-        total = sums[0]
-        for value in self.along(sums[1:]):
-            total = total + value.astype(F32)
+    def column(self, piece):
+        return [piece] + self.along([piece] * (self.shards - 1))
+
+    def plane(self, column):
+        return [column] + self.around(column)
+
+    def settle(self, total):
         total = total.astype(BF16)
         mask = PARTS
         while mask < self.batch_size:
             total = (total.astype(F32) + self.batch(total, mask).astype(F32)).astype(BF16)
             mask *= 2
         return total
-
-    def spread(self, piece):
-        near = jnp.stack([piece] + self.around(piece))
-        return near, self.batch(near, CORE)
 
     def total(self, value):
         mask = 1
@@ -687,6 +743,14 @@
             value = value + self.head(value, mask)
             mask *= 2
         return value
+
+
+def after(value, *events):
+    return lax.optimization_barrier((value, *events))[0]
+
+
+def all_after(values, *events):
+    return lax.optimization_barrier((*values, *events))[: len(values)]
 
 
 def exchange_bits(value, axes):
@@ -740,14 +804,17 @@
     input_piece = lax.dynamic_slice_in_dim(input_weight, part * piece, piece, 1)
     input_piece = jnp.concatenate([input_piece[1], input_piece[2], input_piece[0]], axis=1)
     small = jnp.concatenate([input_bias.reshape(-1), block_swap.astype(F32)])
-    small = jnp.stack([small] + move.along([small] * (shards - 1)))
-    input_near, input_far = move.gather(input_piece)
-    partner = move.head(tokens, 1)
+    small = jnp.stack(move.column(small))
+    input_column = move.column(input_piece)
+    input_plane = move.plane(jnp.stack(input_column))
     up_piece = lax.dynamic_slice_in_dim(up_weight, part * piece, piece, 1).T
     down_piece = lax.dynamic_slice_in_dim(down_weight, part * piece, piece, 0)
-    feed_piece = jnp.concatenate([up_piece, down_piece], axis=1)
-    feed_piece, partner = lax.optimization_barrier((feed_piece, partner))
-    feed_near, feed_far = move.gather(feed_piece)
+    up_column = move.column(after(up_piece, *input_column))
+    partner = move.head(after(tokens, *up_column), 1)
+    input_near = jnp.stack(all_after(input_plane, *up_column))
+    input_far = move.batch(input_near, CORE)
+    up_plane = move.plane(after(jnp.stack(up_column), input_near))
+    down_column = move.column(after(down_piece, partner))
 
     info = jnp.concatenate(
         [
@@ -763,116 +830,160 @@
     bits = [(0, head_bits[1]), (1, head_bits[0])]
     bits += [(2, part_bits[2]), (3, part_bits[1]), (4, part_bits[0])]
     up_bias_rel = exchange_bits(up_bias.reshape(2, 2, 2, 2, 2, piece), bits)
-    up_bias_rel = up_bias_rel.transpose(4, 2, 3, 0, 1, 5).reshape(2, 4, 1, shards * piece)
+    up_bias_rel = up_bias_rel.transpose(4, 2, 3, 0, 1, 5).reshape(PARTS, 1, shards * piece)
     out_parts = out_weight.reshape(shards, width, dim)
 
+    vectors_one = stack8(out_bias, gain_one, shift_one)
+    vectors_two = stack8(gain_one, shift_one, down_bias, gain_two, shift_two)
+    vectors_back = stack8(gain_one)
     qkv, context, stats, rows_one, normed = attend(
         info,
-        tokens,
+        after(tokens, up_bias_rel, vectors_two, vectors_back),
         partner,
         input_near,
         input_far,
         bias,
         out_parts,
-        stack8(out_bias, gain_one, shift_one),
+        vectors_one,
         heads,
         depth,
     )
-    hidden_near, slope_near, branch = feed_forward(False, normed, feed_near, up_bias_rel[0])
-    hidden_far, slope_far, mixed_out, grad_second, grad_branch, sums_two = feed_forward(
+    down_plane = move.plane(jnp.stack(all_after(down_column, normed)))
+    up_near = jnp.stack(all_after(up_plane, normed))
+    up_far = move.batch(up_near, CORE)
+    hidden, slope = feed_up(normed, up_near, up_far, up_bias_rel)
+    down_near = jnp.stack(all_after(down_plane, hidden))
+    down_far = move.batch(down_near, CORE)
+    mixed_out, grad_second, grad_branch, sums_two = feed_down(
+        short_info,
+        hidden,
+        down_near,
+        down_far,
+        rows_one,
+        cotangent,
+        vectors_two,
+    )
+
+    pre_far, down_grads_far, up_bias_far = down_back(1, grad_branch, down_far, hidden, slope)
+    down_received = move.batch(down_grads_far, CORE)
+    pre_near, down_grads_near, up_bias_near = down_back(
+        0, after(grad_branch, pre_far), down_near, hidden, slope
+    )
+    down_own, *down_send = fold_core([down_grads_near], [down_received], dim)
+    down_chips = move.chips(down_send)
+    up_grads_far, grad_normed = up_back(False, after(normed, *down_send), pre_far, up_far)
+    up_received = move.batch(up_grads_far, CORE)
+    up_grads_near, grad_first, grad_proj, sums_one, out_grads_near, out_grads_far = up_back(
         True,
         normed,
-        feed_far,
-        up_bias_rel[1],
-        short_info,
-        branch,
-        rows_one,
-        cotangent,
-        stack8(gain_one, shift_one, down_bias, gain_two, shift_two),
-    )
-
-    feed_grads_far, up_bias_far, grad_normed = feed_back(
-        False, normed, grad_branch, feed_far, hidden_far, slope_far
-    )
-    feed_received = move.batch(feed_grads_far, CORE)
-    (
-        feed_grads_near,
-        up_bias_near,
-        grad_first,
-        grad_proj,
-        sums_one,
-        out_grads_near,
-        out_grads_far,
-    ) = feed_back(
-        True,
-        normed,
-        grad_branch,
-        feed_near,
-        hidden_near,
-        slope_near,
+        pre_near,
+        up_near,
         short_info,
         grad_normed,
         rows_one,
         grad_second,
         context,
-        stack8(gain_one),
+        vectors_back,
     )
     out_received = move.batch(out_grads_far, CORE)
-    lanes = -(-(2 * dim + width) // 256) * 256
-    feed_own, *feed_send = fold_core(
-        [feed_grads_near, out_grads_near], [feed_received, out_received], lanes
-    )
-    own_rows, partner_rows, input_grads_near, input_grads_far, bias_sums = attend_back(
-        info,
-        tokens,
-        partner,
-        grad_proj,
-        input_near,
-        input_far,
-        out_parts,
-        qkv,
-        stats,
-        heads,
-        depth,
-    )
-    feed_total = move.reduce(feed_own, feed_send)
-    out_total = feed_total[:, 2 * dim : 2 * dim + width]
-    out_total = [out_total] + move.along([out_total] * (shards - 1))
-    feed_total = jnp.concatenate([feed_total[:, : 2 * dim]] + out_total, axis=1)
-    feed_done = move.spread(feed_total)
-
-    from_partner = move.head(partner_rows, 1)
-    input_received = move.batch(input_grads_far, CORE)
-    input_own, *input_send = fold_core([input_grads_near], [input_received], 3 * width)
-    input_total = move.reduce(input_own, input_send)
-    input_done = move.spread(input_total)
-    grad_tokens = grad_first + own_rows + from_partner.astype(F32)
+    lanes = -(-(dim + width) // 256) * 256
+    up_own, *up_send = fold_core(
+        [up_grads_near, out_grads_near], [up_received, out_received], lanes
+    )
+    up_chips = move.chips(up_send)
+
+    def back(grad, first_shard, count, carried):
+        return attend_back(
+            info,
+            tokens,
+            partner,
+            grad,
+            input_near,
+            input_far,
+            out_parts,
+            qkv,
+            stats,
+            heads,
+            depth,
+            first_shard,
+            count,
+            carried,
+        )
 
     up_bias_grad = jnp.stack([up_bias_near[:, 0], up_bias_far[:, 0]])
     up_bias_grad = up_bias_grad.reshape(2, 2, 2, 2, 2, piece).transpose(3, 4, 1, 2, 0, 5)
     up_bias_grad = exchange_bits(up_bias_grad, bits).reshape(-1, dim)
+    vectors_now = jnp.concatenate([sums_one[:3], sums_two[:3], up_bias_grad])
+    late_grad, vectors_now = all_after((grad_proj, vectors_now), *up_send)
+    own_rows, partner_rows, late_near, late_far, late_sums = back(
+        late_grad, shards // 2, shards // 2, []
+    )
+    late_received = move.batch(late_far, CORE)
+    down_sums = fold_chips(after(down_own, late_sums), down_chips)
+    down_along = move.along(down_sums[1:])
+    late_own, *late_send = fold_core([late_near], [late_received], 3 * width)
+    late_chips = move.chips(late_send)
+    own_rows, partner_rows, early_near, early_far, early_sums = back(
+        after(grad_proj, *down_sums, *late_send), 0, shards // 2, [own_rows, partner_rows]
+    )
+    early_received = move.batch(early_far, CORE)
+    from_partner = move.head(partner_rows.astype(BF16), 1)
+
+    def sum_of(first, values):
+        for value in values:
+            first = first + value.astype(F32)
+        return move.settle(first)
+
+    up_sums = fold_chips(after(up_own, early_sums), up_chips)
+    up_along = move.along(up_sums[1:])
+    early_own, *early_send = fold_core(
+        [early_near], [after(early_received, *up_sums)], 3 * width
+    )
+    early_chips = move.chips(early_send)
+    down_total = sum_of(after(down_sums[0], early_own), down_along)
+    down_done = move.plane(down_total)
+    late_sums_chips = fold_chips(after(late_own, down_total), late_chips, False)
+    late_along = [move.head(v, q) for q, v in enumerate(late_sums_chips, shards // 2)]
+    up_total = sum_of(after(up_sums[0], *late_sums_chips), up_along)
+    out_total = move.column(up_total[:, dim : dim + width])
+    early_sums_chips = fold_chips(after(early_own, up_total), early_chips)
+    early_along = move.along(early_sums_chips[1:])
+    up_total = jnp.concatenate([up_total[:, :dim], *out_total], axis=1)
+    up_done = move.plane(up_total)
+    input_total = sum_of(early_sums_chips[0], early_along + late_along)
+    input_done = move.plane(input_total)
+    down_done = jnp.stack(down_done)
+    up_done = jnp.stack(up_done)
+    input_done = jnp.stack(input_done)
+    down_done = (down_done, move.batch(down_done, CORE))
+    up_done = (up_done, move.batch(up_done, CORE))
+    input_done = (input_done, move.batch(input_done, CORE))
+    grad_tokens = grad_first + own_rows + from_partner.astype(F32)
+    bias_sums = jnp.concatenate([early_sums, late_sums])
+
     bias_sums = exchange_bits(bias_sums[:, 0].reshape(2, 2, 3, width), bits[:2])
     bias_sums = bias_sums.reshape(shards, 3, width).transpose(1, 0, 2).reshape(3, dim)
-    vectors = move.total(
-        jnp.concatenate([sums_one[:3], sums_two[:3], bias_sums[2:], bias_sums[1:2], up_bias_grad])
-    )
-    grad_input_bias = lax.dynamic_slice_in_dim(vectors[6:8], head_at * width, width, 1)
+    vectors = move.total(jnp.concatenate([vectors_now, bias_sums[2:], bias_sums[1:2]]))
+    grad_input_bias = lax.dynamic_slice_in_dim(vectors[10:12], head_at * width, width, 1)
     grad_up_bias = lax.dynamic_slice_in_dim(
-        vectors[8:].reshape(-1), head_at * hidden_own, hidden_own
-    )
-
-    grad_up, grad_down, grad_out = pl.pallas_call(
-        settle_feed_kernel,
-        in_specs=[SMEM] + [whole(4, piece, 2 * dim + shards * width)] * 2,
-        out_shape=[
-            shape((dim, hidden_own), F32),
-            shape((PARTS, piece, dim), F32),
-            shape((shards, width, dim), F32),
-        ],
+        vectors[6:10].reshape(-1), head_at * hidden_own, hidden_own
+    )
+
+    grad_down = pl.pallas_call(
+        settle_down_kernel,
+        in_specs=[SMEM] + [whole(4, piece, dim)] * 2,
+        out_shape=shape((PARTS, piece, dim), F32),
+        compiler_params=PARAMS,
+        name="settle_down",
+    )(short_info, *down_done)
+    grad_up, grad_out = pl.pallas_call(
+        settle_up_kernel,
+        in_specs=[SMEM] + [whole(4, piece, dim + shards * width)] * 2,
+        out_shape=[shape((dim, hidden_own), F32), shape((shards, width, dim), F32)],
         scratch_shapes=[pltpu.VMEM((PARTS, piece, dim), F32)] * 2,
         compiler_params=PARAMS,
-        name="settle_feed",
-    )(short_info, *feed_done)
+        name="settle_up",
+    )(short_info, *up_done)
     grad_input_weight = pl.pallas_call(
         settle_input_kernel,
         in_specs=[SMEM] + [whole(4, piece, 3 * width)] * 2,

time: 459 us -> 418 us (0.911)
  waiting for transfers between devices: 230 us -> 139 us
  Pallas kernels: 129 us -> 150 us
  starting transfers between devices: 66.1 us -> 78.5 us
  local copies, waits for them, and re-layouts: 19.8 us -> 28.7 us
    ppermute x28 -> x44, waiting for transfers between devices: 138 us -> 76.8 us  [batch(): lax.ppermute(value, 'batch', [(i, i ^ mask) for i in range(self.batch_siz...]
    ppermute x22 -> x28, waiting for transfers between devices: 91.7 us -> 62.1 us  [head(): lax.ppermute(value, 'head', [(i, i ^ mask) for i in range(self.shards)])]
    pallas_call x6 -> x10, Pallas kernels: 86.6 us -> 103 us  [the longest x2 34.4 us: attend_back(): pl.pallas_call(kernel, grid=(count,), in_specs=[SMEM, whole(rows, dim), w...]
    ppermute x28 -> x44, starting transfers between devices: 25.2 us -> 39.1 us  [batch(): lax.ppermute(value, 'batch', [(i, i ^ mask) for i in range(self.batch_siz...]
    unnamed x57 -> x107, local copies, waits for them, and re-layouts: 7.7 us -> 16.7 us
    pallas_call x2 -> x4, Pallas kernels: 8.73 us -> 11.6 us  [fold_chips(): pl.pallas_call(fold_chips_kernel, grid=(lanes // cut,), in_specs=[spec] *...]
    pallas_call x2 -> x4, Pallas kernels: 11.6 us -> 14.3 us  [fold_core(): pl.pallas_call(fold_core_kernel, grid=(shards,), in_specs=specs, out_spec...]
    ppermute x22 -> x28, starting transfers between devices: 40.9 us -> 39.4 us  [head(): lax.ppermute(value, 'head', [(i, i ^ mask) for i in range(self.shards)])]
  transfers between devices with their start and end apart: 50 -> 72, of which waited for: 30 -> 30; matrix products, arithmetic and copies ran while one was open for 5% -> 7% of each run, Pallas kernels for 20% -> 22%
where the time goes in v3:
time: 418 us; the launch traced here: 414 us
  Pallas kernels  150 us (36%)
  waiting for transfers between devices  139 us (33%)
  starting transfers between devices  78.5 us (19%)
  local copies, waits for them, and re-layouts  28.7 us (7%)
  other arithmetic  14 us (3%)
    ppermute x44, waiting for transfers between devices, batch(): lax.ppermute(value, 'batch', [(i, i ^ mask) for i in range(self.batch_siz...  76.8 us
    ppermute x28, waiting for transfers between devices, head(): lax.ppermute(value, 'head', [(i, i ^ mask) for i in range(self.shards)])  62.1 us
    ppermute x28, starting transfers between devices, head(): lax.ppermute(value, 'head', [(i, i ^ mask) for i in range(self.shards)])  39.4 us
    ppermute x44, starting transfers between devices, batch(): lax.ppermute(value, 'batch', [(i, i ^ mask) for i in range(self.batch_siz...  39.1 us
    pallas_call x2, Pallas kernels, attend_back(): pl.pallas_call(kernel, grid=(count,), in_specs=[SMEM, whole(rows, dim), w...  34.4 us
    pallas_call x2, Pallas kernels, up_back(): pl.pallas_call(functools.partial(up_back_kernel, last), grid=(spots,), in...  20 us
    pallas_call x1, Pallas kernels, attend(): pl.pallas_call(functools.partial(attend_kernel, heads, depth), grid=(shar...  19 us
    unnamed x107, local copies, waits for them, and re-layouts  16.7 us
  transfers between devices with their start and end apart: 72, of which 30 were waited for; matrix products, arithmetic and copies ran while one was open for 7% of the time, Pallas kernels for 22%

profile of v3, /device:TPU:0, one launch (start us, length us, event | category | flops | bytes accessed | tf_op | source)
XLA Modules:
  0.0 413.7 jit_solution(7404588030730870722)
XLA Ops:
  2.3 5.1 %collective-permute-start.5 = (bf16[96,576]{1,0:T(8,128)(2,1)S(1)}, bf16[96,576]{1,0:T(8,128)(2,1)S(1)}, u32[]{:S(2)}, u32[]{:S(2)}) collective-permute-start(bf16[96,576]{1,0:T(8,128)(2,1)S(1)} %pad_maximum_fusion.9), channel_id=1, source_target_pairs={{0,3},{1,2},{2,1},{3,0},{4,7},{5,6},{6,5},{7,4},{8,11},{9,10},{10,... | collective-permute-start | bytes 331784 | tf_op jit(solution)/shard_map/ppermute | solution.py:710
  8.4 3.2 collective-permute-done.5
  11.7 6.1 %collective-permute-done.4 = bf16[96,576]{1,0:T(8,128)(2,1)S(1)} collective-permute-done((bf16[96,576]{1,0:T(8,128)(2,1)S(1)}, bf16[96,576]{1,0:T(8,128)(2,1)S(1)}, u32[]{:S(2)}, u32[]{:S(2)}) %collective-permute-start.4) | collective-permute-done | bytes 110624 | tf_op jit(solution)/shard_map/ppermute | solution.py:710
  25.2 4.1 collective-permute-start.6
  36.4 7.4 %collective-permute-done.11 = bf16[4,96,576]{2,1,0:T(8,128)(2,1)} collective-permute-done((bf16[4,96,576]{2,1,0:T(8,128)(2,1)S(1)}, bf16[4,96,576]{2,1,0:T(8,128)(2,1)}, u32[]{:S(2)}, u32[]{:S(2)}) %collective-permute-start.11) | collective-permute-done | bytes 442400 | tf_op jit(solution)/shard_map/ppermute | solution.py:707
  54.9 15.4 %collective-permute-done.9.partner.refs_2_ = bf16[512,768]{1,0:T(8,128)(2,1)} collective-permute-done((bf16[512,768]{1,0:T(8,128)(2,1)}, bf16[512,768]{1,0:T(8,128)(2,1)}, u32[]{:S(2)}, u32[]{:S(2)}) %collective-permute-start.9) | collective-permute-done | bytes 786464 | tf_op jit(solution)/shard_map/ppermute | solution.py:710
  71.0 19.0 %attend.1 = (bf16[4,512,576]{2,1,0:T(8,128)(2,1)}, bf16[4,512,192]{2,1,0:T(8,128)(2,1)}, f32[4,8,512]{2,1,0:T(8,128)}, f32[512,768]{1,0:T(8,128)}, bf16[512,768]{1,0:T(8,128)(2,1)}) custom-call(s32[16]{0:T(128)} %concatenate.36.info_ref.refs_0_, bf16[512,768]{1,0:T(8,128)(2,1)} %tokens.2, bf16[512,768]{1,0:T(8,128)(2,1)} %collective-permute-done.9.partner.refs_2_, ...), custom_call_target="tpu_custom_call" | custom-call | flops 6845104128 | bytes 9437184 | tf_op jit(solution)/shard_map/attend/pallas_call | solution.py:423
  96.0 4.2 %collective-permute-done.20 = bf16[96,768]{1,0:T(8,128)(2,1)S(1)} collective-permute-done((bf16[96,768]{1,0:T(8,128)(2,1)S(1)}, bf16[96,768]{1,0:T(8,128)(2,1)S(1)}, u32[]{:S(2)}, u32[]{:S(2)}) %collective-permute-start.20) | collective-permute-done | bytes 147488 | tf_op jit(solution)/shard_map/ppermute | solution.py:710
  100.2 6.6 %collective-permute-done.19 = bf16[96,768]{1,0:T(8,128)(2,1)S(1)} collective-permute-done((bf16[96,768]{1,0:T(8,128)(2,1)S(1)}, bf16[96,768]{1,0:T(8,128)(2,1)S(1)}, u32[]{:S(2)}, u32[]{:S(2)}) %collective-permute-start.19) | collective-permute-done | bytes 147488 | tf_op jit(solution)/shard_map/ppermute | solution.py:710
  111.9 13.0 %feed_up.1 = (bf16[512,3072]{1,0:T(8,128)(2,1)}, f32[512,3072]{1,0:T(8,128)}) custom-call(bf16[512,768]{1,0:T(8,128)(2,1)} %get-tuple-element.147.normed, bf16[4,4,96,768]{3,2,1,0:T(8,128)(2,1)} %copy-done.2, bf16[4,4,96,768]{3,2,1,0:T(8,128)(2,1)} %copy-done.40, f32[8,1,384]{2,1,0:T(1,128)} %reshape.92.bias), custom_call_target="tpu_custom_call" | custom-call | flops 4831838208 | bytes 11796480 | tf_op jit(solution)/shard_map/feed_up/pallas_call | solution.py:479
  124.9 10.4 %collective-permute-done.22 = bf16[4,96,768]{2,1,0:T(8,128)(2,1)S(1)} collective-permute-done((bf16[4,96,768]{2,1,0:T(8,128)(2,1)S(1)}, bf16[4,96,768]{2,1,0:T(8,128)(2,1)S(1)}, u32[]{:S(2)}, u32[]{:S(2)}) %collective-permute-start.22) | collective-permute-done | bytes 589856 | tf_op jit(solution)/shard_map/ppermute | solution.py:707
  136.5 3.7 collective-permute-done.24.far.weight
  141.6 13.4 %feed_down.1 = (bf16[512,768]{1,0:T(8,128)(2,1)}, f32[512,768]{1,0:T(8,128)}, bf16[512,768]{1,0:T(8,128)(2,1)}, f32[8,768]{1,0:T(8,128)}) custom-call(s32[3]{0:T(128)} %pad_add_fusion.info.refs_0_, bf16[512,3072]{1,0:T(8,128)(2,1)} %get-tuple-element.125.hidden, bf16[4,4,96,768]{3,2,1,0:T(8,128)(2,1)} %copy-done.3, bf16[4,4,96,768]{3,2,1,0:T(8,128)(2,1)} %copy-done.7, ...), custom_call_target="tpu_custom_call" | custom-call | flops 4831838208 | bytes 11796480 | tf_op jit(solution)/shard_map/feed_down/pallas_call | solution.py:500
  155.1 7.2 %down_back.2 = (bf16[512,1536]{1,0:T(8,128)(2,1)}, bf16[4,4,96,768]{3,2,1,0:T(8,128)(2,1)}, f32[4,8,384]{2,1,0:T(8,128)}) custom-call(bf16[512,768]{1,0:T(8,128)(2,1)} %get-tuple-element.140.grad_branch, bf16[4,4,96,768]{3,2,1,0:T(8,128)(2,1)} %copy-done.7, bf16[512,3072]{1,0:T(8,128)(2,1)} %get-tuple-element.125.hidden, f32[512,3072]{1,0:T(8,128)} %get-tuple-element.138.slope), custom_call_target="tpu_custom_call" | custom-call | flops 2415919104 | bytes 11796480 | tf_op jit(solution)/shard_map/down_back/pallas_call | solution.py:531
  162.3 7.1 %down_back.3 = (bf16[512,1536]{1,0:T(8,128)(2,1)}, bf16[4,4,96,768]{3,2,1,0:T(8,128)(2,1)}, f32[4,8,384]{2,1,0:T(8,128)}) custom-call(bf16[512,768]{1,0:T(8,128)(2,1)} %get-tuple-element.140.grad_branch, bf16[4,4,96,768]{3,2,1,0:T(8,128)(2,1)} %copy-done.3, bf16[512,3072]{1,0:T(8,128)(2,1)} %get-tuple-element.125.hidden, f32[512,3072]{1,0:T(8,128)} %get-tuple-element.138.slope), custom_call_target="tpu_custom_call" | custom-call | flops 2415919104 | bytes 11796480 | tf_op jit(solution)/shard_map/down_back/pallas_call | solution.py:531
  170.9 4.5 %fold_core.4 = (f32[4,96,768]{2,1,0:T(8,128)}, bf16[4,96,768]{2,1,0:T(8,128)(2,1)}, bf16[4,96,768]{2,1,0:T(8,128)(2,1)}, bf16[4,96,768]{2,1,0:T(8,128)(2,1)}) custom-call(bf16[4,4,96,768]{3,2,1,0:T(8,128)(2,1)} %get-tuple-element.142.refs_0_, bf16[4,4,96,768]{3,2,1,0:T(8,128)(2,1)} %copy-done.6), custom_call_target="tpu_custom_call" | custom-call | flops 1179648 | bytes 9437184 | tf_op jit(solution)/shard_map/fold_core/pallas_call | solution.py:668
  175.3 7.6 %up_back.2 = (bf16[4,4,96,768]{3,2,1,0:T(8,128)(2,1)}, f32[512,768]{1,0:T(8,128)}) custom-call(bf16[512,768]{1,0:T(8,128)(2,1)} %get-tuple-element.147.normed, bf16[512,1536]{1,0:T(8,128)(2,1)} %get-tuple-element.139.grad_pre, bf16[4,4,96,768]{3,2,1,0:T(8,128)(2,1)} %copy-done.40), custom_call_target="tpu_custom_call" | custom-call | flops 2415919104 | bytes 11796480 | tf_op jit(solution)/shard_map/up_back/pallas_call | solution.py:576
  185.3 12.4 %up_back.3 = (bf16[4,4,96,768]{3,2,1,0:T(8,128)(2,1)}, f32[512,768]{1,0:T(8,128)}, bf16[512,768]{1,0:T(8,128)(2,1)}, f32[8,768]{1,0:T(8,128)}, bf16[4,4,96,192]{...) custom-call(bf16[512,768]{1,0:T(8,128)(2,1)} %get-tuple-element.147.normed, ...), custom_call_target="tpu_custom_call" | custom-call | flops 2415919104 | bytes 11796480 | tf_op jit(solution)/shard_map/up_back/pallas_call | solution.py:576
  202.0 5.0 %fold_core.5 = (f32[4,96,1024]{2,1,0:T(8,128)}, bf16[4,96,1024]{2,1,0:T(8,128)(2,1)}, bf16[4,96,1024]{2,1,0:T(8,128)(2,1)}, bf16[4,96,1024]{2,1,0:T(8,128)(2,1)}) custom-call(bf16[4,4,96,768]{3,2,1,0:T(8,128)(2,1)} %get-tuple-element.158.refs_0_, bf16[4,4,96,192]{3,2,1,0:T(8,128)(2,1)} %get-tuple-element.159.refs_1_, bf16[4,4,96,768]{3,2,1,0:T(8,128)(2,1)} %copy-done.5, ...), custom_call_target="tpu_custom_call" | custom-call | flops 1572864 | bytes 12582912 | tf_op jit(solution)/shard_map/fold_core/pallas_call | solution.py:668
  207.0 16.6 %attend_back.2 = (f32[512,768]{1,0:T(8,128)}, f32[512,768]{1,0:T(8,128)}, bf16[4,2,96,576]{3,2,1,0:T(8,128)(2,1)}, bf16[4,2,96,576]{3,2,1,0:T(8,128)(2,1)}, f32[2,8,576]{2,1,0:T(8,128)}) custom-call(s32[16]{0:T(128)} %concatenate.36.info_ref.refs_0_, bf16[512,768]{1,0:T(8,128)(2,1)} %tokens.2, bf16[512,768]{1,0:T(8,128)(2,1)} %collective-permute-done.9.partner.refs_2_, ...), custom_call_target="tpu_custom_call" | custom-call | flops 7650410496 | bytes 6291456 | tf_op jit(solution)/shard_map/attend_back/pallas_call | solution.py:617
  228.7 11.3 %collective-permute-done.28.a = bf16[4,96,768]{2,1,0:T(8,128)(2,1)S(1)} collective-permute-done((bf16[4,96,768]{2,1,0:T(8,128)(2,1)S(1)}, bf16[4,96,768]{2,1,0:T(8,128)(2,1)S(1)}, u32[]{:S(2)}, u32[]{:S(2)}) %collective-permute-start.28) | collective-permute-done | bytes 589856 | tf_op jit(solution)/shard_map/ppermute | solution.py:707
  241.3 11.6 %collective-permute-done.29.b = bf16[4,96,768]{2,1,0:T(8,128)(2,1)S(1)} collective-permute-done((bf16[4,96,768]{2,1,0:T(8,128)(2,1)S(1)}, bf16[4,96,768]{2,1,0:T(8,128)(2,1)S(1)}, u32[]{:S(2)}, u32[]{:S(2)}) %collective-permute-start.29) | collective-permute-done | bytes 589856 | tf_op jit(solution)/shard_map/ppermute | solution.py:707
  255.4 3.4 fold_chips.4
  262.2 17.8 %attend_back.3 = (f32[512,768]{1,0:T(8,128)}, f32[512,768]{1,0:T(8,128)}, bf16[4,2,96,576]{3,2,1,0:T(8,128)(2,1)}, bf16[4,2,96,576]{3,2,1,0:T(8,128)(2,1)}, f32[2,8,576]{2,1,0:T(8,128)}) custom-call(s32[16]{0:T(128)} %concatenate.36.info_ref.refs_0_, bf16[512,768]{1,0:T(8,128)(2,1)} %tokens.2, bf16[512,768]{1,0:T(8,128)(2,1)} %collective-permute-done.9.partner.refs_2_, ...), custom_call_target="tpu_custom_call" | custom-call | flops 7650410496 | bytes 6291456 | tf_op jit(solution)/shard_map/attend_back/pallas_call | solution.py:617
  289.3 4.0 fold_chips.5
  304.2 8.1 %collective-permute-done.41.b = bf16[2,96,576]{2,1,0:T(8,128)(2,1)S(1)} collective-permute-done((bf16[2,96,576]{2,1,0:T(8,128)(2,1)S(1)}, bf16[2,96,576]{2,1,0:T(8,128)(2,1)S(1)}, u32[]{:S(2)}, u32[]{:S(2)}) %collective-permute-start.41) | collective-permute-done | bytes 221216 | tf_op jit(solution)/shard_map/ppermute | solution.py:707
  328.6 9.4 %collective-permute-done.57 = f32[12,768]{1,0:T(8,128)S(1)} collective-permute-done((f32[12,768]{1,0:T(8,128)S(1)}, f32[12,768]{1,0:T(8,128)S(1)}, u32[]{:S(2)}, u32[]{:S(2)}) %collective-permute-start.57) | collective-permute-done | bytes 36896 | tf_op jit(solution)/shard_map/ppermute | solution.py:707
  339.0 3.2 collective-permute-done.58
  363.2 13.8 %collective-permute-done.50 = bf16[96,576]{1,0:T(8,128)(2,1)S(1)} collective-permute-done((bf16[96,576]{1,0:T(8,128)(2,1)}, bf16[96,576]{1,0:T(8,128)(2,1)S(1)}, u32[]{:S(2)}, u32[]{:S(2)}) %collective-permute-start.50) | collective-permute-done | bytes 110624 | tf_op jit(solution)/shard_map/ppermute | solution.py:710
  401.7 2.8 settle_input.1
  404.5 3.0 copy.40
  408.5 4.7 %settle_up.1 = (f32[768,768]{1,0:T(8,128)}, f32[4,192,768]{2,1,0:T(8,128)}) custom-call(s32[3]{0:T(128)} %pad_add_fusion.info.refs_0_, bf16[4,96,1536]{2,1,0:T(8,128)(2,1)} %copy-done.4, bf16[4,96,1536]{2,1,0:T(8,128)(2,1)} %copy-done.13), custom_call_target="tpu_custom_call" | custom-call | tf_op jit(solution)/shard_map/settle_up/pallas_call | solution.py:979
  (330 shorter events, 145.1 us)
Async XLA Ops:
  23.0 20.8 %collective-permute-start.11 = (bf16[4,96,576]{2,1,0:T(8,128)(2,1)S(1)}, bf16[4,96,576]{2,1,0:T(8,128)(2,1)}, u32[]{:S(2)}, u32[]{:S(2)}) collective-permute-start(bf16[4,96,576]{2,1,0:T(8,128)(2,1)S(1)} %pad_maximum_fusion.7), channel_id=1, source_target_pairs={{0,16},{4,20},{8,24},{12,28},{16,0},{20,4},{24,8},{28,12},{1,17},{... | collective-permute-start | bytes 1327112 | tf_op jit(solution)/shard_map/ppermute | solution.py:707
  23.6 20.3 %collective-permute-start.10 = (bf16[4,96,576]{2,1,0:T(8,128)(2,1)S(1)}, bf16[4,96,576]{2,1,0:T(8,128)(2,1)}, u32[]{:S(2)}, u32[]{:S(2)}) collective-permute-start(bf16[4,96,576]{2,1,0:T(8,128)(2,1)S(1)} %pad_maximum_fusion.7), channel_id=1, source_target_pairs={{0,8},{4,12},{8,0},{12,4},{16,24},{20,28},{24,16},{28,20},{1,9},{5... | collective-permute-start | bytes 1327112 | tf_op jit(solution)/shard_map/ppermute | solution.py:707
  32.0 18.4 %collective-permute-start.2 = (f32[387]{0:T(512)S(1)}, f32[387]{0:T(512)S(1)}, u32[]{:S(2)}, u32[]{:S(2)}) collective-permute-start(f32[387]{0:T(512)S(1)} %pad_maximum_fusion.15), channel_id=1, source_target_pairs={{0,3},{1,2},{2,1},{3,0},{4,7},{5,6},{6,5},{7,4},{8,11},{9,10},{10,... | collective-permute-start | bytes 4652 | tf_op jit(solution)/shard_map/ppermute | solution.py:710
  33.8 16.5 %collective-permute-start.1 = (f32[387]{0:T(512)S(1)}, f32[387]{0:T(512)S(1)}, u32[]{:S(2)}, u32[]{:S(2)}) collective-permute-start(f32[387]{0:T(512)S(1)} %pad_maximum_fusion.15), channel_id=1, source_target_pairs={{0,2},{1,3},{2,0},{3,1},{4,6},{5,7},{6,4},{7,5},{8,10},{9,11},{10,... | collective-permute-start | bytes 4652 | tf_op jit(solution)/shard_map/ppermute | solution.py:710
  45.7 24.6 %collective-permute-start.13 = (bf16[4,4,96,576]{3,2,1,0:T(8,128)(2,1)S(1)}, bf16[4,4,96,576]{3,2,1,0:T(8,128)(2,1)}, u32[]{:S(2)}, u32[]{:S(2)}) collective-permute-start(bf16[4,4,96,576]{3,2,1,0:T(8,128)(2,1)S(1)} %pad_maximum_fusion.2.near.refs_4_), channel_id=1, source_target_pairs={{0,4},{4,0},{8,12},{12,8},{16,20},{20,16},{24,28},{28,24},{1,5},{5... | collective-permute-start | bytes 5308424 | tf_op jit(solution)/shard_map/ppermute | solution.py:707
  50.4 20.0 %collective-permute-start.9 = (bf16[512,768]{1,0:T(8,128)(2,1)}, bf16[512,768]{1,0:T(8,128)(2,1)}, u32[]{:S(2)}, u32[]{:S(2)}) collective-permute-start(bf16[512,768]{1,0:T(8,128)(2,1)} %tokens.2), channel_id=1, source_target_pairs={{0,1},{1,0},{2,3},{3,2},{4,5},{5,4},{6,7},{7,6},{8,9},{9,8},{10,11... | collective-permute-start | bytes 2359304 | tf_op jit(solution)/shard_map/ppermute | solution.py:710
  51.3 38.7 %collective-permute-start.16 = (bf16[4,96,768]{2,1,0:T(8,128)(2,1)S(1)}, bf16[4,96,768]{2,1,0:T(8,128)(2,1)S(1)}, u32[]{:S(2)}, u32[]{:S(2)}) collective-permute-start(bf16[4,96,768]{2,1,0:T(8,128)(2,1)S(1)} %pad_maximum_fusion.4), channel_id=1, source_target_pairs={{0,24},{4,28},{8,16},{12,20},{16,8},{20,12},{24,0},{28,4},{1,25},{... | collective-permute-start | bytes 1769480 | tf_op jit(solution)/shard_map/ppermute | solution.py:707
  53.1 37.0 %collective-permute-start.15 = (bf16[4,96,768]{2,1,0:T(8,128)(2,1)S(1)}, bf16[4,96,768]{2,1,0:T(8,128)(2,1)S(1)}, u32[]{:S(2)}, u32[]{:S(2)}) collective-permute-start(bf16[4,96,768]{2,1,0:T(8,128)(2,1)S(1)} %pad_maximum_fusion.4), channel_id=1, source_target_pairs={{0,16},{4,20},{8,24},{12,28},{16,0},{20,4},{24,8},{28,12},{1,17},{... | collective-permute-start | bytes 1769480 | tf_op jit(solution)/shard_map/ppermute | solution.py:707
  54.3 35.8 %collective-permute-start.14 = (bf16[4,96,768]{2,1,0:T(8,128)(2,1)S(1)}, bf16[4,96,768]{2,1,0:T(8,128)(2,1)S(1)}, u32[]{:S(2)}, u32[]{:S(2)}) collective-permute-start(bf16[4,96,768]{2,1,0:T(8,128)(2,1)S(1)} %pad_maximum_fusion.4), channel_id=1, source_target_pairs={{0,8},{4,12},{8,0},{12,4},{16,24},{20,28},{24,16},{28,20},{1,9},{5... | collective-permute-start | bytes 1769480 | tf_op jit(solution)/shard_map/ppermute | solution.py:707
  90.4 20.2 %collective-permute-start.17 = (bf16[4,4,96,768]{3,2,1,0:T(8,128)(2,1)S(1)}, bf16[4,4,96,768]{3,2,1,0:T(8,128)(2,1)S(1)}, u32[]{:S(2)}, u32[]{:S(2)}) collective-permute-start(bf16[4,4,96,768]{3,2,1,0:T(8,128)(2,1)S(1)} %pad_maximum_fusion.near.weight), channel_id=1, source_target_pairs={{0,4},{4,0},{8,12},{12,8},{16,20},{20,16},{24,28},{28,24},{1,5},{5... | collective-permute-start | bytes 7077896 | tf_op jit(solution)/shard_map/ppermute | solution.py:707
  107.0 17.9 %collective-permute-start.23 = (bf16[4,96,768]{2,1,0:T(8,128)(2,1)S(1)}, bf16[4,96,768]{2,1,0:T(8,128)(2,1)S(1)}, u32[]{:S(2)}, u32[]{:S(2)}) collective-permute-start(bf16[4,96,768]{2,1,0:T(8,128)(2,1)S(1)} %pad_maximum_fusion.5), channel_id=1, source_target_pairs={{0,24},{4,28},{8,16},{12,20},{16,8},{20,12},{24,0},{28,4},{1,25},{... | collective-permute-start | bytes 1769480 | tf_op jit(solution)/shard_map/ppermute | solution.py:707
  108.7 26.6 %collective-permute-start.22 = (bf16[4,96,768]{2,1,0:T(8,128)(2,1)S(1)}, bf16[4,96,768]{2,1,0:T(8,128)(2,1)S(1)}, u32[]{:S(2)}, u32[]{:S(2)}) collective-permute-start(bf16[4,96,768]{2,1,0:T(8,128)(2,1)S(1)} %pad_maximum_fusion.5), channel_id=1, source_target_pairs={{0,16},{4,20},{8,24},{12,28},{16,0},{20,4},{24,8},{28,12},{1,17},{... | collective-permute-start | bytes 1769480 | tf_op jit(solution)/shard_map/ppermute | solution.py:707
  109.9 25.4 %collective-permute-start.21 = (bf16[4,96,768]{2,1,0:T(8,128)(2,1)S(1)}, bf16[4,96,768]{2,1,0:T(8,128)(2,1)S(1)}, u32[]{:S(2)}, u32[]{:S(2)}) collective-permute-start(bf16[4,96,768]{2,1,0:T(8,128)(2,1)S(1)} %pad_maximum_fusion.5), channel_id=1, source_target_pairs={{0,8},{4,12},{8,0},{12,4},{16,24},{20,28},{24,16},{28,20},{1,9},{5... | collective-permute-start | bytes 1769480 | tf_op jit(solution)/shard_map/ppermute | solution.py:707
  183.0 17.4 %collective-permute-start.26 = (bf16[4,4,96,768]{3,2,1,0:T(8,128)(2,1)}, bf16[4,4,96,768]{3,2,1,0:T(8,128)(2,1)S(1)}, u32[]{:S(2)}, u32[]{:S(2)}) collective-permute-start(bf16[4,4,96,768]{3,2,1,0:T(8,128)(2,1)} %get-tuple-element.160), channel_id=1, source_target_pairs={{0,4},{4,0},{8,12},{12,8},{16,20},{20,16},{24,28},{28,24},{1,5},{5... | collective-permute-start | bytes 7077896 | tf_op jit(solution)/shard_map/ppermute | solution.py:707
  223.6 35.3 %collective-permute-start.31 = (bf16[4,2,96,576]{3,2,1,0:T(8,128)(2,1)}, bf16[4,2,96,576]{3,2,1,0:T(8,128)(2,1)S(1)}, u32[]{:S(2)}, u32[]{:S(2)}) collective-permute-start(bf16[4,2,96,576]{3,2,1,0:T(8,128)(2,1)} %get-tuple-element.175), channel_id=1, source_target_pairs={{0,4},{4,0},{8,12},{12,8},{16,20},{20,16},{24,28},{28,24},{1,5},{5... | collective-permute-start | bytes 2654216 | tf_op jit(solution)/shard_map/ppermute | solution.py:707
  225.2 27.8 %collective-permute-start.29 = (bf16[4,96,768]{2,1,0:T(8,128)(2,1)S(1)}, bf16[4,96,768]{2,1,0:T(8,128)(2,1)S(1)}, u32[]{:S(2)}, u32[]{:S(2)}) collective-permute-start(bf16[4,96,768]{2,1,0:T(8,128)(2,1)S(1)} %copy-done.42), channel_id=1, source_target_pairs={{0,16},{4,20},{8,24},{12,28},{16,0},{20,4},{24,8},{28,12},{1,17},{... | collective-permute-start | bytes 1769480 | tf_op jit(solution)/shard_map/ppermute | solution.py:707
  226.0 28.6 %collective-permute-start.30 = (bf16[4,96,768]{2,1,0:T(8,128)(2,1)S(1)}, bf16[4,96,768]{2,1,0:T(8,128)(2,1)S(1)}, u32[]{:S(2)}, u32[]{:S(2)}) collective-permute-start(bf16[4,96,768]{2,1,0:T(8,128)(2,1)S(1)} %copy-done.41), channel_id=1, source_target_pairs={{0,24},{4,28},{8,16},{12,20},{16,8},{20,12},{24,0},{28,4},{1,25},{... | collective-permute-start | bytes 1769480 | tf_op jit(solution)/shard_map/ppermute | solution.py:707
  227.3 55.1 %collective-permute-start.34 = (bf16[4,96,1024]{2,1,0:T(8,128)(2,1)}, bf16[4,96,1024]{2,1,0:T(8,128)(2,1)S(1)}, u32[]{:S(2)}, u32[]{:S(2)}) collective-permute-start(bf16[4,96,1024]{2,1,0:T(8,128)(2,1)} %get-tuple-element.162), channel_id=1, source_target_pairs={{0,8},{4,12},{8,0},{12,4},{16,24},{20,28},{24,16},{28,20},{1,9},{5... | collective-permute-start | bytes 2359304 | tf_op jit(solution)/shard_map/ppermute | solution.py:707
  239.9 46.9 %collective-permute-start.35 = (bf16[4,96,1024]{2,1,0:T(8,128)(2,1)}, bf16[4,96,1024]{2,1,0:T(8,128)(2,1)S(1)}, u32[]{:S(2)}, u32[]{:S(2)}) collective-permute-start(bf16[4,96,1024]{2,1,0:T(8,128)(2,1)} %get-tuple-element.163), channel_id=1, source_target_pairs={{0,16},{4,20},{8,24},{12,28},{16,0},{20,4},{24,8},{28,12},{1,17},{... | collective-permute-start | bytes 2359304 | tf_op jit(solution)/shard_map/ppermute | solution.py:707
  252.9 35.4 %collective-permute-start.36 = (bf16[4,96,1024]{2,1,0:T(8,128)(2,1)}, bf16[4,96,1024]{2,1,0:T(8,128)(2,1)S(1)}, u32[]{:S(2)}, u32[]{:S(2)}) collective-permute-start(bf16[4,96,1024]{2,1,0:T(8,128)(2,1)} %get-tuple-element.164), channel_id=1, source_target_pairs={{0,24},{4,28},{8,16},{12,20},{16,8},{20,12},{24,0},{28,4},{1,25},{... | collective-permute-start | bytes 2359304 | tf_op jit(solution)/shard_map/ppermute | solution.py:707
  280.1 16.6 %collective-permute-start.37 = (bf16[96,768]{1,0:T(8,128)(2,1)}, bf16[96,768]{1,0:T(8,128)(2,1)S(1)}, u32[]{:S(2)}, u32[]{:S(2)}) collective-permute-start(bf16[96,768]{1,0:T(8,128)(2,1)} %get-tuple-element.171), channel_id=1, source_target_pairs={{0,1},{1,0},{2,3},{3,2},{4,5},{5,4},{6,7},{7,6},{8,9},{9,8},{10,11... | collective-permute-start | bytes 442376 | tf_op jit(solution)/shard_map/ppermute | solution.py:710
  293.3 22.4 %collective-permute-start.43 = (bf16[96,1024]{1,0:T(8,128)(2,1)}, bf16[96,1024]{1,0:T(8,128)(2,1)S(1)}, u32[]{:S(2)}, u32[]{:S(2)}) collective-permute-start(bf16[96,1024]{1,0:T(8,128)(2,1)} %get-tuple-element.190), channel_id=1, source_target_pairs={{0,1},{1,0},{2,3},{3,2},{4,5},{5,4},{6,7},{7,6},{8,9},{9,8},{10,11... | collective-permute-start | bytes 589832 | tf_op jit(solution)/shard_map/ppermute | solution.py:710
  296.7 19.1 %collective-permute-start.44 = (bf16[96,1024]{1,0:T(8,128)(2,1)S(1)}, bf16[96,1024]{1,0:T(8,128)(2,1)S(1)}, u32[]{:S(2)}, u32[]{:S(2)}) collective-permute-start(bf16[96,1024]{1,0:T(8,128)(2,1)S(1)} %copy-done.47), channel_id=1, source_target_pairs={{0,2},{1,3},{2,0},{3,1},{4,6},{5,7},{6,4},{7,5},{8,10},{9,11},{10,... | collective-permute-start | bytes 589832 | tf_op jit(solution)/shard_map/ppermute | solution.py:710
  298.7 17.0 %collective-permute-start.45 = (bf16[96,1024]{1,0:T(8,128)(2,1)S(1)}, bf16[96,1024]{1,0:T(8,128)(2,1)S(1)}, u32[]{:S(2)}, u32[]{:S(2)}) collective-permute-start(bf16[96,1024]{1,0:T(8,128)(2,1)S(1)} %copy-done.46), channel_id=1, source_target_pairs={{0,3},{1,2},{2,1},{3,0},{4,7},{5,6},{6,5},{7,4},{8,11},{9,10},{10,... | collective-permute-start | bytes 589832 | tf_op jit(solution)/shard_map/ppermute | solution.py:710
  323.9 25.6 %collective-permute-start.66 = (bf16[96,1536]{1,0:T(8,128)(2,1)S(1)}, bf16[96,1536]{1,0:T(8,128)(2,1)S(1)}, u32[]{:S(2)}, u32[]{:S(2)}) collective-permute-start(bf16[96,1536]{1,0:T(8,128)(2,1)S(1)} %concatenate.45), channel_id=1, source_target_pairs={{0,24},{4,28},{8,16},{12,20},{16,8},{20,12},{24,0},{28,4},{1,25},{... | collective-permute-start | bytes 884744 | tf_op jit(solution)/shard_map/ppermute | solution.py:707
  325.4 25.3 %collective-permute-start.65 = (bf16[96,1536]{1,0:T(8,128)(2,1)S(1)}, bf16[96,1536]{1,0:T(8,128)(2,1)S(1)}, u32[]{:S(2)}, u32[]{:S(2)}) collective-permute-start(bf16[96,1536]{1,0:T(8,128)(2,1)S(1)} %concatenate.45), channel_id=1, source_target_pairs={{0,16},{4,20},{8,24},{12,28},{16,0},{20,4},{24,8},{28,12},{1,17},{... | collective-permute-start | bytes 884744 | tf_op jit(solution)/shard_map/ppermute | solution.py:707
  326.5 25.6 %collective-permute-start.64 = (bf16[96,1536]{1,0:T(8,128)(2,1)S(1)}, bf16[96,1536]{1,0:T(8,128)(2,1)S(1)}, u32[]{:S(2)}, u32[]{:S(2)}) collective-permute-start(bf16[96,1536]{1,0:T(8,128)(2,1)S(1)} %concatenate.45), channel_id=1, source_target_pairs={{0,8},{4,12},{8,0},{12,4},{16,24},{20,28},{24,16},{28,20},{1,9},{5... | collective-permute-start | bytes 884744 | tf_op jit(solution)/shard_map/ppermute | solution.py:707
  352.3 55.2 %collective-permute-start.67 = (bf16[4,96,1536]{2,1,0:T(8,128)(2,1)S(1)}, bf16[4,96,1536]{2,1,0:T(8,128)(2,1)S(1)}, u32[]{:S(2)}, u32[]{:S(2)}) collective-permute-start(bf16[4,96,1536]{2,1,0:T(8,128)(2,1)S(1)} %pad_maximum_fusion.3.near), channel_id=1, source_target_pairs={{0,4},{4,0},{8,12},{12,8},{16,20},{20,16},{24,28},{28,24},{1,5},{5... | collective-permute-start | bytes 3538952 | tf_op jit(solution)/shard_map/ppermute | solution.py:707
  355.1 39.6 %collective-permute-start.32 = (bf16[512,768]{1,0:T(8,128)(2,1)}, bf16[512,768]{1,0:T(8,128)(2,1)}, u32[]{:S(2)}, u32[]{:S(2)}) collective-permute-start(bf16[512,768]{1,0:T(8,128)(2,1)} %convert_element_type.54), channel_id=1, source_target_pairs={{0,1},{1,0},{2,3},{3,2},{4,5},{5,4},{6,7},{7,6},{8,9},{9,8},{10,11... | collective-permute-start | bytes 2359304 | tf_op jit(solution)/shard_map/ppermute | solution.py:710
  356.8 20.1 %collective-permute-start.50 = (bf16[96,576]{1,0:T(8,128)(2,1)}, bf16[96,576]{1,0:T(8,128)(2,1)S(1)}, u32[]{:S(2)}, u32[]{:S(2)}) collective-permute-start(bf16[96,576]{1,0:T(8,128)(2,1)} %get-tuple-element.198), channel_id=1, source_target_pairs={{0,2},{1,3},{2,0},{3,1},{4,6},{5,7},{6,4},{7,5},{8,10},{9,11},{10,... | collective-permute-start | bytes 331784 | tf_op jit(solution)/shard_map/ppermute | solution.py:710
  358.7 22.4 %collective-permute-start.51 = (bf16[96,576]{1,0:T(8,128)(2,1)S(1)}, bf16[96,576]{1,0:T(8,128)(2,1)S(1)}, u32[]{:S(2)}, u32[]{:S(2)}) collective-permute-start(bf16[96,576]{1,0:T(8,128)(2,1)S(1)} %copy-done.48), channel_id=1, source_target_pairs={{0,3},{1,2},{2,1},{3,0},{4,7},{5,6},{6,5},{7,4},{8,11},{9,10},{10,... | collective-permute-start | bytes 331784 | tf_op jit(solution)/shard_map/ppermute | solution.py:710
  362.5 20.3 %collective-permute-start.49 = (bf16[96,576]{1,0:T(8,128)(2,1)}, bf16[96,576]{1,0:T(8,128)(2,1)S(1)}, u32[]{:S(2)}, u32[]{:S(2)}) collective-permute-start(bf16[96,576]{1,0:T(8,128)(2,1)} %get-tuple-element.206), channel_id=1, source_target_pairs={{0,1},{1,0},{2,3},{3,2},{4,5},{5,4},{6,7},{7,6},{8,9},{9,8},{10,11... | collective-permute-start | bytes 331784 | tf_op jit(solution)/shard_map/ppermute | solution.py:710
  (91 other events, 836.4 us)
